TPU v7x, 256 devices: a whole 4x4x8 slice. The times are simulated.
256 devices in a mesh: gx: 16 (over z, core), gy: 16 (over y, x).
Axes of the slice: x: 4, y: 4, z: 8, core: 2. Of those that a mesh axis runs over, the one named last changes fastest.
Arguments:
- diffusivity: float32 [64, 512, 16], P('gx', 'gy'), may hold values from 0.2 to 27
- labels: int32 [64, 512, 16], P('gx', 'gy'), may hold values from 0 to 64, as said below
- obstacles: int32 [64, 512, 16], P('gx', 'gy'), may hold values 0 or 1
Outputs:
- solution: float32 [64, 512, 1024], P('gx', 'gy')
- residual: float32 [64, 512, 1024], P('gx', 'gy')
Inputs may be any that keep to these rules, and one draw needn't show every extreme that they name: `labels`: 0 marks a voxel without receptors, k marks a voxel of receptor cluster k; on obstacle voxels the label has no effect.
All inputs are finite; a program needn't handle non-finite values. No bound on the sum of `obstacles` on one device may be relied on, other than what follows from the above.
Results may differ from a plain program's by a relative error of at most 0.0003.
Values sent between devices are 32-bit elements; how exact they have to be, the bound alone decides.
No kernel may reach another device: no remote copies, remote signals or barrier semaphores. Data moves between devices by JAX's collectives and lax.ppermute only.
A program may use at most 64 MiB of HBM per device.

v0:
```python
import jax
import jax.numpy as jnp
from jax import lax
from jax.sharding import PartitionSpec as P

NZ = 16
K = 64
ITERS = 3


HIGH = lax.Precision.HIGHEST


def extended(block, sides, width):
    for axis, dim in sides:
        count = lax.axis_size(axis)
        forward = [(i, i + 1) for i in range(count - 1)]
        backward = [(target, source) for source, target in forward]
        low = lax.ppermute(
            lax.slice_in_dim(block, block.shape[dim] - width, None, axis=dim), axis, forward
        )
        high = lax.ppermute(lax.slice_in_dim(block, 0, width, axis=dim), axis, backward)
        block = jnp.concatenate([low, block, high], axis=dim)
    return block


def neighbour_views(padded):
    return [
        padded[2:, 1:-1, 1:-1],
        padded[:-2, 1:-1, 1:-1],
        padded[1:-1, 2:, 1:-1],
        padded[1:-1, :-2, 1:-1],
        padded[1:-1, 1:-1, 2:],
        padded[1:-1, 1:-1, :-2],
    ]


def assemble(padded_cond, padded_label, free_cells, cluster_ids):
    center = padded_cond[1:-1, 1:-1, 1:-1]
    face_cond = []
    for neighbour in neighbour_views(padded_cond):
        product = center * neighbour
        face_cond.append(2.0 * product / jnp.where(product > 0, center + neighbour, 1.0))
    label_nbrs = neighbour_views(padded_label)
    diagonal = free_cells * (
        face_cond[0] + face_cond[1] + face_cond[2] + face_cond[3] + face_cond[4] + face_cond[5]
    ) + (1.0 - free_cells)
    couple = [
        free_cells * conduct * (label_nbr == 0.0).astype(jnp.float32)
        for conduct, label_nbr in zip(face_cond, label_nbrs)
    ]
    source = jnp.zeros(center.shape + (cluster_ids.shape[0],), jnp.float32)
    for conduct, label_nbr in zip(face_cond, label_nbrs):
        hits = (label_nbr[..., None] == cluster_ids).astype(jnp.float32)
        source = source + (free_cells * conduct)[..., None] * hits
    return (diagonal, couple, source)


def apply_operator(padded4, diagonal, couple):
    center = padded4[1:-1, 1:-1]
    zpad = jnp.pad(center, ((0, 0), (0, 0), (1, 1), (0, 0)))
    result = diagonal[..., None] * center
    result = result - couple[0][..., None] * padded4[2:, 1:-1]
    result = result - couple[1][..., None] * padded4[:-2, 1:-1]
    result = result - couple[2][..., None] * padded4[1:-1, 2:]
    result = result - couple[3][..., None] * padded4[1:-1, :-2]
    result = result - couple[4][..., None] * zpad[:, :, 2:]
    result = result - couple[5][..., None] * zpad[:, :, :-2]
    return result


def inner_block(first_block, second_block):
    width = first_block.shape[-1]
    return lax.dot_general(
        first_block.reshape(-1, width),
        second_block.reshape(-1, width),
        (((0,), (0,)), ((), ())),
        precision=HIGH,
    )


def times_block(field, matrix):
    width = field.shape[-1]
    return jnp.dot(field.reshape(-1, width), matrix, precision=HIGH).reshape(field.shape)


def solve_gram(matrix, right_side):
    factor = jnp.linalg.cholesky(matrix)
    return jax.scipy.linalg.cho_solve((factor, True), right_side)


def extend_faces(search):
    rows_here, cols_here = (search.shape[0], search.shape[1])
    flat_search = search.reshape(rows_here, cols_here, NZ * K)
    padded = extended(flat_search, (("gx", 0), ("gy", 1)), 1)
    return padded.reshape(rows_here + 2, cols_here + 2, NZ, K)


def shards(diffusivity, labels, obstacles):
    rows_here, cols_here = (diffusivity.shape[0], diffusivity.shape[1])
    conductive = diffusivity * (1 - obstacles).astype(jnp.float32)
    free_cells = ((obstacles == 0) & (labels == 0)).astype(jnp.float32)
    packed_cells = jnp.concatenate([conductive, labels.astype(jnp.float32)], axis=2)
    rim_cells = extended(packed_cells, (("gx", 0), ("gy", 1)), 1)
    padded_cond = jnp.pad(rim_cells[:, :, :NZ], ((0, 0), (0, 0), (1, 1)))
    padded_label = jnp.pad(rim_cells[:, :, NZ:], ((0, 0), (0, 0), (1, 1)))
    cluster_ids = (jnp.arange(K) + 1).astype(jnp.float32)
    diagonal, couple, source = assemble(padded_cond, padded_label, free_cells, cluster_ids)
    solution = jnp.zeros_like(source)
    residual = source
    search = source
    norm_now = lax.psum(inner_block(residual, residual), ("gx", "gy"))
    for iteration in range(ITERS):
        image_block = apply_operator(extend_faces(search), diagonal, couple)
        curve_gram = lax.psum(inner_block(search, image_block), ("gx", "gy"))
        step_size = solve_gram(curve_gram, norm_now)
        solution = solution + times_block(search, step_size)
        residual = residual - times_block(image_block, step_size)
        if iteration + 1 < ITERS:
            norm_next = lax.psum(inner_block(residual, residual), ("gx", "gy"))
            direction_mix = solve_gram(norm_now, norm_next)
            search = residual + times_block(search, direction_mix)
            norm_now = norm_next
    return (
        solution.reshape(rows_here, cols_here, NZ * K),
        residual.reshape(rows_here, cols_here, NZ * K),
    )


def solution(mesh):
    in_specs = (P("gx", "gy", None), P("gx", "gy", None), P("gx", "gy", None))
    out_specs = (P("gx", "gy", None), P("gx", "gy", None))
    return jax.shard_map(shards, mesh=mesh, in_specs=in_specs, out_specs=out_specs, check_vma=False)
```

profile of v0, /device:TPU:1, one launch (start us, length us, event | category | flops | bytes accessed | tf_op | source)
XLA Modules:
  0.0 636.8 jit_solution(15543476628922478109)
XLA Ops:
  2.2 5.1 collective-permute-start
  7.3 1.9 collective-permute-start.1
  9.3 1.1 collective-permute-done.1
  10.5 1.3 collective-permute-start.2
  11.8 4.0 collective-permute-start.3
  17.6 1.5 subtract_add_fusion
  27.2 3.4 select_add_fusion
  31.9 1.2 mul.300.clone
  35.7 1.2 eq.193.clone
  37.9 1.2 eq.195.clone
  43.2 1.2 eq.197.clone
  44.4 1.1 eq.212
  50.9 5.0 collective-permute-start.4
  56.8 2.1 collective-permute-start.5
  58.9 2.7 select_add_fusion.1
  61.6 1.8 collective-permute-done.5
  64.2 4.0 collective-permute-start.6
  68.3 1.9 collective-permute-start.7
  70.3 9.4 %convolution_bitcast_fusion.9 = f32[64,64]{0,1:T(8,128)} fusion(f32[4,32,16]{1,2,0:T(8,128)S(1)} %copy-done.53, f32[4,32,16]{1,2,0:T(8,128)S(1)} %copy-done.64, f32[4,32,16]{1,2,0:T(8,128)S(1)} %copy-done.49, f32[4,32,16]{1,2,0:T(8,128)S(1)} %copy-done.58, f32[4,32,16]{1,2,0:T(8,128)S(1)} %get-tuple-element.41, f32[4,32,16]{1,2,0:T(8,128)S(1)} %get-tuple-element.42, ...), kind=kOutput, calls=%fused_computation.22 | convolution fusion | flops 102891520 | bytes 114944 | tf_op jit(solution)/shard_map/dot_general | solution.py:74
  82.1 2.3 fusion.2
  84.6 5.2 convolution_bitcast_fusion.10
  89.8 87.6 %all-reduce.5 = (f32[64,64]{0,1:T(8,128)S(1)}, f32[64,64]{0,1:T(8,128)S(1)}) all-reduce(f32[64,64]{0,1:T(8,128)S(1)} %copy-done.82, f32[64,64]{0,1:T(8,128)S(1)} %convolution_bitcast_fusion.10), channel_id=1, replica_groups=mesh['gx'=16,'gy'=16] {'gx','gy'}, use_global_device_ids=true, to_apply=%region_3.5 | all-reduce | flops 8192 | bytes 65536 | tf_op jit(solution)/shard_map/psum | solution.py:112
  177.6 5.8 cholesky.89
  184.8 4.9 custom-call.11
  190.7 6.2 convolution_subtract_fusion.2
  197.0 1.9 convolution_bitcast_fusion.7
  198.9 73.7 %psum.44 = f32[64,64]{0,1:T(8,128)S(1)} all-reduce(f32[64,64]{0,1:T(8,128)S(1)} %convolution_bitcast_fusion.7), channel_id=1, replica_groups=mesh['gx'=16,'gy'=16] {'gx','gy'}, use_global_device_ids=true, to_apply=%region_4.7 | all-reduce | flops 4096 | bytes 32768 | tf_op jit(solution)/shard_map/psum | solution.py:120
  272.6 5.8 cholesky.122
  278.5 5.9 cholesky.100
  285.7 4.9 custom-call.12
  291.0 4.0 convolution_add_fusion.3
  296.8 4.2 collective-permute-start.8
  303.2 1.9 collective-permute-start.9
  306.7 2.8 collective-permute-done.9
  309.6 3.1 collective-permute-start.10
  312.7 1.5 collective-permute-start.11
  314.9 4.9 custom-call.14
  320.9 1.7 reshape.332
  322.7 2.3 fusion.6
  325.9 2.1 convolution_bitcast_fusion.5
  328.0 77.6 %psum.45 = f32[64,64]{0,1:T(8,128)S(1)} all-reduce(f32[64,64]{0,1:T(8,128)S(1)} %convolution_bitcast_fusion.5), channel_id=1, replica_groups=mesh['gx'=16,'gy'=16] {'gx','gy'}, use_global_device_ids=true, to_apply=%region_5.8 | all-reduce | flops 4096 | bytes 32768 | tf_op jit(solution)/shard_map/psum | solution.py:115
  405.7 5.8 cholesky.111
  412.9 4.9 custom-call.13
  418.2 2.4 convolution_subtract_fusion.1
  420.6 1.9 convolution_bitcast_fusion.3
  422.5 73.6 %psum.46 = f32[64,64]{1,0:T(8,128)S(1)} all-reduce(f32[64,64]{1,0:T(8,128)S(1)} %convolution_bitcast_fusion.3), channel_id=1, replica_groups=mesh['gx'=16,'gy'=16] {'gx','gy'}, use_global_device_ids=true, to_apply=%region_6.9 | all-reduce | flops 4096 | bytes 32768 | tf_op jit(solution)/shard_map/psum | solution.py:120
  500.3 4.8 collective-permute-start.12
  505.2 6.3 fusion.55
  513.2 1.9 copy.53
  515.1 1.7 slice.263
  516.8 2.0 collective-permute-start.13
  520.9 2.5 collective-permute-done.13
  523.5 3.2 collective-permute-start.14
  526.7 1.3 collective-permute-start.15
  528.1 1.9 convolution_add_fusion.2
  530.0 1.3 collective-permute-done.15
  531.3 1.1 pad_maximum_fusion.2
  532.4 1.7 reshape.334
  535.0 2.2 fusion.10
  538.2 2.1 convolution_bitcast_fusion.1
  540.3 76.9 %psum.47 = f32[64,64]{0,1:T(8,128)S(1)} all-reduce(f32[64,64]{0,1:T(8,128)S(1)} %convolution_bitcast_fusion.1), channel_id=1, replica_groups=mesh['gx'=16,'gy'=16] {'gx','gy'}, use_global_device_ids=true, to_apply=%region_7.10 | all-reduce | flops 4096 | bytes 32768 | tf_op jit(solution)/shard_map/psum | solution.py:115
  617.2 5.8 cholesky.133
  624.4 4.9 custom-call.15
  629.7 2.4 convolution_subtract_fusion
  (300 shorter events, 60.1 us)
Async XLA Ops:
  2.2 7.1 %collective-permute-start = (f32[1,32,32]{1,2,0:T(8,128)S(1)}, f32[1,32,32]{1,2,0:T(8,128)S(1)}, u32[]{:S(2)}, u32[]{:S(2)}) collective-permute-start(f32[1,32,32]{1,2,0:T(8,128)S(1)} %get-tuple-element.51), channel_id=1, source_target_pairs={{16,0},{32,16},{48,32},{64,48},{80,64},{96,80},{112,96},{128,112},... | collective-permute-start | bytes 12296 | tf_op jit(solution)/shard_map/ppermute | solution.py:22
  7.3 3.1 collective-permute-start.1
  10.5 6.1 collective-permute-start.2
  11.8 5.6 collective-permute-start.3
  19.7 50.4 %copy-start.25 = (f32[4,32,16]{1,2,0:T(8,128)}, f32[4,32,16]{1,2,0:T(8,128)S(1)}, u32[]{:S(2)}) copy-start(f32[4,32,16]{1,2,0:T(8,128)S(1)} %get-tuple-element.11) | copy-start | bytes 24580
  19.7 50.4 %copy-start.27 = (f32[4,32,16]{1,2,0:T(8,128)}, f32[4,32,16]{1,2,0:T(8,128)S(1)}, u32[]{:S(2)}) copy-start(f32[4,32,16]{1,2,0:T(8,128)S(1)} %get-tuple-element.12) | copy-start | bytes 24580
  19.7 50.5 %copy-start.30 = (f32[4,32,16]{1,2,0:T(8,128)}, f32[4,32,16]{1,2,0:T(8,128)S(1)}, u32[]{:S(2)}) copy-start(f32[4,32,16]{1,2,0:T(8,128)S(1)} %get-tuple-element.48) | copy-start | bytes 24580
  19.7 50.5 %copy-start.33 = (f32[4,32,16]{1,2,0:T(8,128)}, f32[4,32,16]{1,2,0:T(8,128)S(1)}, u32[]{:S(2)}) copy-start(f32[4,32,16]{1,2,0:T(8,128)S(1)} %get-tuple-element.49) | copy-start | bytes 24580
  21.4 48.8 %copy-start.36 = (f32[4,32,16]{1,2,0:T(8,128)}, f32[4,32,16]{1,2,0:T(8,128)S(1)}, u32[]{:S(2)}) copy-start(f32[4,32,16]{1,2,0:T(8,128)S(1)} %get-tuple-element.17) | copy-start | bytes 24580
  21.4 48.8 %copy-start.39 = (f32[4,32,16]{1,2,0:T(8,128)}, f32[4,32,16]{1,2,0:T(8,128)S(1)}, u32[]{:S(2)}) copy-start(f32[4,32,16]{1,2,0:T(8,128)S(1)} %get-tuple-element.18) | copy-start | bytes 24580
  21.4 48.8 %copy-start.42 = (f32[4,32,16]{1,2,0:T(8,128)}, f32[4,32,16]{1,2,0:T(8,128)S(1)}, u32[]{:S(2)}) copy-start(f32[4,32,16]{1,2,0:T(8,128)S(1)} %get-tuple-element.41) | copy-start | bytes 24580
  21.4 48.8 %copy-start.45 = (f32[4,32,16]{1,2,0:T(8,128)}, f32[4,32,16]{1,2,0:T(8,128)S(1)}, u32[]{:S(2)}) copy-start(f32[4,32,16]{1,2,0:T(8,128)S(1)} %get-tuple-element.42) | copy-start | bytes 24580
  49.8 9.0 %copy-start.11 = (f32[4,32,1024]{2,1,0:T(8,128)S(1)}, f32[4,32,1024]{2,1,0:T(8,128)}, u32[]{:S(2)}) copy-start(f32[4,32,1024]{2,1,0:T(8,128)} %mul.329) | copy-start | bytes 1572868
  49.9 9.0 %copy-start.12 = (f32[4,32,1024]{2,1,0:T(8,128)S(1)}, f32[4,32,1024]{2,1,0:T(8,128)}, u32[]{:S(2)}) copy-start(f32[4,32,1024]{2,1,0:T(8,128)} %mul.331) | copy-start | bytes 1572868
  49.9 9.0 %copy-start.13 = (f32[4,32,1024]{2,1,0:T(8,128)S(1)}, f32[4,32,1024]{2,1,0:T(8,128)}, u32[]{:S(2)}) copy-start(f32[4,32,1024]{2,1,0:T(8,128)} %eq.208) | copy-start | bytes 1572868
  50.9 10.8 %collective-permute-start.4 = (f32[1,32,1024]{2,1,0:T(8,128)}, f32[1,32,1024]{2,1,0:T(8,128)S(1)}, u32[]{:S(2)}, u32[]{:S(2)}) collective-permute-start(f32[1,32,1024]{2,1,0:T(8,128)} %slice.235), channel_id=1, source_target_pairs={{0,16},{16,32},{32,48},{48,64},{64,80},{80,96},{96,112},{112,128},... | collective-permute-start | bytes 393224 | tf_op jit(solution)/shard_map/ppermute | solution.py:19
  56.8 13.4 %copy-start.49 = (f32[4,32,16]{1,2,0:T(8,128)S(1)}, f32[4,32,16]{1,2,0:T(8,128)}, u32[]{:S(2)}) copy-start(f32[4,32,16]{1,2,0:T(8,128)} %copy-done.48) | copy-start | bytes 24580
  56.8 13.4 %copy-start.53 = (f32[4,32,16]{1,2,0:T(8,128)S(1)}, f32[4,32,16]{1,2,0:T(8,128)}, u32[]{:S(2)}) copy-start(f32[4,32,16]{1,2,0:T(8,128)} %copy-done.52) | copy-start | bytes 24580
  56.8 13.4 %copy-start.58 = (f32[4,32,16]{1,2,0:T(8,128)S(1)}, f32[4,32,16]{1,2,0:T(8,128)}, u32[]{:S(2)}) copy-start(f32[4,32,16]{1,2,0:T(8,128)} %copy-done.57) | copy-start | bytes 24580
  56.8 13.5 %copy-start.64 = (f32[4,32,16]{1,2,0:T(8,128)S(1)}, f32[4,32,16]{1,2,0:T(8,128)}, u32[]{:S(2)}) copy-start(f32[4,32,16]{1,2,0:T(8,128)} %copy-done.63) | copy-start | bytes 24580
  56.8 6.6 %collective-permute-start.5 = (f32[1,32,1024]{2,1,0:T(8,128)}, f32[1,32,1024]{2,1,0:T(8,128)S(1)}, u32[]{:S(2)}, u32[]{:S(2)}) collective-permute-start(f32[1,32,1024]{2,1,0:T(8,128)} %slice.237), channel_id=1, source_target_pairs={{16,0},{32,16},{48,32},{64,48},{80,64},{96,80},{112,96},{128,112},... | collective-permute-start | bytes 393224 | tf_op jit(solution)/shard_map/ppermute | solution.py:22
  61.6 18.1 %copy-start.18 = (f32[1,32,1024]{2,1,0:T(8,128)}, f32[1,32,1024]{2,1,0:T(8,128)S(1)}, u32[]{:S(2)}) copy-start(f32[1,32,1024]{2,1,0:T(8,128)S(1)} %collective-permute-done.4) | copy-start | bytes 393220
  64.2 16.2 %collective-permute-start.6 = (f32[6,1,1024]{2,1,0:T(1,128)S(1)}, f32[6,1,1024]{2,1,0:T(1,128)S(1)}, u32[]{:S(2)}, u32[]{:S(2)}) collective-permute-start(f32[6,1,1024]{2,1,0:T(1,128)S(1)} %get-tuple-element.36), channel_id=1, source_target_pairs={{0,1},{1,2},{2,3},{3,4},{4,5},{5,6},{6,7},{7,8},{8,9},{9,10},{10,1... | collective-permute-start | bytes 73736 | tf_op jit(solution)/shard_map/ppermute | solution.py:19
  68.2 11.6 %copy-start.75 = (f32[4,32,16]{1,2,0:T(8,128)S(1)}, f32[4,32,16]{1,2,0:T(8,128)}, u32[]{:S(2)}) copy-start(f32[4,32,16]{1,2,0:T(8,128)} %get-tuple-element.10) | copy-start | bytes 24580
  68.2 11.6 %copy-start.74 = (f32[4,32,16]{1,2,0:T(8,128)S(1)}, f32[4,32,16]{1,2,0:T(8,128)}, u32[]{:S(2)}) copy-start(f32[4,32,16]{1,2,0:T(8,128)} %get-tuple-element.47) | copy-start | bytes 24580
  68.2 11.7 %copy-start.77 = (f32[4,32,16]{1,2,0:T(8,128)S(1)}, f32[4,32,16]{1,2,0:T(8,128)}, u32[]{:S(2)}) copy-start(f32[4,32,16]{1,2,0:T(8,128)} %get-tuple-element.16) | copy-start | bytes 24580
  68.2 11.8 %copy-start.76 = (f32[4,32,16]{1,2,0:T(8,128)S(1)}, f32[4,32,16]{1,2,0:T(8,128)}, u32[]{:S(2)}) copy-start(f32[4,32,16]{1,2,0:T(8,128)} %get-tuple-element.40) | copy-start | bytes 24580
  68.2 11.9 %copy-start.79 = (f32[4,32,16]{1,2,0:T(8,128)S(1)}, f32[4,32,16]{1,2,0:T(8,128)}, u32[]{:S(2)}) copy-start(f32[4,32,16]{1,2,0:T(8,128)} %get-tuple-element.22) | copy-start | bytes 24580
  68.2 11.9 %copy-start.78 = (f32[4,32,16]{1,2,0:T(8,128)S(1)}, f32[4,32,16]{1,2,0:T(8,128)}, u32[]{:S(2)}) copy-start(f32[4,32,16]{1,2,0:T(8,128)} %get-tuple-element.38) | copy-start | bytes 24580
  68.2 12.0 %copy-start.73 = (f32[4,32,16]{1,2,0:T(8,128)S(1)}, f32[4,32,16]{1,2,0:T(8,128)}, u32[]{:S(2)}) copy-start(f32[4,32,16]{1,2,0:T(8,128)} %get-tuple-element.6) | copy-start | bytes 24580
  68.3 12.1 %copy-start.20 = (f32[1,32,1024]{2,1,0:T(8,128)S(1)}, f32[1,32,1024]{2,1,0:T(8,128)}, u32[]{:S(2)}) copy-start(f32[1,32,1024]{2,1,0:T(8,128)} %copy-done.19) | copy-start | bytes 393220
  68.3 12.1 %collective-permute-start.7 = (f32[6,1,1024]{2,1,0:T(1,128)S(1)}, f32[6,1,1024]{2,1,0:T(1,128)S(1)}, u32[]{:S(2)}, u32[]{:S(2)}) collective-permute-start(f32[6,1,1024]{2,1,0:T(1,128)S(1)} %get-tuple-element.37), channel_id=1, source_target_pairs={{1,0},{2,1},{3,2},{4,3},{5,4},{6,5},{7,6},{8,7},{9,8},{10,9},{11,1... | collective-permute-start | bytes 73736 | tf_op jit(solution)/shard_map/ppermute | solution.py:22
  80.3 242.3 %copy-start.14 = (f32[4,32,16]{2,1,0:T(8,128)}, f32[4,32,16]{2,1,0:T(8,128)S(1)}, u32[]{:S(2)}) copy-start(f32[4,32,16]{2,1,0:T(8,128)S(1)} %copy.15) | copy-start | bytes 24580
  84.5 106.2 %copy-start.60 = (f32[4,32,16]{1,2,0:T(8,128)S(1)}, f32[4,32,16]{1,2,0:T(8,128)}, u32[]{:S(2)}) copy-start(f32[4,32,16]{1,2,0:T(8,128)} %copy-done.57) | copy-start | bytes 24580
  84.5 106.2 %copy-start.66 = (f32[4,32,16]{1,2,0:T(8,128)S(1)}, f32[4,32,16]{1,2,0:T(8,128)}, u32[]{:S(2)}) copy-start(f32[4,32,16]{1,2,0:T(8,128)} %copy-done.63) | copy-start | bytes 24580
  196.9 98.1 %copy-start.8 = (f32[4,32,16,64]{3,1,2,0:T(8,128)}, f32[4,32,16,64]{3,1,2,0:T(8,128)S(1)}, u32[]{:S(2)}) copy-start(f32[4,32,16,64]{3,1,2,0:T(8,128)S(1)} %convolution_subtract_fusion.2) | copy-start | bytes 1572868
  197.0 94.0 %copy-start.55 = (f32[4,32,16]{1,2,0:T(8,128)S(1)}, f32[4,32,16]{1,2,0:T(8,128)}, u32[]{:S(2)}) copy-start(f32[4,32,16]{1,2,0:T(8,128)} %copy-done.52) | copy-start | bytes 24580
  197.0 94.0 %copy-start.61 = (f32[4,32,16]{1,2,0:T(8,128)S(1)}, f32[4,32,16]{1,2,0:T(8,128)}, u32[]{:S(2)}) copy-start(f32[4,32,16]{1,2,0:T(8,128)} %copy-done.57) | copy-start | bytes 24580
  197.0 94.0 %copy-start.67 = (f32[4,32,16]{1,2,0:T(8,128)S(1)}, f32[4,32,16]{1,2,0:T(8,128)}, u32[]{:S(2)}) copy-start(f32[4,32,16]{1,2,0:T(8,128)} %copy-done.63) | copy-start | bytes 24580
  295.0 29.9 %copy-start = (f32[4,32,16,64]{3,1,2,0:T(8,128)}, f32[4,32,16,64]{3,1,2,0:T(8,128)S(1)}, u32[]{:S(2)}) copy-start(f32[4,32,16,64]{3,1,2,0:T(8,128)S(1)} %convolution_add_fusion.3) | copy-start | bytes 1572868
  296.8 9.0 %collective-permute-start.8 = (f32[1,32,1024]{2,1,0:T(8,128)}, f32[1,32,1024]{2,1,0:T(8,128)}, u32[]{:S(2)}, u32[]{:S(2)}) collective-permute-start(f32[1,32,1024]{2,1,0:T(8,128)} %slice.248), channel_id=1, source_target_pairs={{0,16},{16,32},{32,48},{48,64},{64,80},{80,96},{96,112},{112,128},... | collective-permute-start | bytes 393224 | tf_op jit(solution)/shard_map/ppermute | solution.py:19
  303.2 6.3 collective-permute-start.9
  309.6 10.2 %collective-permute-start.10 = (f32[6,1,1024]{2,1,0:T(1,128)S(1)}, f32[6,1,1024]{2,1,0:T(1,128)S(1)}, u32[]{:S(2)}, u32[]{:S(2)}) collective-permute-start(f32[6,1,1024]{2,1,0:T(1,128)S(1)} %get-tuple-element.34), channel_id=1, source_target_pairs={{0,1},{1,2},{2,3},{3,4},{4,5},{5,6},{6,7},{7,8},{8,9},{9,10},{10,1... | collective-permute-start | bytes 73736 | tf_op jit(solution)/shard_map/ppermute | solution.py:19
  312.7 7.1 %collective-permute-start.11 = (f32[6,1,1024]{2,1,0:T(1,128)S(1)}, f32[6,1,1024]{2,1,0:T(1,128)S(1)}, u32[]{:S(2)}, u32[]{:S(2)}) collective-permute-start(f32[6,1,1024]{2,1,0:T(1,128)S(1)} %get-tuple-element.35), channel_id=1, source_target_pairs={{1,0},{2,1},{3,2},{4,3},{5,4},{6,5},{7,6},{8,7},{9,8},{10,9},{11,1... | collective-permute-start | bytes 73736 | tf_op jit(solution)/shard_map/ppermute | solution.py:22
  325.9 92.3 %copy-start.9 = (f32[4,32,16,64]{3,1,2,0:T(8,128)S(1)}, f32[4,32,16,64]{3,1,2,0:T(8,128)}, u32[]{:S(2)}) copy-start(f32[4,32,16,64]{3,1,2,0:T(8,128)} %copy-done.8) | copy-start | bytes 1572868
  420.6 75.9 %copy-start.1 = (f32[4,32,16,64]{3,1,2,0:T(8,128)S(1)}, f32[4,32,16,64]{3,1,2,0:T(8,128)}, u32[]{:S(2)}) copy-start(f32[4,32,16,64]{3,1,2,0:T(8,128)} %copy-done) | copy-start | bytes 1572868
  498.6 6.6 %copy-start.35 = (f32[4,32,16]{1,2,0:T(8,128)S(1)}, f32[4,32,16]{1,2,0:T(8,128)}, u32[]{:S(2)}) copy-start(f32[4,32,16]{1,2,0:T(8,128)} %copy-done.33) | copy-start | bytes 24580
  498.6 6.6 %copy-start.38 = (f32[4,32,16]{1,2,0:T(8,128)S(1)}, f32[4,32,16]{1,2,0:T(8,128)}, u32[]{:S(2)}) copy-start(f32[4,32,16]{1,2,0:T(8,128)} %copy-done.36) | copy-start | bytes 24580
  498.6 6.6 %copy-start.41 = (f32[4,32,16]{1,2,0:T(8,128)S(1)}, f32[4,32,16]{1,2,0:T(8,128)}, u32[]{:S(2)}) copy-start(f32[4,32,16]{1,2,0:T(8,128)} %copy-done.39) | copy-start | bytes 24580
  498.6 6.6 %copy-start.44 = (f32[4,32,16]{1,2,0:T(8,128)S(1)}, f32[4,32,16]{1,2,0:T(8,128)}, u32[]{:S(2)}) copy-start(f32[4,32,16]{1,2,0:T(8,128)} %copy-done.42) | copy-start | bytes 24580
  498.6 6.6 %copy-start.47 = (f32[4,32,16]{1,2,0:T(8,128)S(1)}, f32[4,32,16]{1,2,0:T(8,128)}, u32[]{:S(2)}) copy-start(f32[4,32,16]{1,2,0:T(8,128)} %copy-done.45) | copy-start | bytes 24580
  498.6 6.6 %copy-start.51 = (f32[4,32,16]{1,2,0:T(8,128)S(1)}, f32[4,32,16]{1,2,0:T(8,128)}, u32[]{:S(2)}) copy-start(f32[4,32,16]{1,2,0:T(8,128)} %copy-done.48) | copy-start | bytes 24580
  498.6 6.6 %copy-start.56 = (f32[4,32,16]{1,2,0:T(8,128)S(1)}, f32[4,32,16]{1,2,0:T(8,128)}, u32[]{:S(2)}) copy-start(f32[4,32,16]{1,2,0:T(8,128)} %copy-done.52) | copy-start | bytes 24580
  498.6 6.6 %copy-start.62 = (f32[4,32,16]{1,2,0:T(8,128)S(1)}, f32[4,32,16]{1,2,0:T(8,128)}, u32[]{:S(2)}) copy-start(f32[4,32,16]{1,2,0:T(8,128)} %copy-done.57) | copy-start | bytes 24580
  498.7 6.6 %copy-start.68 = (f32[4,32,16]{1,2,0:T(8,128)S(1)}, f32[4,32,16]{1,2,0:T(8,128)}, u32[]{:S(2)}) copy-start(f32[4,32,16]{1,2,0:T(8,128)} %copy-done.63) | copy-start | bytes 24580
  498.7 6.6 %copy-start.81 = (f32[64,64,1,1]{1,0,3,2:T(8,128)S(1)}, f32[64,64,1,1]{1,0,3,2:T(8,128)}, u32[]{:S(2)}) copy-start(f32[64,64,1,1]{1,0,3,2:T(8,128)} %copy-done.80) | copy-start | bytes 49156
  500.3 11.2 %copy-start.3 = (f32[4,32,16,64]{3,1,2,0:T(8,128)S(1)}, f32[4,32,16,64]{3,1,2,0:T(8,128)}, u32[]{:S(2)}) copy-start(f32[4,32,16,64]{3,1,2,0:T(8,128)} %copy-done.2) | copy-start | bytes 1572868
  500.3 18.6 %collective-permute-start.12 = (f32[1,32,1024]{2,1,0:T(8,128)}, f32[1,32,1024]{2,1,0:T(8,128)}, u32[]{:S(2)}, u32[]{:S(2)}) collective-permute-start(f32[1,32,1024]{2,1,0:T(8,128)} %slice.261), channel_id=1, source_target_pairs={{0,16},{16,32},{32,48},{48,64},{64,80},{80,96},{96,112},{112,128},... | collective-permute-start | bytes 393224 | tf_op jit(solution)/shard_map/ppermute | solution.py:19
  513.2 14.8 %copy-start.16 = (f32[4,32,16,64]{3,1,2,0:T(8,128)S(1)}, f32[4,32,16,64]{3,1,2,0:T(8,128)}, u32[]{:S(2)}) copy-start(f32[4,32,16,64]{3,1,2,0:T(8,128)} %fusion.55) | copy-start | bytes 1572868
  516.8 11.2 %copy-start.22 = (f32[64,64,1,1]{1,0,3,2:T(8,128)S(1)}, f32[64,64,1,1]{1,0,3,2:T(8,128)}, u32[]{:S(2)}) copy-start(f32[64,64,1,1]{1,0,3,2:T(8,128)} %copy-done.21) | copy-start | bytes 49156
  516.8 6.6 %collective-permute-start.13 = (f32[1,32,1024]{2,1,0:T(8,128)}, f32[1,32,1024]{2,1,0:T(8,128)S(1)}, u32[]{:S(2)}, u32[]{:S(2)}) collective-permute-start(f32[1,32,1024]{2,1,0:T(8,128)} %slice.263), channel_id=1, source_target_pairs={{16,0},{32,16},{48,32},{64,48},{80,64},{96,80},{112,96},{128,112},... | collective-permute-start | bytes 393224 | tf_op jit(solution)/shard_map/ppermute | solution.py:22
  523.5 6.5 %collective-permute-start.14 = (f32[6,1,1024]{2,1,0:T(1,128)S(1)}, f32[6,1,1024]{2,1,0:T(1,128)S(1)}, u32[]{:S(2)}, u32[]{:S(2)}) collective-permute-start(f32[6,1,1024]{2,1,0:T(1,128)S(1)} %get-tuple-element.32), channel_id=1, source_target_pairs={{0,1},{1,2},{2,3},{3,4},{4,5},{5,6},{6,7},{7,8},{8,9},{9,10},{10,1... | collective-permute-start | bytes 73736 | tf_op jit(solution)/shard_map/ppermute | solution.py:19
  526.7 4.6 collective-permute-start.15
  538.2 91.1 %copy-start.24 = (f32[64,64]{1,0:T(8,128)S(1)}, f32[64,64]{1,0:T(8,128)}, u32[]{:S(2)}) copy-start(f32[64,64]{1,0:T(8,128)} %copy-done.23) | copy-start | bytes 49156
  (35 other events, 88.8 us)
where the time goes:
time: 647 us; the launch traced here: 637 us
  blocking collectives  389 us (60%)
  other arithmetic  81.9 us (13%)
  local copies, waits for them, and re-layouts  54.7 us (8%)
  matrix products  49.8 us (8%)
  starting transfers between devices  47.4 us (7%)
  waiting for transfers between devices  11.1 us (2%)
    psum x2, blocking collectives, shards(): curve_gram = lax.psum(inner_block(search, image_block), ('gx', 'gy'))  154 us
    psum x2, blocking collectives, shards(): norm_next = lax.psum(inner_block(residual, residual), ('gx', 'gy'))  147 us
    psum x1, blocking collectives, shards(): norm_now = lax.psum(inner_block(residual, residual), ('gx', 'gy'))  87.6 us
    another operation x15, other arithmetic, solve_gram(): factor = jnp.linalg.cholesky(matrix)  32.6 us
    ppermute x8, starting transfers between devices, extended(): lax.ppermute(lax.slice_in_dim(block, block.shape[dim] - width, None, axis...  30.3 us
    another operation x10, other arithmetic, solve_gram(): return jax.scipy.linalg.cho_solve((factor, True), right_side)  27.7 us
    dot_general x8, matrix products, times_block(): jnp.dot(field.reshape(-1, width), matrix, precision=HIGH)  25.2 us
    dot_general x6, matrix products, inner_block(): lax.dot_general(first_block.reshape(-1, width), second_block.reshape(-1,...  22.6 us
  transfers between devices with their start and end apart: 16, of which 7 were waited for; matrix products, arithmetic and copies ran while one was open for 6% of the time, Pallas kernels for 0%

commit v1 on v0

v1 whole, which is shorter than its diff:
```python
import jax
import jax.numpy as jnp
from jax import lax
from jax.experimental import pallas as pl
from jax.experimental.pallas import tpu as pltpu
from jax.sharding import PartitionSpec as P

NZ = 16
K = 64
ITERS = 3
DEEP = ITERS + 1

HIGH = lax.Precision.HIGHEST
F32 = jnp.float32


def face(here, there):
    product = here * there
    return 2.0 * product / jnp.where(product > 0, here + there, 1.0)


def krylov_kernel(
    up_ref, here_ref, down_ref, fields_ref, moments_ref,
    cond, label, couple, weight, nbr, diag, v0, v1, v2, v3,
):
    rows = here_ref.shape[1]
    lanes = here_ref.shape[2]
    own = fields_ref.shape[1] // rows
    tall = rows + 2 * DEEP
    for plane, ref in ((0, cond), (1, label)):
        ref[0:DEEP, :] = up_ref[plane]
        ref[DEEP:DEEP + rows, :] = here_ref[plane]
        ref[DEEP + rows:tall, :] = down_ref[plane]
    inner = tall - 2
    lane = lax.broadcasted_iota(jnp.int32, (inner, lanes), 1)
    depth = lane & (NZ - 1)
    center = cond[1:1 + inner, :]
    free = jnp.where((center > 0) & (label[1:1 + inner, :] == 0), 1.0, 0.0)

    def views(ref):
        mid = ref[1:1 + inner, :]
        return [
            ref[2:2 + inner, :],
            ref[0:inner, :],
            pltpu.roll(mid, lanes - NZ, 1),
            pltpu.roll(mid, NZ, 1),
            jnp.where(depth == NZ - 1, 0.0, pltpu.roll(mid, lanes - 1, 1)),
            jnp.where(depth == 0, 0.0, pltpu.roll(mid, 1, 1)),
        ]

    total = jnp.zeros((inner, lanes), F32)
    for side, (there, mark) in enumerate(zip(views(cond), views(label))):
        conduct = face(center, there)
        total = total + conduct
        weight[side] = free * conduct
        nbr[side] = mark
        couple[side] = jnp.where(mark == 0, free * conduct, 0.0)
    diag[...] = free * total + (1.0 - free)

    step = 16
    cluster = lax.broadcasted_iota(jnp.int32, (step, lanes), 0)

    def fill(row, carry):
        for part in range(0, K, step):
            ids = (cluster + (part + 1)).astype(F32)
            acc = jnp.zeros((step, lanes), F32)
            for side in range(6):
                hit = nbr[side, pl.ds(row, 1), :] == ids
                acc = acc + jnp.where(hit, weight[side, pl.ds(row, 1), :], 0.0)
            v0[row, part:part + step, :] = acc
        return carry

    lax.fori_loop(0, inner, fill, 0)

    def power(source, target, offset, count):
        def body(row, carry):
            at = row + offset + 1
            for part in range(0, K, step):
                cut = slice(part, part + step)
                mid = source[row + 1, cut, :]
                acc = diag[pl.ds(at, 1), :] * mid
                acc = acc - couple[0, pl.ds(at, 1), :] * source[row + 2, cut, :]
                acc = acc - couple[1, pl.ds(at, 1), :] * source[row, cut, :]
                acc = acc - couple[2, pl.ds(at, 1), :] * pltpu.roll(mid, lanes - NZ, 1)
                acc = acc - couple[3, pl.ds(at, 1), :] * pltpu.roll(mid, NZ, 1)
                acc = acc - couple[4, pl.ds(at, 1), :] * pltpu.roll(mid, lanes - 1, 1)
                acc = acc - couple[5, pl.ds(at, 1), :] * pltpu.roll(mid, 1, 1)
                target[row, cut, :] = acc
            return carry

        lax.fori_loop(0, count, body, 0)

    power(v0, v1, 0, inner - 2)
    power(v1, v2, 1, inner - 4)
    power(v2, v3, 2, inner - 6)
    for order, ref in enumerate((v0, v1, v2, v3)):
        for row in range(rows):
            fields_ref[order * K:(order + 1) * K, row * own:(row + 1) * own] = ref[
                row + ITERS - order, :, 0:own
            ]
    chunk = 256
    wide = fields_ref.shape[1]
    for pair in range(ITERS):
        parts = []
        for at in range(0, wide, chunk):
            left = fields_ref[pair * K:(pair + 1) * K, at:at + chunk]
            right = fields_ref[pair * K:(pair + 2) * K, at:at + chunk]
            parts.append(lax.dot_general(
                left, right, (((1,), (1,)), ((), ())), precision=HIGH, preferred_element_type=F32
            ))
        while len(parts) > 1:
            parts = [parts[i] + parts[i + 1] for i in range(0, len(parts), 2)]
        moments_ref[pair * K:(pair + 1) * K, :] = parts[0]


def krylov(up, here, down):
    rows, lanes = here.shape[1:]
    own = lanes - 2 * DEEP * NZ
    tall = rows + 2 * DEEP
    inner = tall - 2
    return pl.pallas_call(
        krylov_kernel,
        out_shape=(
            jax.ShapeDtypeStruct(((ITERS + 1) * K, rows * own), F32),
            jax.ShapeDtypeStruct((ITERS * K, 2 * K), F32),
        ),
        in_specs=[pl.BlockSpec(memory_space=pltpu.VMEM)] * 3,
        out_specs=[pl.BlockSpec(memory_space=pltpu.VMEM)] * 2,
        scratch_shapes=[
            pltpu.VMEM((tall, lanes), F32),
            pltpu.VMEM((tall, lanes), F32),
            pltpu.VMEM((6, inner, lanes), F32),
            pltpu.VMEM((6, inner, lanes), F32),
            pltpu.VMEM((6, inner, lanes), F32),
            pltpu.VMEM((inner, lanes), F32),
            pltpu.VMEM((inner, K, lanes), F32),
            pltpu.VMEM((inner - 2, K, lanes), F32),
            pltpu.VMEM((inner - 4, K, lanes), F32),
            pltpu.VMEM((inner - 6, K, lanes), F32),
        ],
        compiler_params=pltpu.CompilerParams(vmem_limit_bytes=40 * 1024 * 1024),
    )(up, here, down)


def gauss_jordan(work, size, panel=8):
    total = work.shape[1]
    sub = lax.broadcasted_iota(jnp.int32, (panel, 128), 0)
    for at in range(0, size, panel):
        tiles = [t for t in range(0, total, 128) if t + 128 > at + panel]
        base = at // 128 * 128
        column = work[:, base:base + 128]
        spread = [
            jnp.broadcast_to(column[:, at - base + j:at - base + j + 1], (size, 128))
            for j in range(panel)
        ]
        small = [s[at:at + panel] for s in spread]
        rows = [work[at:at + panel, t:t + 128] for t in tiles]
        for j in range(panel):
            inverse = 1.0 / jnp.broadcast_to(small[j][j:j + 1], (panel, 128))
            mine = sub == j
            factor = small[j]
            for m in range(j + 1, panel):
                scaled = jnp.broadcast_to(small[m][j:j + 1], (panel, 128)) * inverse
                small[m] = jnp.where(mine, scaled, small[m] - factor * scaled)
            for i, value in enumerate(rows):
                scaled = jnp.broadcast_to(value[j:j + 1], (panel, 128)) * inverse
                rows[i] = jnp.where(mine, scaled, value - factor * scaled)
        for i, t in enumerate(tiles):
            for first, last in ((0, at), (at + panel, size)):
                if first == last:
                    continue
                acc = work[first:last, t:t + 128]
                for j in range(panel):
                    acc = acc - spread[j][first:last] * rows[i][j:j + 1]
                work[first:last, t:t + 128] = acc
            work[at:at + panel, t:t + 128] = rows[i]


def finish_kernel(moments_ref, fields_ref, solution_ref, residual_ref, work, coeff, mixed):
    rows, cols = solution_ref.shape[:2]
    size = ITERS * K

    def moment(k):
        pair, half = divmod(k, 2)
        return moments_ref[pair * K:(pair + 1) * K, half * K:(half + 1) * K]

    moments = []
    for k in range(2 * ITERS):
        value = moment(k)
        moments.append(0.5 * (value + value.T))
    for i in range(ITERS):
        for j in range(ITERS):
            work[i * K:(i + 1) * K, j * K:(j + 1) * K] = moments[i + j + 1]
        work[i * K:(i + 1) * K, size:size + K] = moments[i]
    gauss_jordan(work, size)
    answer = work[:, size:size + K]
    coeff[0:size, 0:K] = answer
    coeff[size:size + K, 0:K] = jnp.zeros((K, K), F32)
    coeff[0:K, K:2 * K] = (
        lax.broadcasted_iota(jnp.int32, (K, K), 0) == lax.broadcasted_iota(jnp.int32, (K, K), 1)
    ).astype(F32)
    coeff[K:K + size, K:2 * K] = -answer
    own = cols * NZ
    low = lax.broadcasted_iota(jnp.int32, (cols, 2 * K), 1) < K
    for row in range(rows):
        mixed[...] = lax.dot_general(
            fields_ref[:, row * own:(row + 1) * own], coeff[...], (((0,), (0,)), ((), ())),
            precision=HIGH, preferred_element_type=F32,
        )
        for z in range(0, NZ, 2):
            even = mixed[pl.ds(z, cols, stride=NZ), :]
            odd = mixed[pl.ds(z + 1, cols, stride=NZ), :]
            solution_ref[row, :, z * K:(z + 2) * K] = jnp.where(low, even, pltpu.roll(odd, K, 1))
            residual_ref[row, :, z * K:(z + 2) * K] = jnp.where(low, pltpu.roll(even, K, 1), odd)


def finish(moments, fields, rows, cols):
    out = jax.ShapeDtypeStruct((rows, cols, NZ * K), F32)
    return pl.pallas_call(
        finish_kernel,
        out_shape=(out, out),
        in_specs=[pl.BlockSpec(memory_space=pltpu.VMEM)] * 2,
        out_specs=[pl.BlockSpec(memory_space=pltpu.VMEM)] * 2,
        scratch_shapes=[
            pltpu.VMEM((ITERS * K, (ITERS + 1) * K), F32),
            pltpu.VMEM(((ITERS + 1) * K, 2 * K), F32),
            pltpu.VMEM((cols * NZ, 2 * K), F32),
        ],
        compiler_params=pltpu.CompilerParams(vmem_limit_bytes=40 * 1024 * 1024),
    )(moments, fields)


def total_over(value, axis):
    count = lax.axis_size(axis)
    stride = 1
    while stride < count:
        value = value + lax.ppermute(value, axis, [(i, i ^ stride) for i in range(count)])
        stride *= 2
    return value


def from_both(first, last, axis):
    count = lax.axis_size(axis)
    forward = [(i, i + 1) for i in range(count - 1)]
    backward = [(target, source) for source, target in forward]
    return lax.ppermute(last, axis, forward), lax.ppermute(first, axis, backward)


def shards(diffusivity, labels, obstacles):
    rows, cols = diffusivity.shape[:2]
    conductive = diffusivity * (1 - obstacles).astype(F32)
    cells = jnp.stack([conductive, labels.astype(F32)]).reshape(2, rows, cols * NZ)
    edge = DEEP * NZ
    before, after = from_both(cells[:, :, :edge], cells[:, :, -edge:], "gy")
    here = jnp.concatenate([cells, after, before], axis=2)
    up, down = from_both(here[:, :DEEP], here[:, rows - DEEP:], "gx")
    fields, moments = krylov(up, here, down)
    moments = total_over(total_over(moments, "gx"), "gy")
    return finish(moments, fields, rows, cols)


def solution(mesh):
    in_specs = (P("gx", "gy", None), P("gx", "gy", None), P("gx", "gy", None))
    out_specs = (P("gx", "gy", None), P("gx", "gy", None))
    return jax.shard_map(shards, mesh=mesh, in_specs=in_specs, out_specs=out_specs, check_vma=False)
```

time: 647 us -> 92.1 us (0.14)
  the two profiles are of different devices: /device:TPU:1 before, /device:TPU:16 now
where the time goes in v1:
time: 92.1 us; the launch traced here: 91.8 us
  waiting for transfers between devices  39.3 us (43%)
  starting transfers between devices  28 us (30%)
  Pallas kernels  21.6 us (23%)
  other arithmetic  1.72 us (2%)
    ppermute x8, waiting for transfers between devices, total_over(): lax.ppermute(value, axis, [(i, i ^ stride) for i in range(count)])  32.8 us
    ppermute x8, starting transfers between devices, total_over(): lax.ppermute(value, axis, [(i, i ^ stride) for i in range(count)])  17.2 us
    pallas_call x1, Pallas kernels, finish(): pl.pallas_call(finish_kernel, out_shape=(out, out), in_specs=[pl.BlockSpe...  12.3 us
    pallas_call x1, Pallas kernels, krylov(): pl.pallas_call(krylov_kernel, out_shape=(jax.ShapeDtypeStruct(((ITERS + 1...  9.28 us
    ppermute x2, waiting for transfers between devices, from_both(): lax.ppermute(last, axis, forward)  6.49 us
    ppermute x2, starting transfers between devices, from_both(): lax.ppermute(first, axis, backward)  5.83 us
    ppermute x2, starting transfers between devices, from_both(): lax.ppermute(last, axis, forward)  4.95 us
  transfers between devices with their start and end apart: 12, of which 10 were waited for; matrix products, arithmetic and copies ran while one was open for 0% of the time, Pallas kernels for 0%

profile of v1, /device:TPU:16, one launch (start us, length us, event | category | flops | bytes accessed | tf_op | source)
XLA Modules:
  0.0 91.8 jit_solution(249967495084618250)
XLA Ops:
  0.6 0.8 convert_multiply_fusion
  1.4 0.1 copy.7
  1.5 0.1 stack.9
  1.6 0.8 convert_element_type.7
  2.4 0.1 copy.8
  2.4 0.1 stack.10
  2.6 0.1 fusion
  2.6 4.5 %collective-permute-start = (f32[2,4,64]{2,1,0:T(4,128)S(1)}, f32[2,4,64]{2,1,0:T(4,128)S(1)}, u32[]{:S(2)}, u32[]{:S(2)}) collective-permute-start(f32[2,4,64]{2,1,0:T(4,128)S(1)} %get-tuple-element.6), channel_id=1, source_target_pairs={{1,0},{2,1},{3,2},{4,3},{5,4},{6,5},{7,6},{8,7},{9,8},{10,9},{11,1... | collective-permute-start | bytes 6152 | tf_op jit(solution)/shard_map/ppermute | solution.py:246
  7.2 1.9 %collective-permute-start.1 = (f32[2,4,64]{2,1,0:T(4,128)S(1)}, f32[2,4,64]{2,1,0:T(4,128)S(1)}, u32[]{:S(2)}, u32[]{:S(2)}) collective-permute-start(f32[2,4,64]{2,1,0:T(4,128)S(1)} %get-tuple-element.7), channel_id=1, source_target_pairs={{0,1},{1,2},{2,3},{3,4},{4,5},{5,6},{6,7},{7,8},{8,9},{9,10},{10,1... | collective-permute-start | bytes 6152 | tf_op jit(solution)/shard_map/ppermute | solution.py:246
  9.1 0.0 collective-permute-done
  9.1 5.7 %collective-permute-done.1 = f32[2,4,64]{2,1,0:T(4,128)S(1)} collective-permute-done((f32[2,4,64]{2,1,0:T(4,128)S(1)}, f32[2,4,64]{2,1,0:T(4,128)S(1)}, u32[]{:S(2)}, u32[]{:S(2)}) %collective-permute-start.1) | collective-permute-done | bytes 2080 | tf_op jit(solution)/shard_map/ppermute | solution.py:246
  14.8 0.1 pad_maximum_fusion.here_ref
  14.9 1.3 %collective-permute-start.3 = (f32[2,4,640]{2,1,0:T(4,128)S(1)}, f32[2,4,640]{2,1,0:T(4,128)S(1)}, u32[]{:S(2)}, u32[]{:S(2)}) collective-permute-start(f32[2,4,640]{2,1,0:T(4,128)S(1)} %pad_maximum_fusion.here_ref), channel_id=1, source_target_pairs={{16,0},{32,16},{48,32},{64,48},{80,64},{96,80},{112,96},{128,112},... | collective-permute-start | bytes 61448 | tf_op jit(solution)/shard_map/ppermute | solution.py:246
  16.2 3.0 %collective-permute-start.2 = (f32[2,4,640]{2,1,0:T(4,128)S(1)}, f32[2,4,640]{2,1,0:T(4,128)S(1)}, u32[]{:S(2)}, u32[]{:S(2)}) collective-permute-start(f32[2,4,640]{2,1,0:T(4,128)S(1)} %pad_maximum_fusion.here_ref), channel_id=1, source_target_pairs={{0,16},{16,32},{32,48},{48,64},{64,80},{80,96},{96,112},{112,128},... | collective-permute-start | bytes 61448 | tf_op jit(solution)/shard_map/ppermute | solution.py:246
  19.2 0.0 collective-permute-done.3.down_ref
  19.2 0.8 collective-permute-done.2.up_ref
  20.0 9.3 %shard_map.50 = (f32[256,2048]{1,0:T(8,128)S(1)}, f32[192,128]{1,0:T(8,128)S(1)}) custom-call(f32[2,4,640]{2,1,0:T(4,128)S(1)} %collective-permute-done.2.up_ref, f32[2,4,640]{2,1,0:T(4,128)S(1)} %pad_maximum_fusion.here_ref, f32[2,4,640]{2,1,0:T(4,128)S(1)} %collective-permute-done.3.down_ref), custom_call_target="tpu_custom_call" | custom-call | tf_op jit(solution)/shard_map/pallas_call | solution.py:121
  29.3 1.7 %collective-permute-start.4 = (f32[192,128]{1,0:T(8,128)S(1)}, f32[192,128]{1,0:T(8,128)S(1)}, u32[]{:S(2)}, u32[]{:S(2)}) collective-permute-start(f32[192,128]{1,0:T(8,128)S(1)} %get-tuple-element.4), channel_id=1, source_target_pairs={{0,16},{16,0},{32,48},{48,32},{64,80},{80,64},{96,112},{112,96},{1... | collective-permute-start | bytes 294920 | tf_op jit(solution)/shard_map/ppermute | solution.py:237
  31.0 0.9 %collective-permute-done.4 = f32[192,128]{1,0:T(8,128)S(1)} collective-permute-done((f32[192,128]{1,0:T(8,128)S(1)}, f32[192,128]{1,0:T(8,128)S(1)}, u32[]{:S(2)}, u32[]{:S(2)}) %collective-permute-start.4) | collective-permute-done | bytes 98336 | tf_op jit(solution)/shard_map/ppermute | solution.py:237
  32.0 2.6 %collective-permute-start.5 = (f32[192,128]{1,0:T(8,128)S(1)}, f32[192,128]{1,0:T(8,128)S(1)}, u32[]{:S(2)}, u32[]{:S(2)}) collective-permute-start(f32[192,128]{1,0:T(8,128)S(1)} %add.24), channel_id=1, source_target_pairs={{0,32},{16,48},{32,0},{48,16},{64,96},{80,112},{96,64},{112,80},{1... | collective-permute-start | bytes 294920 | tf_op jit(solution)/shard_map/ppermute | solution.py:237
  34.6 3.1 %collective-permute-done.5 = f32[192,128]{1,0:T(8,128)S(1)} collective-permute-done((f32[192,128]{1,0:T(8,128)S(1)}, f32[192,128]{1,0:T(8,128)S(1)}, u32[]{:S(2)}, u32[]{:S(2)}) %collective-permute-start.5) | collective-permute-done | bytes 98336 | tf_op jit(solution)/shard_map/ppermute | solution.py:237
  37.7 4.1 %collective-permute-start.6 = (f32[192,128]{1,0:T(8,128)S(1)}, f32[192,128]{1,0:T(8,128)S(1)}, u32[]{:S(2)}, u32[]{:S(2)}) collective-permute-start(f32[192,128]{1,0:T(8,128)S(1)} %add.25), channel_id=1, source_target_pairs={{0,64},{16,80},{32,96},{48,112},{64,0},{80,16},{96,32},{112,48},{1... | collective-permute-start | bytes 294920 | tf_op jit(solution)/shard_map/ppermute | solution.py:237
  41.9 4.8 %collective-permute-done.6 = f32[192,128]{1,0:T(8,128)S(1)} collective-permute-done((f32[192,128]{1,0:T(8,128)S(1)}, f32[192,128]{1,0:T(8,128)S(1)}, u32[]{:S(2)}, u32[]{:S(2)}) %collective-permute-start.6) | collective-permute-done | bytes 98336 | tf_op jit(solution)/shard_map/ppermute | solution.py:237
  46.7 6.4 %collective-permute-start.7 = (f32[192,128]{1,0:T(8,128)S(1)}, f32[192,128]{1,0:T(8,128)S(1)}, u32[]{:S(2)}, u32[]{:S(2)}) collective-permute-start(f32[192,128]{1,0:T(8,128)S(1)} %add.26), channel_id=1, source_target_pairs={{0,128},{16,144},{32,160},{48,176},{64,192},{80,208},{96,224},{112... | collective-permute-start | bytes 294920 | tf_op jit(solution)/shard_map/ppermute | solution.py:237
  53.2 2.8 %collective-permute-done.7 = f32[192,128]{1,0:T(8,128)S(1)} collective-permute-done((f32[192,128]{1,0:T(8,128)S(1)}, f32[192,128]{1,0:T(8,128)S(1)}, u32[]{:S(2)}, u32[]{:S(2)}) %collective-permute-start.7) | collective-permute-done | bytes 98336 | tf_op jit(solution)/shard_map/ppermute | solution.py:237
  55.9 0.1 collective-permute-start.8
  56.0 5.2 %collective-permute-done.8 = f32[192,128]{1,0:T(8,128)S(1)} collective-permute-done((f32[192,128]{1,0:T(8,128)S(1)}, f32[192,128]{1,0:T(8,128)S(1)}, u32[]{:S(2)}, u32[]{:S(2)}) %collective-permute-start.8) | collective-permute-done | bytes 98336 | tf_op jit(solution)/shard_map/ppermute | solution.py:237
  61.2 0.1 collective-permute-start.9
  61.3 6.1 %collective-permute-done.9 = f32[192,128]{1,0:T(8,128)S(1)} collective-permute-done((f32[192,128]{1,0:T(8,128)S(1)}, f32[192,128]{1,0:T(8,128)S(1)}, u32[]{:S(2)}, u32[]{:S(2)}) %collective-permute-start.9) | collective-permute-done | bytes 98336 | tf_op jit(solution)/shard_map/ppermute | solution.py:237
  67.5 1.8 %collective-permute-start.10 = (f32[192,128]{1,0:T(8,128)S(1)}, f32[192,128]{1,0:T(8,128)S(1)}, u32[]{:S(2)}, u32[]{:S(2)}) collective-permute-start(f32[192,128]{1,0:T(8,128)S(1)} %add.29), channel_id=1, source_target_pairs={{0,4},{1,5},{2,6},{3,7},{4,0},{5,1},{6,2},{7,3},{8,12},{9,13},{10,... | collective-permute-start | bytes 294920 | tf_op jit(solution)/shard_map/ppermute | solution.py:237
  69.3 3.7 %collective-permute-done.10 = f32[192,128]{1,0:T(8,128)S(1)} collective-permute-done((f32[192,128]{1,0:T(8,128)S(1)}, f32[192,128]{1,0:T(8,128)S(1)}, u32[]{:S(2)}, u32[]{:S(2)}) %collective-permute-start.10) | collective-permute-done | bytes 98336 | tf_op jit(solution)/shard_map/ppermute | solution.py:237
  73.0 0.3 collective-permute-start.11
  73.3 6.1 %collective-permute-done.11 = f32[192,128]{1,0:T(8,128)S(1)} collective-permute-done((f32[192,128]{1,0:T(8,128)S(1)}, f32[192,128]{1,0:T(8,128)S(1)}, u32[]{:S(2)}, u32[]{:S(2)}) %collective-permute-start.11) | collective-permute-done | bytes 98336 | tf_op jit(solution)/shard_map/ppermute | solution.py:237
  79.5 12.3 %shard_map.51 = (f32[4,32,1024]{2,1,0:T(8,128)}, f32[4,32,1024]{2,1,0:T(8,128)}) custom-call(f32[192,128]{1,0:T(8,128)S(1)} %add.31.moments_ref, f32[256,2048]{1,0:T(8,128)S(1)} %get-tuple-element.5.fields_ref), custom_call_target="tpu_custom_call" | custom-call | tf_op jit(solution)/shard_map/pallas_call | solution.py:219
  (10 shorter events, 0.1 us)
Async XLA Ops:
  2.6 6.5 %collective-permute-start = (f32[2,4,64]{2,1,0:T(4,128)S(1)}, f32[2,4,64]{2,1,0:T(4,128)S(1)}, u32[]{:S(2)}, u32[]{:S(2)}) collective-permute-start(f32[2,4,64]{2,1,0:T(4,128)S(1)} %get-tuple-element.6), channel_id=1, source_target_pairs={{1,0},{2,1},{3,2},{4,3},{5,4},{6,5},{7,6},{8,7},{9,8},{10,9},{11,1... | collective-permute-start | bytes 6152 | tf_op jit(solution)/shard_map/ppermute | solution.py:246
  7.2 7.6 %collective-permute-start.1 = (f32[2,4,64]{2,1,0:T(4,128)S(1)}, f32[2,4,64]{2,1,0:T(4,128)S(1)}, u32[]{:S(2)}, u32[]{:S(2)}) collective-permute-start(f32[2,4,64]{2,1,0:T(4,128)S(1)} %get-tuple-element.7), channel_id=1, source_target_pairs={{0,1},{1,2},{2,3},{3,4},{4,5},{5,6},{6,7},{7,8},{8,9},{9,10},{10,1... | collective-permute-start | bytes 6152 | tf_op jit(solution)/shard_map/ppermute | solution.py:246
  14.9 4.3 %collective-permute-start.3 = (f32[2,4,640]{2,1,0:T(4,128)S(1)}, f32[2,4,640]{2,1,0:T(4,128)S(1)}, u32[]{:S(2)}, u32[]{:S(2)}) collective-permute-start(f32[2,4,640]{2,1,0:T(4,128)S(1)} %pad_maximum_fusion.here_ref), channel_id=1, source_target_pairs={{16,0},{32,16},{48,32},{64,48},{80,64},{96,80},{112,96},{128,112},... | collective-permute-start | bytes 61448 | tf_op jit(solution)/shard_map/ppermute | solution.py:246
  16.2 3.9 %collective-permute-start.2 = (f32[2,4,640]{2,1,0:T(4,128)S(1)}, f32[2,4,640]{2,1,0:T(4,128)S(1)}, u32[]{:S(2)}, u32[]{:S(2)}) collective-permute-start(f32[2,4,640]{2,1,0:T(4,128)S(1)} %pad_maximum_fusion.here_ref), channel_id=1, source_target_pairs={{0,16},{16,32},{32,48},{48,64},{64,80},{80,96},{96,112},{112,128},... | collective-permute-start | bytes 61448 | tf_op jit(solution)/shard_map/ppermute | solution.py:246
  29.3 2.6 %collective-permute-start.4 = (f32[192,128]{1,0:T(8,128)S(1)}, f32[192,128]{1,0:T(8,128)S(1)}, u32[]{:S(2)}, u32[]{:S(2)}) collective-permute-start(f32[192,128]{1,0:T(8,128)S(1)} %get-tuple-element.4), channel_id=1, source_target_pairs={{0,16},{16,0},{32,48},{48,32},{64,80},{80,64},{96,112},{112,96},{1... | collective-permute-start | bytes 294920 | tf_op jit(solution)/shard_map/ppermute | solution.py:237
  32.0 5.7 %collective-permute-start.5 = (f32[192,128]{1,0:T(8,128)S(1)}, f32[192,128]{1,0:T(8,128)S(1)}, u32[]{:S(2)}, u32[]{:S(2)}) collective-permute-start(f32[192,128]{1,0:T(8,128)S(1)} %add.24), channel_id=1, source_target_pairs={{0,32},{16,48},{32,0},{48,16},{64,96},{80,112},{96,64},{112,80},{1... | collective-permute-start | bytes 294920 | tf_op jit(solution)/shard_map/ppermute | solution.py:237
  37.7 9.0 %collective-permute-start.6 = (f32[192,128]{1,0:T(8,128)S(1)}, f32[192,128]{1,0:T(8,128)S(1)}, u32[]{:S(2)}, u32[]{:S(2)}) collective-permute-start(f32[192,128]{1,0:T(8,128)S(1)} %add.25), channel_id=1, source_target_pairs={{0,64},{16,80},{32,96},{48,112},{64,0},{80,16},{96,32},{112,48},{1... | collective-permute-start | bytes 294920 | tf_op jit(solution)/shard_map/ppermute | solution.py:237
  46.7 9.2 %collective-permute-start.7 = (f32[192,128]{1,0:T(8,128)S(1)}, f32[192,128]{1,0:T(8,128)S(1)}, u32[]{:S(2)}, u32[]{:S(2)}) collective-permute-start(f32[192,128]{1,0:T(8,128)S(1)} %add.26), channel_id=1, source_target_pairs={{0,128},{16,144},{32,160},{48,176},{64,192},{80,208},{96,224},{112... | collective-permute-start | bytes 294920 | tf_op jit(solution)/shard_map/ppermute | solution.py:237
  55.9 5.3 %collective-permute-start.8 = (f32[192,128]{1,0:T(8,128)S(1)}, f32[192,128]{1,0:T(8,128)S(1)}, u32[]{:S(2)}, u32[]{:S(2)}) collective-permute-start(f32[192,128]{1,0:T(8,128)S(1)} %add.27), channel_id=1, source_target_pairs={{0,1},{1,0},{2,3},{3,2},{4,5},{5,4},{6,7},{7,6},{8,9},{9,8},{10,11... | collective-permute-start | bytes 294920 | tf_op jit(solution)/shard_map/ppermute | solution.py:237
  61.2 6.2 %collective-permute-start.9 = (f32[192,128]{1,0:T(8,128)S(1)}, f32[192,128]{1,0:T(8,128)S(1)}, u32[]{:S(2)}, u32[]{:S(2)}) collective-permute-start(f32[192,128]{1,0:T(8,128)S(1)} %add.28), channel_id=1, source_target_pairs={{0,2},{1,3},{2,0},{3,1},{4,6},{5,7},{6,4},{7,5},{8,10},{9,11},{10,... | collective-permute-start | bytes 294920 | tf_op jit(solution)/shard_map/ppermute | solution.py:237
  67.5 5.6 %collective-permute-start.10 = (f32[192,128]{1,0:T(8,128)S(1)}, f32[192,128]{1,0:T(8,128)S(1)}, u32[]{:S(2)}, u32[]{:S(2)}) collective-permute-start(f32[192,128]{1,0:T(8,128)S(1)} %add.29), channel_id=1, source_target_pairs={{0,4},{1,5},{2,6},{3,7},{4,0},{5,1},{6,2},{7,3},{8,12},{9,13},{10,... | collective-permute-start | bytes 294920 | tf_op jit(solution)/shard_map/ppermute | solution.py:237
  73.0 6.4 %collective-permute-start.11 = (f32[192,128]{1,0:T(8,128)S(1)}, f32[192,128]{1,0:T(8,128)S(1)}, u32[]{:S(2)}, u32[]{:S(2)}) collective-permute-start(f32[192,128]{1,0:T(8,128)S(1)} %add.30), channel_id=1, source_target_pairs={{0,8},{1,9},{2,10},{3,11},{4,12},{5,13},{6,14},{7,15},{8,0},{9,1},... | collective-permute-start | bytes 294920 | tf_op jit(solution)/shard_map/ppermute | solution.py:237

commit v2 on v1

--- a/solution.py
+++ b/solution.py
@@ -1,3 +1,5 @@
+import math
+
 import jax
 import jax.numpy as jnp
 from jax import lax
@@ -10,6 +12,9 @@
 ITERS = 3
 DEEP = ITERS + 1
 
+BODY = 3 * K // 4
+TAIL = 8
+
 HIGH = lax.Precision.HIGHEST
 F32 = jnp.float32
 
@@ -20,8 +25,8 @@
 
 
 def krylov_kernel(
-    up_ref, here_ref, down_ref, fields_ref, moments_ref,
-    cond, label, couple, weight, nbr, diag, v0, v1, v2, v3,
+    up_ref, here_ref, down_ref, fields_ref, keep_ref, send_ref, unit_ref,
+    cond, label, couple, weight, nbr, diag, v0, v1, v2, v3, gram,
 ):
     rows = here_ref.shape[1]
     lanes = here_ref.shape[2]
@@ -55,7 +60,12 @@
         weight[side] = free * conduct
         nbr[side] = mark
         couple[side] = jnp.where(mark == 0, free * conduct, 0.0)
-    diag[...] = free * total + (1.0 - free)
+    mean = jnp.sum(free * total, keepdims=True) / jnp.maximum(jnp.sum(free, keepdims=True), 1.0)
+    unit, inverse = power_of_two(1.5 * mean)
+    unit_ref[...] = jnp.broadcast_to(unit, unit_ref.shape)
+    diag[...] = free * (total * inverse - 1.0)
+    for side in range(6):
+        couple[side] = couple[side] * inverse
 
     step = 16
     cluster = lax.broadcasted_iota(jnp.int32, (step, lanes), 0)
@@ -100,17 +110,113 @@
             ]
     chunk = 256
     wide = fields_ref.shape[1]
-    for pair in range(ITERS):
-        parts = []
-        for at in range(0, wide, chunk):
-            left = fields_ref[pair * K:(pair + 1) * K, at:at + chunk]
-            right = fields_ref[pair * K:(pair + 2) * K, at:at + chunk]
-            parts.append(lax.dot_general(
-                left, right, (((1,), (1,)), ((), ())), precision=HIGH, preferred_element_type=F32
+    for at in range(0, wide, chunk):
+        part = lax.dot_general(
+            fields_ref[0:ITERS * K, at:at + chunk], fields_ref[:, at:at + chunk],
+            (((1,), (1,)), ((), ())), precision=HIGH, preferred_element_type=F32,
+        )
+        gram[...] = part if at == 0 else gram[...] + part
+    pack(gram, unit, keep_ref, send_ref)
+
+
+def power_of_two(value):
+    unit = jnp.full(value.shape, 2.0 ** -4, F32)
+    inverse = jnp.full(value.shape, 2.0 ** 4, F32)
+    for exponent in range(-4, 9):
+        more = value > 2.0 ** (exponent + 0.5)
+        unit = jnp.where(more, 2.0 ** (exponent + 1), unit)
+        inverse = jnp.where(more, 2.0 ** (-exponent - 1), inverse)
+    return unit, inverse
+
+
+def pair_add(pair, value):
+    high, low = pair
+    total = high + value
+    back = total - high
+    return total, low + ((high - (total - back)) + (value - back))
+
+
+EXPANSION = []
+for k in range(2 * ITERS):
+    first, second = k // 2, k - k // 2
+    terms = {}
+    for a in range(first + 1):
+        for b in range(second + 1):
+            terms[a, b] = math.comb(first, a) * math.comb(second, b)
+    EXPANSION.append(sorted(terms.items(), reverse=True))
+
+
+def pack(gram, unit, keep_ref, send_ref):
+    row = lax.broadcasted_iota(jnp.int32, (K, K), 0)
+    col = lax.broadcasted_iota(jnp.int32, (K, K), 1)
+    blocks = {}
+    lines = {}
+    for k in range(2 * ITERS):
+        for at, _ in EXPANSION[k]:
+            if at not in blocks:
+                a, b = at
+                blocks[at] = gram[a * K:(a + 1) * K, b * K:(b + 1) * K]
+                lines[at] = jnp.sum(jnp.where(row == col, blocks[at], 0.0), axis=0, keepdims=True)
+    scale = jnp.ones_like(unit)
+    moments, highs, lows = [], [], []
+    for k in range(2 * ITERS):
+        moment = jnp.zeros((K, K), F32)
+        pair = (jnp.zeros((1, K), F32), jnp.zeros((1, K), F32))
+        for at, factor in EXPANSION[k]:
+            moment = moment + float(factor) * blocks[at]
+            bit = 1
+            while bit <= factor:
+                if factor & bit:
+                    pair = pair_add(pair, float(bit) * lines[at])
+                bit *= 2
+        moments.append(moment * scale)
+        highs.append(pair[0] * scale)
+        lows.append(pair[1] * scale)
+        scale = scale * unit
+    packs = [
+        jnp.where(row > col, moments[i], jnp.where(row < col, moments[i + 1], 0.0))
+        for i in range(0, 2 * ITERS, 2)
+    ]
+    first = jnp.concatenate(packs[:2], axis=1)
+    second = jnp.concatenate([packs[2][:K // 2], packs[2][K // 2:]], axis=1)
+    gap = jnp.zeros((1, K), F32)
+    rest = jnp.zeros((2, 2 * K), F32)
+
+    def tail(at):
+        return [
+            jnp.concatenate([highs[at], highs[at + 1]], axis=1),
+            jnp.concatenate([highs[at + 2], gap], axis=1),
+            rest,
+            jnp.concatenate([lows[at], lows[at + 1]], axis=1),
+            jnp.concatenate([lows[at + 2], gap], axis=1),
+            rest,
+        ]
+
+    top = jnp.concatenate([first[:BODY]] + tail(0), axis=0)
+    bottom = jnp.concatenate([first[BODY:], second] + tail(3), axis=0)
+    low_core = lax.rem(lax.axis_index("gx"), 2) == 0
+    keep_ref[...] = jnp.where(low_core, top, bottom)
+    send_ref[...] = jnp.where(low_core, bottom, top)
+
+
+def unpack(top, bottom):
+    row = lax.broadcasted_iota(jnp.int32, (K, K), 0)
+    col = lax.broadcasted_iota(jnp.int32, (K, K), 1)
+    first = jnp.concatenate([top[:BODY], bottom[:K - BODY]], axis=0)
+    second = bottom[K - BODY:BODY]
+    packs = [first[:, :K], first[:, K:], jnp.concatenate([second[:, :K], second[:, K:]], axis=0)]
+    moments, pairs = [], []
+    for value in packs:
+        flip = value.T
+        moments.append(jnp.where(row > col, value, flip))
+        moments.append(jnp.where(row < col, value, flip))
+    for half in (top, bottom):
+        for at in ((0, 0), (0, K), (1, 0)):
+            pairs.append(tuple(
+                half[BODY + shift + at[0]:BODY + shift + at[0] + 1, at[1]:at[1] + K]
+                for shift in (0, TAIL // 2)
             ))
-        while len(parts) > 1:
-            parts = [parts[i] + parts[i + 1] for i in range(0, len(parts), 2)]
-        moments_ref[pair * K:(pair + 1) * K, :] = parts[0]
+    return moments, pairs
 
 
 def krylov(up, here, down):
@@ -122,10 +228,12 @@
         krylov_kernel,
         out_shape=(
             jax.ShapeDtypeStruct(((ITERS + 1) * K, rows * own), F32),
-            jax.ShapeDtypeStruct((ITERS * K, 2 * K), F32),
+            jax.ShapeDtypeStruct((BODY + TAIL, 2 * K), F32),
+            jax.ShapeDtypeStruct((BODY + TAIL, 2 * K), F32),
+            jax.ShapeDtypeStruct((8, 2 * K), F32),
         ),
         in_specs=[pl.BlockSpec(memory_space=pltpu.VMEM)] * 3,
-        out_specs=[pl.BlockSpec(memory_space=pltpu.VMEM)] * 2,
+        out_specs=[pl.BlockSpec(memory_space=pltpu.VMEM)] * 4,
         scratch_shapes=[
             pltpu.VMEM((tall, lanes), F32),
             pltpu.VMEM((tall, lanes), F32),
@@ -137,6 +245,7 @@
             pltpu.VMEM((inner - 2, K, lanes), F32),
             pltpu.VMEM((inner - 4, K, lanes), F32),
             pltpu.VMEM((inner - 6, K, lanes), F32),
+            pltpu.VMEM((ITERS * K, (ITERS + 1) * K), F32),
         ],
         compiler_params=pltpu.CompilerParams(vmem_limit_bytes=40 * 1024 * 1024),
     )(up, here, down)
@@ -176,30 +285,61 @@
             work[at:at + panel, t:t + 128] = rows[i]
 
 
-def finish_kernel(moments_ref, fields_ref, solution_ref, residual_ref, work, coeff, mixed):
+def finish_kernel(
+    mine_ref, other_ref, unit_ref, fields_ref, solution_ref, residual_ref, work, coeff, mixed
+):
     rows, cols = solution_ref.shape[:2]
     size = ITERS * K
-
-    def moment(k):
-        pair, half = divmod(k, 2)
-        return moments_ref[pair * K:(pair + 1) * K, half * K:(half + 1) * K]
-
-    moments = []
+    low_core = lax.rem(lax.axis_index("gx"), 2) == 0
+    mine, other = mine_ref[...], other_ref[...]
+    moments, pairs = unpack(
+        jnp.where(low_core, mine, other), jnp.where(low_core, other, mine)
+    )
+    common, inverse = power_of_two(
+        jnp.sum(pairs[1][0], keepdims=True) / jnp.sum(pairs[0][0], keepdims=True)
+    )
+    scale = jnp.ones_like(common)
     for k in range(2 * ITERS):
-        value = moment(k)
-        moments.append(0.5 * (value + value.T))
-    for i in range(ITERS):
-        for j in range(ITERS):
-            work[i * K:(i + 1) * K, j * K:(j + 1) * K] = moments[i + j + 1]
-        work[i * K:(i + 1) * K, size:size + K] = moments[i]
+        moments[k] = moments[k] * scale
+        pairs[k] = (pairs[k][0] * scale, pairs[k][1] * scale)
+        scale = scale * inverse
+    eye = (
+        lax.broadcasted_iota(jnp.int32, (K, K), 0) == lax.broadcasted_iota(jnp.int32, (K, K), 1)
+    )
+
+    def whole(k):
+        return jnp.where(eye, pairs[k][0] + pairs[k][1], moments[k])
+
+    for level in range(2 * ITERS - 1):
+        if level < ITERS:
+            work[level * K:(level + 1) * K, size:size + K] = whole(0)
+        block = whole(1)
+        for i in range(ITERS):
+            j = level - i
+            if 0 <= j < ITERS:
+                work[i * K:(i + 1) * K, j * K:(j + 1) * K] = block
+        for k in range(len(moments) - 1):
+            high, low = pair_add(pairs[k + 1], -pairs[k][0])
+            pairs[k] = (high, low - pairs[k][1])
+            moments[k] = moments[k + 1] - moments[k]
+        moments.pop()
+        pairs.pop()
     gauss_jordan(work, size)
-    answer = work[:, size:size + K]
-    coeff[0:size, 0:K] = answer
-    coeff[size:size + K, 0:K] = jnp.zeros((K, K), F32)
-    coeff[0:K, K:2 * K] = (
-        lax.broadcasted_iota(jnp.int32, (K, K), 0) == lax.broadcasted_iota(jnp.int32, (K, K), 1)
-    ).astype(F32)
-    coeff[K:K + size, K:2 * K] = -answer
+    unit = unit_ref[0:1, 0:1]
+    ratio = unit * inverse
+    shift = ratio - 1.0
+    y0, y1, y2 = (work[i * K:(i + 1) * K, size:size + K] * inverse for i in range(ITERS))
+    y0 = y0 + shift * y1 + (shift * shift) * y2
+    y1 = ratio * y1 + (2.0 * ratio * shift) * y2
+    y2 = (ratio * ratio) * y2
+    coeff[0:K, 0:K] = y0
+    coeff[K:2 * K, 0:K] = y1
+    coeff[2 * K:3 * K, 0:K] = y2
+    coeff[3 * K:4 * K, 0:K] = jnp.zeros((K, K), F32)
+    coeff[0:K, K:2 * K] = eye.astype(F32) - unit * y0
+    coeff[K:2 * K, K:2 * K] = -unit * (y0 + y1)
+    coeff[2 * K:3 * K, K:2 * K] = -unit * (y1 + y2)
+    coeff[3 * K:4 * K, K:2 * K] = -unit * y2
     own = cols * NZ
     low = lax.broadcasted_iota(jnp.int32, (cols, 2 * K), 1) < K
     for row in range(rows):
@@ -214,12 +354,12 @@
             residual_ref[row, :, z * K:(z + 2) * K] = jnp.where(low, pltpu.roll(even, K, 1), odd)
 
 
-def finish(moments, fields, rows, cols):
+def finish(mine, other, unit, fields, rows, cols):
     out = jax.ShapeDtypeStruct((rows, cols, NZ * K), F32)
     return pl.pallas_call(
         finish_kernel,
         out_shape=(out, out),
-        in_specs=[pl.BlockSpec(memory_space=pltpu.VMEM)] * 2,
+        in_specs=[pl.BlockSpec(memory_space=pltpu.VMEM)] * 4,
         out_specs=[pl.BlockSpec(memory_space=pltpu.VMEM)] * 2,
         scratch_shapes=[
             pltpu.VMEM((ITERS * K, (ITERS + 1) * K), F32),
@@ -227,16 +367,43 @@
             pltpu.VMEM((cols * NZ, 2 * K), F32),
         ],
         compiler_params=pltpu.CompilerParams(vmem_limit_bytes=40 * 1024 * 1024),
-    )(moments, fields)
-
-
-def total_over(value, axis):
+    )(mine, other, unit, fields)
+
+
+def add_parts(value, *others):
+    for other in others:
+        total = value + other
+        back = total - value
+        error = (value - (total - back)) + (other - back)
+        half = BODY + TAIL // 2
+        value = jnp.concatenate([total[:half], total[half:] + error[BODY:half]], axis=0)
+    return value
+
+
+def from_ahead(value, axis, distance, stride, ring):
+    def place(i, d):
+        low, high = i % stride, i // (stride * ring)
+        return (high * ring + (i // stride + d) % ring) * stride + low
+
     count = lax.axis_size(axis)
-    stride = 1
-    while stride < count:
-        value = value + lax.ppermute(value, axis, [(i, i ^ stride) for i in range(count)])
-        stride *= 2
-    return value
+    return lax.ppermute(value, axis, [(i, place(i, -distance)) for i in range(count)])
+
+
+def sum_of_four(value, axis, stride):
+    return add_parts(value, *(from_ahead(value, axis, d, stride, 4) for d in (1, -1, 2)))
+
+
+def sum_of_eight(value, axis, stride):
+    ahead, behind = (from_ahead(value, axis, d, stride, 8) for d in (1, -1))
+    two = add_parts(value, ahead)
+    three = add_parts(two, behind)
+    return add_parts(
+        three, from_ahead(three, axis, 3, stride, 8), from_ahead(two, axis, -3, stride, 8)
+    )
+
+
+def swap_cores(value):
+    return lax.ppermute(value, "gx", [(i, i ^ 1) for i in range(lax.axis_size("gx"))])
 
 
 def from_both(first, last, axis):
@@ -254,9 +421,12 @@
     before, after = from_both(cells[:, :, :edge], cells[:, :, -edge:], "gy")
     here = jnp.concatenate([cells, after, before], axis=2)
     up, down = from_both(here[:, :DEEP], here[:, rows - DEEP:], "gx")
-    fields, moments = krylov(up, here, down)
-    moments = total_over(total_over(moments, "gx"), "gy")
-    return finish(moments, fields, rows, cols)
+    fields, keep, send, unit = krylov(up, here, down)
+    mine = add_parts(keep, swap_cores(send))
+    mine = sum_of_eight(mine, "gx", 2)
+    mine = sum_of_four(mine, "gy", 1)
+    mine = sum_of_four(mine, "gy", 4)
+    return finish(mine, swap_cores(mine), unit, fields, rows, cols)
 
 
 def solution(mesh):

time: 92.1 us -> 83.4 us (0.906)
  the two profiles are of different devices: /device:TPU:16 before, /device:TPU:1 now
where the time goes in v2:
time: 83.4 us; the launch traced here: 83.1 us
  starting transfers between devices  40 us (48%)
  Pallas kernels  21 us (25%)
  waiting for transfers between devices  19 us (23%)
  other arithmetic  1.94 us (2%)
    ppermute x10, starting transfers between devices, from_ahead(): lax.ppermute(value, axis, [(i, place(i, -distance)) for i in range(count)])  19.5 us
    ppermute x10, waiting for transfers between devices, from_ahead(): lax.ppermute(value, axis, [(i, place(i, -distance)) for i in range(count)])  15.2 us
    pallas_call x1, Pallas kernels, finish(): pl.pallas_call(finish_kernel, out_shape=(out, out), in_specs=[pl.BlockSpe...  12.4 us
    pallas_call x1, Pallas kernels, krylov(): pl.pallas_call(krylov_kernel, out_shape=(jax.ShapeDtypeStruct(((ITERS + 1...  8.55 us
    ppermute x2, starting transfers between devices, swap_cores(): lax.ppermute(value, 'gx', [(i, i ^ 1) for i in range(lax.axis_size('gx'))])  7.02 us
    ppermute x2, starting transfers between devices, from_both(): lax.ppermute(first, axis, backward)  6.97 us
    ppermute x2, starting transfers between devices, from_both(): lax.ppermute(last, axis, forward)  6.49 us
    ppermute x2, waiting for transfers between devices, swap_cores(): lax.ppermute(value, 'gx', [(i, i ^ 1) for i in range(lax.axis_size('gx'))])  1.89 us
  transfers between devices with their start and end apart: 16, of which 14 were waited for; matrix products, arithmetic and copies ran while one was open for 0% of the time, Pallas kernels for 0%

profile of v2, /device:TPU:1, one launch (start us, length us, event | category | flops | bytes accessed | tf_op | source)
XLA Modules:
  0.0 83.1 jit_solution(13323552853182998228)
XLA Ops:
  0.6 0.8 convert_multiply_fusion
  1.4 0.1 copy.7
  1.5 0.1 stack.9
  1.6 0.8 convert_element_type.7
  2.4 0.1 copy.8
  2.4 0.1 stack.10
  2.6 0.1 fusion.38
  2.6 1.3 %collective-permute-start = (f32[2,4,64]{2,1,0:T(4,128)S(1)}, f32[2,4,64]{2,1,0:T(4,128)S(1)}, u32[]{:S(2)}, u32[]{:S(2)}) collective-permute-start(f32[2,4,64]{2,1,0:T(4,128)S(1)} %get-tuple-element.12), channel_id=1, source_target_pairs={{1,0},{2,1},{3,2},{4,3},{5,4},{6,5},{7,6},{8,7},{9,8},{10,9},{11,1... | collective-permute-start | bytes 6152 | tf_op jit(solution)/shard_map/ppermute | solution.py:413
  3.9 4.6 %collective-permute-start.1 = (f32[2,4,64]{2,1,0:T(4,128)S(1)}, f32[2,4,64]{2,1,0:T(4,128)S(1)}, u32[]{:S(2)}, u32[]{:S(2)}) collective-permute-start(f32[2,4,64]{2,1,0:T(4,128)S(1)} %get-tuple-element.13), channel_id=1, source_target_pairs={{0,1},{1,2},{2,3},{3,4},{4,5},{5,6},{6,7},{7,8},{8,9},{9,10},{10,1... | collective-permute-start | bytes 6152 | tf_op jit(solution)/shard_map/ppermute | solution.py:413
  8.5 0.0 collective-permute-done
  8.5 0.7 collective-permute-done.1
  9.2 0.1 pad_maximum_fusion.11.here_ref
  9.3 5.7 %collective-permute-start.3 = (f32[2,4,640]{2,1,0:T(4,128)S(1)}, f32[2,4,640]{2,1,0:T(4,128)S(1)}, u32[]{:S(2)}, u32[]{:S(2)}) collective-permute-start(f32[2,4,640]{2,1,0:T(4,128)S(1)} %pad_maximum_fusion.11.here_ref), channel_id=1, source_target_pairs={{16,0},{32,16},{48,32},{64,48},{80,64},{96,80},{112,96},{128,112},... | collective-permute-start | bytes 61448 | tf_op jit(solution)/shard_map/ppermute | solution.py:413
  15.0 1.9 %collective-permute-start.2 = (f32[2,4,640]{2,1,0:T(4,128)S(1)}, f32[2,4,640]{2,1,0:T(4,128)S(1)}, u32[]{:S(2)}, u32[]{:S(2)}) collective-permute-start(f32[2,4,640]{2,1,0:T(4,128)S(1)} %pad_maximum_fusion.11.here_ref), channel_id=1, source_target_pairs={{0,16},{16,32},{32,48},{48,64},{64,80},{80,96},{96,112},{112,128},... | collective-permute-start | bytes 61448 | tf_op jit(solution)/shard_map/ppermute | solution.py:413
  16.9 0.0 collective-permute-done.3.down_ref
  17.0 1.1 %collective-permute-done.2.up_ref = f32[2,4,640]{2,1,0:T(4,128)S(1)} collective-permute-done((f32[2,4,640]{2,1,0:T(4,128)S(1)}, f32[2,4,640]{2,1,0:T(4,128)S(1)}, u32[]{:S(2)}, u32[]{:S(2)}) %collective-permute-start.2) | collective-permute-done | bytes 20512 | tf_op jit(solution)/shard_map/ppermute | solution.py:413
  18.1 8.6 %shard_map.50 = (f32[256,2048]{1,0:T(8,128)S(1)}, f32[56,128]{1,0:T(8,128)S(1)}, f32[56,128]{1,0:T(8,128)S(1)}, f32[8,128]{1,0:T(8,128)S(1)}) custom-call(f32[2,4,640]{2,1,0:T(4,128)S(1)} %collective-permute-done.2.up_ref, f32[2,4,640]{2,1,0:T(4,128)S(1)} %pad_maximum_fusion.11.here_ref, f32[2,4,640]{2,1,0:T(4,128)S(1)} %collective-permute-done.3.down_ref), custom_call_target="tpu_custom_call" | custom-call | tf_op jit(solution)/shard_map/pallas_call | solution.py:227
  26.7 0.2 collective-permute-start.4
  26.9 1.0 %collective-permute-done.4 = f32[56,128]{1,0:T(8,128)S(1)} collective-permute-done((f32[56,128]{1,0:T(8,128)S(1)}, f32[56,128]{1,0:T(8,128)S(1)}, u32[]{:S(2)}, u32[]{:S(2)}) %collective-permute-start.4) | collective-permute-done | bytes 28704 | tf_op jit(solution)/shard_map/ppermute | solution.py:406
  28.0 5.6 %collective-permute-start.5 = (f32[56,128]{1,0:T(8,128)S(1)}, f32[56,128]{1,0:T(8,128)S(1)}, u32[]{:S(2)}, u32[]{:S(2)}) collective-permute-start(f32[56,128]{1,0:T(8,128)S(1)} %pad_maximum_fusion), channel_id=1, source_target_pairs={{0,224},{16,240},{32,0},{48,16},{64,32},{80,48},{96,64},{112,80},{... | collective-permute-start | bytes 86024 | tf_op jit(solution)/shard_map/ppermute | solution.py:389
  33.6 0.0 collective-permute-start.6
  33.6 1.0 %collective-permute-done.5 = f32[56,128]{1,0:T(8,128)S(1)} collective-permute-done((f32[56,128]{1,0:T(8,128)S(1)}, f32[56,128]{1,0:T(8,128)S(1)}, u32[]{:S(2)}, u32[]{:S(2)}) %collective-permute-start.5) | collective-permute-done | bytes 28704 | tf_op jit(solution)/shard_map/ppermute | solution.py:389
  34.6 2.9 %collective-permute-done.6 = f32[56,128]{1,0:T(8,128)S(1)} collective-permute-done((f32[56,128]{1,0:T(8,128)S(1)}, f32[56,128]{1,0:T(8,128)S(1)}, u32[]{:S(2)}, u32[]{:S(2)}) %collective-permute-start.6) | collective-permute-done | bytes 28704 | tf_op jit(solution)/shard_map/ppermute | solution.py:389
  37.5 1.7 %collective-permute-start.7 = (f32[56,128]{1,0:T(8,128)S(1)}, f32[56,128]{1,0:T(8,128)S(1)}, u32[]{:S(2)}, u32[]{:S(2)}) collective-permute-start(f32[56,128]{1,0:T(8,128)S(1)} %pad_maximum_fusion.2), channel_id=1, source_target_pairs={{0,160},{16,176},{32,192},{48,208},{64,224},{80,240},{96,0},{112,1... | collective-permute-start | bytes 86024 | tf_op jit(solution)/shard_map/ppermute | solution.py:389
  39.2 1.6 %collective-permute-start.8 = (f32[56,128]{1,0:T(8,128)S(1)}, f32[56,128]{1,0:T(8,128)S(1)}, u32[]{:S(2)}, u32[]{:S(2)}) collective-permute-start(f32[56,128]{1,0:T(8,128)S(1)} %get-tuple-element.11), channel_id=1, source_target_pairs={{0,96},{16,112},{32,128},{48,144},{64,160},{80,176},{96,192},{112,... | collective-permute-start | bytes 86024 | tf_op jit(solution)/shard_map/ppermute | solution.py:389
  40.9 1.3 %collective-permute-done.7 = f32[56,128]{1,0:T(8,128)S(1)} collective-permute-done((f32[56,128]{1,0:T(8,128)S(1)}, f32[56,128]{1,0:T(8,128)S(1)}, u32[]{:S(2)}, u32[]{:S(2)}) %collective-permute-start.7) | collective-permute-done | bytes 28704 | tf_op jit(solution)/shard_map/ppermute | solution.py:389
  42.2 3.1 %collective-permute-done.8 = f32[56,128]{1,0:T(8,128)S(1)} collective-permute-done((f32[56,128]{1,0:T(8,128)S(1)}, f32[56,128]{1,0:T(8,128)S(1)}, u32[]{:S(2)}, u32[]{:S(2)}) %collective-permute-start.8) | collective-permute-done | bytes 28704 | tf_op jit(solution)/shard_map/ppermute | solution.py:389
  45.3 4.7 %collective-permute-start.9 = (f32[56,128]{1,0:T(8,128)S(1)}, f32[56,128]{1,0:T(8,128)S(1)}, u32[]{:S(2)}, u32[]{:S(2)}) collective-permute-start(f32[56,128]{1,0:T(8,128)S(1)} %pad_maximum_fusion.4), channel_id=1, source_target_pairs={{0,3},{1,0},{2,1},{3,2},{4,7},{5,4},{6,5},{7,6},{8,11},{9,8},{10,9... | collective-permute-start | bytes 86024 | tf_op jit(solution)/shard_map/ppermute | solution.py:389
  50.0 0.0 collective-permute-start.11
  50.0 0.7 collective-permute-start.10
  50.6 0.3 collective-permute-done.9
  51.0 2.9 %collective-permute-done.10 = f32[56,128]{1,0:T(8,128)S(1)} collective-permute-done((f32[56,128]{1,0:T(8,128)S(1)}, f32[56,128]{1,0:T(8,128)S(1)}, u32[]{:S(2)}, u32[]{:S(2)}) %collective-permute-start.10) | collective-permute-done | bytes 28704 | tf_op jit(solution)/shard_map/ppermute | solution.py:389
  53.9 0.3 collective-permute-done.11
  54.3 4.4 %collective-permute-start.12 = (f32[56,128]{1,0:T(8,128)S(1)}, f32[56,128]{1,0:T(8,128)S(1)}, u32[]{:S(2)}, u32[]{:S(2)}) collective-permute-start(f32[56,128]{1,0:T(8,128)S(1)} %pad_maximum_fusion.7), channel_id=1, source_target_pairs={{0,12},{1,13},{2,14},{3,15},{4,0},{5,1},{6,2},{7,3},{8,4},{9,5},{1... | collective-permute-start | bytes 86024 | tf_op jit(solution)/shard_map/ppermute | solution.py:389
  58.7 0.1 collective-permute-start.14
  58.8 0.7 collective-permute-start.13
  59.5 0.2 collective-permute-done.12
  59.7 3.0 %collective-permute-done.13 = f32[56,128]{1,0:T(8,128)S(1)} collective-permute-done((f32[56,128]{1,0:T(8,128)S(1)}, f32[56,128]{1,0:T(8,128)S(1)}, u32[]{:S(2)}, u32[]{:S(2)}) %collective-permute-start.13) | collective-permute-done | bytes 28704 | tf_op jit(solution)/shard_map/ppermute | solution.py:389
  62.7 0.3 collective-permute-done.14
  63.0 6.8 %collective-permute-start.15 = (f32[56,128]{1,0:T(8,128)S(1)}, f32[56,128]{1,0:T(8,128)S(1)}, u32[]{:S(2)}, u32[]{:S(2)}) collective-permute-start(f32[56,128]{1,0:T(8,128)S(1)} %pad_maximum_fusion.10.mine_ref), channel_id=1, source_target_pairs={{0,16},{16,0},{32,48},{48,32},{64,80},{80,64},{96,112},{112,96},{1... | collective-permute-start | bytes 86024 | tf_op jit(solution)/shard_map/ppermute | solution.py:406
  69.8 0.9 %collective-permute-done.15.other_ref = f32[56,128]{1,0:T(8,128)S(1)} collective-permute-done((f32[56,128]{1,0:T(8,128)S(1)}, f32[56,128]{1,0:T(8,128)S(1)}, u32[]{:S(2)}, u32[]{:S(2)}) %collective-permute-start.15) | collective-permute-done | bytes 28704 | tf_op jit(solution)/shard_map/ppermute | solution.py:406
  70.7 12.4 %shard_map.51 = (f32[4,32,1024]{2,1,0:T(8,128)}, f32[4,32,1024]{2,1,0:T(8,128)}) custom-call(f32[56,128]{1,0:T(8,128)S(1)} %pad_maximum_fusion.10.mine_ref, f32[56,128]{1,0:T(8,128)S(1)} %collective-permute-done.15.other_ref, f32[8,128]{1,0:T(8,128)S(1)} %get-tuple-element.8.unit_ref, f32[256,2048]{1,0:T(8,128)S(1)} %get-tuple-element.9.fields_ref), custom_call_target="tpu_custom_call" | custom-call | tf_op jit(solution)/shard_map/pallas_call | solution.py:359
  (29 shorter events, 0.3 us)
Async XLA Ops:
  2.6 5.9 %collective-permute-start = (f32[2,4,64]{2,1,0:T(4,128)S(1)}, f32[2,4,64]{2,1,0:T(4,128)S(1)}, u32[]{:S(2)}, u32[]{:S(2)}) collective-permute-start(f32[2,4,64]{2,1,0:T(4,128)S(1)} %get-tuple-element.12), channel_id=1, source_target_pairs={{1,0},{2,1},{3,2},{4,3},{5,4},{6,5},{7,6},{8,7},{9,8},{10,9},{11,1... | collective-permute-start | bytes 6152 | tf_op jit(solution)/shard_map/ppermute | solution.py:413
  3.9 5.3 %collective-permute-start.1 = (f32[2,4,64]{2,1,0:T(4,128)S(1)}, f32[2,4,64]{2,1,0:T(4,128)S(1)}, u32[]{:S(2)}, u32[]{:S(2)}) collective-permute-start(f32[2,4,64]{2,1,0:T(4,128)S(1)} %get-tuple-element.13), channel_id=1, source_target_pairs={{0,1},{1,2},{2,3},{3,4},{4,5},{5,6},{6,7},{7,8},{8,9},{9,10},{10,1... | collective-permute-start | bytes 6152 | tf_op jit(solution)/shard_map/ppermute | solution.py:413
  9.3 7.6 %collective-permute-start.3 = (f32[2,4,640]{2,1,0:T(4,128)S(1)}, f32[2,4,640]{2,1,0:T(4,128)S(1)}, u32[]{:S(2)}, u32[]{:S(2)}) collective-permute-start(f32[2,4,640]{2,1,0:T(4,128)S(1)} %pad_maximum_fusion.11.here_ref), channel_id=1, source_target_pairs={{16,0},{32,16},{48,32},{64,48},{80,64},{96,80},{112,96},{128,112},... | collective-permute-start | bytes 61448 | tf_op jit(solution)/shard_map/ppermute | solution.py:413
  15.0 3.1 %collective-permute-start.2 = (f32[2,4,640]{2,1,0:T(4,128)S(1)}, f32[2,4,640]{2,1,0:T(4,128)S(1)}, u32[]{:S(2)}, u32[]{:S(2)}) collective-permute-start(f32[2,4,640]{2,1,0:T(4,128)S(1)} %pad_maximum_fusion.11.here_ref), channel_id=1, source_target_pairs={{0,16},{16,32},{32,48},{48,64},{64,80},{80,96},{96,112},{112,128},... | collective-permute-start | bytes 61448 | tf_op jit(solution)/shard_map/ppermute | solution.py:413
  26.7 1.3 %collective-permute-start.4 = (f32[56,128]{1,0:T(8,128)S(1)}, f32[56,128]{1,0:T(8,128)S(1)}, u32[]{:S(2)}, u32[]{:S(2)}) collective-permute-start(f32[56,128]{1,0:T(8,128)S(1)} %get-tuple-element.7), channel_id=1, source_target_pairs={{0,16},{16,0},{32,48},{48,32},{64,80},{80,64},{96,112},{112,96},{1... | collective-permute-start | bytes 86024 | tf_op jit(solution)/shard_map/ppermute | solution.py:406
  28.0 6.6 %collective-permute-start.5 = (f32[56,128]{1,0:T(8,128)S(1)}, f32[56,128]{1,0:T(8,128)S(1)}, u32[]{:S(2)}, u32[]{:S(2)}) collective-permute-start(f32[56,128]{1,0:T(8,128)S(1)} %pad_maximum_fusion), channel_id=1, source_target_pairs={{0,224},{16,240},{32,0},{48,16},{64,32},{80,48},{96,64},{112,80},{... | collective-permute-start | bytes 86024 | tf_op jit(solution)/shard_map/ppermute | solution.py:389
  33.6 3.9 %collective-permute-start.6 = (f32[56,128]{1,0:T(8,128)S(1)}, f32[56,128]{1,0:T(8,128)S(1)}, u32[]{:S(2)}, u32[]{:S(2)}) collective-permute-start(f32[56,128]{1,0:T(8,128)S(1)} %pad_maximum_fusion), channel_id=1, source_target_pairs={{0,32},{16,48},{32,64},{48,80},{64,96},{80,112},{96,128},{112,144}... | collective-permute-start | bytes 86024 | tf_op jit(solution)/shard_map/ppermute | solution.py:389
  37.5 4.6 %collective-permute-start.7 = (f32[56,128]{1,0:T(8,128)S(1)}, f32[56,128]{1,0:T(8,128)S(1)}, u32[]{:S(2)}, u32[]{:S(2)}) collective-permute-start(f32[56,128]{1,0:T(8,128)S(1)} %pad_maximum_fusion.2), channel_id=1, source_target_pairs={{0,160},{16,176},{32,192},{48,208},{64,224},{80,240},{96,0},{112,1... | collective-permute-start | bytes 86024 | tf_op jit(solution)/shard_map/ppermute | solution.py:389
  39.2 6.0 %collective-permute-start.8 = (f32[56,128]{1,0:T(8,128)S(1)}, f32[56,128]{1,0:T(8,128)S(1)}, u32[]{:S(2)}, u32[]{:S(2)}) collective-permute-start(f32[56,128]{1,0:T(8,128)S(1)} %get-tuple-element.11), channel_id=1, source_target_pairs={{0,96},{16,112},{32,128},{48,144},{64,160},{80,176},{96,192},{112,... | collective-permute-start | bytes 86024 | tf_op jit(solution)/shard_map/ppermute | solution.py:389
  45.3 5.7 %collective-permute-start.9 = (f32[56,128]{1,0:T(8,128)S(1)}, f32[56,128]{1,0:T(8,128)S(1)}, u32[]{:S(2)}, u32[]{:S(2)}) collective-permute-start(f32[56,128]{1,0:T(8,128)S(1)} %pad_maximum_fusion.4), channel_id=1, source_target_pairs={{0,3},{1,0},{2,1},{3,2},{4,7},{5,4},{6,5},{7,6},{8,11},{9,8},{10,9... | collective-permute-start | bytes 86024 | tf_op jit(solution)/shard_map/ppermute | solution.py:389
  50.0 4.2 %collective-permute-start.11 = (f32[56,128]{1,0:T(8,128)S(1)}, f32[56,128]{1,0:T(8,128)S(1)}, u32[]{:S(2)}, u32[]{:S(2)}) collective-permute-start(f32[56,128]{1,0:T(8,128)S(1)} %pad_maximum_fusion.4), channel_id=1, source_target_pairs={{0,2},{1,3},{2,0},{3,1},{4,6},{5,7},{6,4},{7,5},{8,10},{9,11},{10,... | collective-permute-start | bytes 86024 | tf_op jit(solution)/shard_map/ppermute | solution.py:389
  50.0 3.9 %collective-permute-start.10 = (f32[56,128]{1,0:T(8,128)S(1)}, f32[56,128]{1,0:T(8,128)S(1)}, u32[]{:S(2)}, u32[]{:S(2)}) collective-permute-start(f32[56,128]{1,0:T(8,128)S(1)} %pad_maximum_fusion.4), channel_id=1, source_target_pairs={{0,1},{1,2},{2,3},{3,0},{4,5},{5,6},{6,7},{7,4},{8,9},{9,10},{10,1... | collective-permute-start | bytes 86024 | tf_op jit(solution)/shard_map/ppermute | solution.py:389
  54.3 5.4 %collective-permute-start.12 = (f32[56,128]{1,0:T(8,128)S(1)}, f32[56,128]{1,0:T(8,128)S(1)}, u32[]{:S(2)}, u32[]{:S(2)}) collective-permute-start(f32[56,128]{1,0:T(8,128)S(1)} %pad_maximum_fusion.7), channel_id=1, source_target_pairs={{0,12},{1,13},{2,14},{3,15},{4,0},{5,1},{6,2},{7,3},{8,4},{9,5},{1... | collective-permute-start | bytes 86024 | tf_op jit(solution)/shard_map/ppermute | solution.py:389
  58.7 4.3 %collective-permute-start.14 = (f32[56,128]{1,0:T(8,128)S(1)}, f32[56,128]{1,0:T(8,128)S(1)}, u32[]{:S(2)}, u32[]{:S(2)}) collective-permute-start(f32[56,128]{1,0:T(8,128)S(1)} %pad_maximum_fusion.7), channel_id=1, source_target_pairs={{0,8},{1,9},{2,10},{3,11},{4,12},{5,13},{6,14},{7,15},{8,0},{9,1},... | collective-permute-start | bytes 86024 | tf_op jit(solution)/shard_map/ppermute | solution.py:389
  58.8 3.9 %collective-permute-start.13 = (f32[56,128]{1,0:T(8,128)S(1)}, f32[56,128]{1,0:T(8,128)S(1)}, u32[]{:S(2)}, u32[]{:S(2)}) collective-permute-start(f32[56,128]{1,0:T(8,128)S(1)} %pad_maximum_fusion.7), channel_id=1, source_target_pairs={{0,4},{1,5},{2,6},{3,7},{4,8},{5,9},{6,10},{7,11},{8,12},{9,13},{1... | collective-permute-start | bytes 86024 | tf_op jit(solution)/shard_map/ppermute | solution.py:389
  63.0 7.6 %collective-permute-start.15 = (f32[56,128]{1,0:T(8,128)S(1)}, f32[56,128]{1,0:T(8,128)S(1)}, u32[]{:S(2)}, u32[]{:S(2)}) collective-permute-start(f32[56,128]{1,0:T(8,128)S(1)} %pad_maximum_fusion.10.mine_ref), channel_id=1, source_target_pairs={{0,16},{16,0},{32,48},{48,32},{64,80},{80,64},{96,112},{112,96},{1... | collective-permute-start | bytes 86024 | tf_op jit(solution)/shard_map/ppermute | solution.py:406

commit v3 on v2

--- a/solution.py
+++ b/solution.py
@@ -14,6 +14,7 @@
 
 BODY = 3 * K // 4
 TAIL = 8
+PANEL = 8
 
 HIGH = lax.Precision.HIGHEST
 F32 = jnp.float32
@@ -80,7 +81,7 @@
             v0[row, part:part + step, :] = acc
         return carry
 
-    lax.fori_loop(0, inner, fill, 0)
+    lax.fori_loop(0, inner, fill, 0, unroll=True)
 
     def power(source, target, offset, count):
         def body(row, carry):
@@ -98,7 +99,7 @@
                 target[row, cut, :] = acc
             return carry
 
-        lax.fori_loop(0, count, body, 0)
+        lax.fori_loop(0, count, body, 0, unroll=True)
 
     power(v0, v1, 0, inner - 2)
     power(v1, v2, 1, inner - 4)
@@ -251,38 +252,76 @@
     )(up, here, down)
 
 
-def gauss_jordan(work, size, panel=8):
+def splat(value, j):
+    return jnp.broadcast_to(value[:, j:j + 1], (value.shape[0], 128))
+
+
+def line(value, j):
+    return jnp.broadcast_to(value[j:j + 1], (PANEL, 128))
+
+
+def gauss_jordan(work, start, stop):
     total = work.shape[1]
-    sub = lax.broadcasted_iota(jnp.int32, (panel, 128), 0)
-    for at in range(0, size, panel):
-        tiles = [t for t in range(0, total, 128) if t + 128 > at + panel]
+    sub = lax.broadcasted_iota(jnp.int32, (PANEL, 128), 0)
+    small = None
+    for at in range(start, stop, PANEL):
         base = at // 128 * 128
-        column = work[:, base:base + 128]
-        spread = [
-            jnp.broadcast_to(column[:, at - base + j:at - base + j + 1], (size, 128))
-            for j in range(panel)
-        ]
-        small = [s[at:at + panel] for s in spread]
-        rows = [work[at:at + panel, t:t + 128] for t in tiles]
-        for j in range(panel):
-            inverse = 1.0 / jnp.broadcast_to(small[j][j:j + 1], (panel, 128))
-            mine = sub == j
-            factor = small[j]
-            for m in range(j + 1, panel):
-                scaled = jnp.broadcast_to(small[m][j:j + 1], (panel, 128)) * inverse
-                small[m] = jnp.where(mine, scaled, small[m] - factor * scaled)
-            for i, value in enumerate(rows):
-                scaled = jnp.broadcast_to(value[j:j + 1], (panel, 128)) * inverse
-                rows[i] = jnp.where(mine, scaled, value - factor * scaled)
-        for i, t in enumerate(tiles):
-            for first, last in ((0, at), (at + panel, size)):
-                if first == last:
+        column = work[start:stop, base:base + 128]
+        spread = [splat(column, at - base + j) for j in range(PANEL)]
+        if small is None:
+            small = [value[at - start:at - start + PANEL] for value in spread]
+        after = at + PANEL
+        ahead, below = [], []
+        if after < stop:
+            base = after // 128 * 128
+            strip = work[at:after, base:base + 128]
+            ahead = [splat(strip, after - base + j) for j in range(PANEL)]
+            strip = work[after:after + PANEL, base:base + 128]
+            below = [splat(strip, after - base + j) for j in range(PANEL)]
+        tiles = [t for t in range(0, total, 128) if t + 128 > after]
+        values = small + ahead + [work[at:after, t:t + 128] for t in tiles]
+        for j in range(PANEL):
+            factor = values[j]
+            inverse = 1.0 / line(factor, j)
+            for i in range(j + 1, len(values)):
+                scaled = line(values[i], j) * inverse
+                values[i] = jnp.where(sub == j, scaled, values[i] - factor * scaled)
+        ahead = values[PANEL:PANEL + len(ahead)]
+        rows = values[PANEL + len(ahead):]
+        if after < stop:
+            small = []
+            for value, column in zip(below, ahead):
+                for j in range(PANEL):
+                    value = value - spread[j][after - start:after - start + PANEL] * line(column, j)
+                small.append(value)
+        for row, t in zip(rows, tiles):
+            for first, last in ((after, min(after + PANEL, stop)), (after + PANEL, stop), (start, at)):
+                if first >= last:
                     continue
                 acc = work[first:last, t:t + 128]
-                for j in range(panel):
-                    acc = acc - spread[j][first:last] * rows[i][j:j + 1]
+                for j in range(PANEL):
+                    acc = acc - spread[j][first - start:last - start] * row[j:j + 1]
                 work[first:last, t:t + 128] = acc
-            work[at:at + panel, t:t + 128] = rows[i]
+            work[at:after, t:t + 128] = row
+
+
+def solve(work, size):
+    total = work.shape[1]
+    for start in range(0, size, K):
+        stop = start + K
+        gauss_jordan(work, start, stop)
+        if stop < size:
+            base = stop // 128 * 128
+            work[stop:size, base:total] = work[stop:size, base:total] - jnp.dot(
+                work[stop:size, start:stop], work[start:stop, base:total],
+                precision=HIGH, preferred_element_type=F32,
+            )
+    for start in range(size - 2 * K, -1, -K):
+        stop = start + K
+        work[start:stop, size:total] = work[start:stop, size:total] - jnp.dot(
+            work[start:stop, stop:size], work[stop:size, size:total],
+            precision=HIGH, preferred_element_type=F32,
+        )
 
 
 def finish_kernel(
@@ -324,7 +363,7 @@
             moments[k] = moments[k + 1] - moments[k]
         moments.pop()
         pairs.pop()
-    gauss_jordan(work, size)
+    solve(work, size)
     unit = unit_ref[0:1, 0:1]
     ratio = unit * inverse
     shift = ratio - 1.0
@@ -344,9 +383,9 @@
     low = lax.broadcasted_iota(jnp.int32, (cols, 2 * K), 1) < K
     for row in range(rows):
         mixed[...] = lax.dot_general(
-            fields_ref[:, row * own:(row + 1) * own], coeff[...], (((0,), (0,)), ((), ())),
+            coeff[...], fields_ref[:, row * own:(row + 1) * own], (((0,), (0,)), ((), ())),
             precision=HIGH, preferred_element_type=F32,
-        )
+        ).T
         for z in range(0, NZ, 2):
             even = mixed[pl.ds(z, cols, stride=NZ), :]
             odd = mixed[pl.ds(z + 1, cols, stride=NZ), :]
@@ -371,39 +410,26 @@
 
 
 def add_parts(value, *others):
+    half = BODY + TAIL // 2
+    lost = jnp.zeros_like(value[BODY:half])
     for other in others:
         total = value + other
-        back = total - value
-        error = (value - (total - back)) + (other - back)
-        half = BODY + TAIL // 2
-        value = jnp.concatenate([total[:half], total[half:] + error[BODY:half]], axis=0)
-    return value
-
-
-def from_ahead(value, axis, distance, stride, ring):
-    def place(i, d):
-        low, high = i % stride, i // (stride * ring)
-        return (high * ring + (i // stride + d) % ring) * stride + low
-
+        old, new, add = value[BODY:half], total[BODY:half], other[BODY:half]
+        back = new - old
+        lost = lost + ((old - (new - back)) + (add - back))
+        value = total
+    return jnp.concatenate([value[:half], value[half:] + lost], axis=0)
+
+
+def flipped(value, axis, *masks):
     count = lax.axis_size(axis)
-    return lax.ppermute(value, axis, [(i, place(i, -distance)) for i in range(count)])
-
-
-def sum_of_four(value, axis, stride):
-    return add_parts(value, *(from_ahead(value, axis, d, stride, 4) for d in (1, -1, 2)))
-
-
-def sum_of_eight(value, axis, stride):
-    ahead, behind = (from_ahead(value, axis, d, stride, 8) for d in (1, -1))
-    two = add_parts(value, ahead)
-    three = add_parts(two, behind)
-    return add_parts(
-        three, from_ahead(three, axis, 3, stride, 8), from_ahead(two, axis, -3, stride, 8)
-    )
-
-
-def swap_cores(value):
-    return lax.ppermute(value, "gx", [(i, i ^ 1) for i in range(lax.axis_size("gx"))])
+    return [lax.ppermute(value, axis, [(i, i ^ mask) for i in range(count)]) for mask in masks]
+
+
+def sum_of_all(value, axis):
+    count = lax.axis_size(axis)
+    parts = lax.all_to_all(jnp.broadcast_to(value[None], (count,) + value.shape), axis, 0, 0)
+    return add_parts(*(parts[i] for i in range(count)))
 
 
 def from_both(first, last, axis):
@@ -416,17 +442,19 @@
 def shards(diffusivity, labels, obstacles):
     rows, cols = diffusivity.shape[:2]
     conductive = diffusivity * (1 - obstacles).astype(F32)
-    cells = jnp.stack([conductive, labels.astype(F32)]).reshape(2, rows, cols * NZ)
+    plane = lax.broadcasted_iota(jnp.int32, (2,) + conductive.shape, 0)
+    cells = jnp.where(plane == 0, conductive[None], labels.astype(F32)[None])
+    cells = cells.reshape(2, rows, cols * NZ)
     edge = DEEP * NZ
     before, after = from_both(cells[:, :, :edge], cells[:, :, -edge:], "gy")
     here = jnp.concatenate([cells, after, before], axis=2)
     up, down = from_both(here[:, :DEEP], here[:, rows - DEEP:], "gx")
     fields, keep, send, unit = krylov(up, here, down)
-    mine = add_parts(keep, swap_cores(send))
-    mine = sum_of_eight(mine, "gx", 2)
-    mine = sum_of_four(mine, "gy", 1)
-    mine = sum_of_four(mine, "gy", 4)
-    return finish(mine, swap_cores(mine), unit, fields, rows, cols)
+    mine = add_parts(keep, *flipped(send, "gx", 1))
+    mine = add_parts(mine, *flipped(mine, "gx", 2, 4, 6))
+    mine = add_parts(mine, *flipped(mine, "gx", 8))
+    mine = sum_of_all(mine, "gy")
+    return finish(mine, *flipped(mine, "gx", 1), unit, fields, rows, cols)
 
 
 def solution(mesh):

time: 83.4 us -> 73.3 us (0.88)
  blocking collectives: 0 us -> 17.8 us
  starting transfers between devices: 40 us -> 28.6 us
  waiting for transfers between devices: 19 us -> 8.1 us
  Pallas kernels: 21 us -> 15.4 us
    all_to_all x0 -> x1, blocking collectives: none -> 17.8 us  [sum_of_all(): lax.all_to_all(jnp.broadcast_to(value[None], (count,) + value.shape), axi...]
    ppermute x12 -> x6, starting transfers between devices: 26.5 us -> 15.1 us  [flipped(): lax.ppermute(value, axis, [(i, i ^ mask) for i in range(count)])]
    ppermute x12 -> x6, waiting for transfers between devices: 17.1 us -> 6.22 us  [flipped(): lax.ppermute(value, axis, [(i, i ^ mask) for i in range(count)])]
    pallas_call x1, Pallas kernels: 12.4 us -> 9.24 us  [finish(): pl.pallas_call(finish_kernel, out_shape=(out, out), in_specs=[pl.BlockSpe...]
    pallas_call x1, Pallas kernels: 8.55 us -> 6.14 us  [krylov(): pl.pallas_call(krylov_kernel, out_shape=(jax.ShapeDtypeStruct(((ITERS + 1...]
  transfers between devices with their start and end apart: 16 -> 10, of which waited for: 14 -> 7; matrix products, arithmetic and copies ran while one was open for 0% -> 0% of each run, Pallas kernels for 0% -> 0%
where the time goes in v3:
time: 73.3 us; the launch traced here: 73 us
  starting transfers between devices  28.6 us (39%)
  blocking collectives  17.8 us (24%)
  Pallas kernels  15.4 us (21%)
  waiting for transfers between devices  8.1 us (11%)
  other arithmetic  1.87 us (3%)
  between operations  0.76 us (1%)
    all_to_all x1, blocking collectives, sum_of_all(): lax.all_to_all(jnp.broadcast_to(value[None], (count,) + value.shape), axi...  17.8 us
    ppermute x6, starting transfers between devices, flipped(): lax.ppermute(value, axis, [(i, i ^ mask) for i in range(count)])  15.1 us
    pallas_call x1, Pallas kernels, finish(): pl.pallas_call(finish_kernel, out_shape=(out, out), in_specs=[pl.BlockSpe...  9.24 us
    ppermute x2, starting transfers between devices, from_both(): lax.ppermute(first, axis, backward)  6.97 us
    ppermute x2, starting transfers between devices, from_both(): lax.ppermute(last, axis, forward)  6.49 us
    ppermute x6, waiting for transfers between devices, flipped(): lax.ppermute(value, axis, [(i, i ^ mask) for i in range(count)])  6.22 us
    pallas_call x1, Pallas kernels, krylov(): pl.pallas_call(krylov_kernel, out_shape=(jax.ShapeDtypeStruct(((ITERS + 1...  6.14 us
    ppermute x2, waiting for transfers between devices, from_both(): lax.ppermute(last, axis, forward)  1.87 us
  transfers between devices with their start and end apart: 10, of which 7 were waited for; matrix products, arithmetic and copies ran while one was open for 0% of the time, Pallas kernels for 0%

profile of v3, /device:TPU:1, one launch (start us, length us, event | category | flops | bytes accessed | tf_op | source)
XLA Modules:
  0.0 73.0 jit_solution(16570768780632602310)
XLA Ops:
  0.6 0.8 %convert_multiply_fusion = f32[4,32,16]{1,2,0:T(8,128)S(1)} fusion(f32[4,32,16]{1,2,0:T(8,128)} %param.3, s32[4,32,16]{1,2,0:T(8,128)} %param.5), kind=kLoop, calls=%fused_computation | loop fusion | flops 6144 | bytes 24576 | tf_op jit(solution)/shard_map/mul | solution.py:444
  1.4 0.1 copy.5
  1.5 0.1 broadcast_in_dim.28
  1.6 0.8 %convert_element_type.7 = f32[4,32,16]{1,2,0:T(8,128)S(1)} convert(s32[4,32,16]{1,2,0:T(8,128)} %param.4) | non-fusion elementwise | flops 2048 | bytes 16384 | tf_op jit(solution)/shard_map/convert_element_type | solution.py:446
  2.4 0.1 copy.6
  2.4 0.1 broadcast_in_dim.30
  2.5 0.1 broadcast_select_fusion
  2.6 0.1 fusion.56
  2.7 1.3 %collective-permute-start = (f32[2,4,64]{2,1,0:T(4,128)S(1)}, f32[2,4,64]{2,1,0:T(4,128)S(1)}, u32[]{:S(2)}, u32[]{:S(2)}) collective-permute-start(f32[2,4,64]{2,1,0:T(4,128)S(1)} %get-tuple-element.28), channel_id=1, source_target_pairs={{1,0},{2,1},{3,2},{4,3},{5,4},{6,5},{7,6},{8,7},{9,8},{10,9},{11,1... | collective-permute-start | bytes 6152 | tf_op jit(solution)/shard_map/ppermute | solution.py:439
  4.0 4.6 %collective-permute-start.1 = (f32[2,4,64]{2,1,0:T(4,128)S(1)}, f32[2,4,64]{2,1,0:T(4,128)S(1)}, u32[]{:S(2)}, u32[]{:S(2)}) collective-permute-start(f32[2,4,64]{2,1,0:T(4,128)S(1)} %get-tuple-element.29), channel_id=1, source_target_pairs={{0,1},{1,2},{2,3},{3,4},{4,5},{5,6},{6,7},{7,8},{8,9},{9,10},{10,1... | collective-permute-start | bytes 6152 | tf_op jit(solution)/shard_map/ppermute | solution.py:439
  8.6 0.0 collective-permute-done
  8.6 0.7 collective-permute-done.1
  9.3 0.1 pad_maximum_fusion.4.here_ref
  9.4 5.7 %collective-permute-start.3 = (f32[2,4,640]{2,1,0:T(4,128)S(1)}, f32[2,4,640]{2,1,0:T(4,128)S(1)}, u32[]{:S(2)}, u32[]{:S(2)}) collective-permute-start(f32[2,4,640]{2,1,0:T(4,128)S(1)} %pad_maximum_fusion.4.here_ref), channel_id=1, source_target_pairs={{16,0},{32,16},{48,32},{64,48},{80,64},{96,80},{112,96},{128,112},... | collective-permute-start | bytes 61448 | tf_op jit(solution)/shard_map/ppermute | solution.py:439
  15.1 1.9 %collective-permute-start.2 = (f32[2,4,640]{2,1,0:T(4,128)S(1)}, f32[2,4,640]{2,1,0:T(4,128)S(1)}, u32[]{:S(2)}, u32[]{:S(2)}) collective-permute-start(f32[2,4,640]{2,1,0:T(4,128)S(1)} %pad_maximum_fusion.4.here_ref), channel_id=1, source_target_pairs={{0,16},{16,32},{32,48},{48,64},{64,80},{80,96},{96,112},{112,128},... | collective-permute-start | bytes 61448 | tf_op jit(solution)/shard_map/ppermute | solution.py:439
  17.0 0.0 collective-permute-done.3.down_ref
  17.0 1.1 %collective-permute-done.2.up_ref = f32[2,4,640]{2,1,0:T(4,128)S(1)} collective-permute-done((f32[2,4,640]{2,1,0:T(4,128)S(1)}, f32[2,4,640]{2,1,0:T(4,128)S(1)}, u32[]{:S(2)}, u32[]{:S(2)}) %collective-permute-start.2) | collective-permute-done | bytes 20512 | tf_op jit(solution)/shard_map/ppermute | solution.py:439
  18.2 6.1 %shard_map.50 = (f32[256,2048]{1,0:T(8,128)S(1)}, f32[56,128]{1,0:T(8,128)S(1)}, f32[56,128]{1,0:T(8,128)S(1)}, f32[8,128]{1,0:T(8,128)S(1)}) custom-call(f32[2,4,640]{2,1,0:T(4,128)S(1)} %collective-permute-done.2.up_ref, f32[2,4,640]{2,1,0:T(4,128)S(1)} %pad_maximum_fusion.4.here_ref, f32[2,4,640]{2,1,0:T(4,128)S(1)} %collective-permute-done.3.down_ref), custom_call_target="tpu_custom_call" | custom-call | tf_op jit(solution)/shard_map/pallas_call | solution.py:228
  24.3 0.3 collective-permute-start.4
  24.6 1.0 %collective-permute-done.4 = f32[56,128]{1,0:T(8,128)S(1)} collective-permute-done((f32[56,128]{1,0:T(8,128)S(1)}, f32[56,128]{1,0:T(8,128)S(1)}, u32[]{:S(2)}, u32[]{:S(2)}) %collective-permute-start.4) | collective-permute-done | bytes 28704 | tf_op jit(solution)/shard_map/ppermute | solution.py:426
  25.6 3.0 %collective-permute-start.6 = (f32[56,128]{1,0:T(8,128)S(1)}, f32[56,128]{1,0:T(8,128)S(1)}, u32[]{:S(2)}, u32[]{:S(2)}) collective-permute-start(f32[56,128]{1,0:T(8,128)S(1)} %pad_maximum_fusion), channel_id=1, source_target_pairs={{0,64},{16,80},{32,96},{48,112},{64,0},{80,16},{96,32},{112,48},{1... | collective-permute-start | bytes 86024 | tf_op jit(solution)/shard_map/ppermute | solution.py:426
  28.7 2.2 %collective-permute-start.7 = (f32[56,128]{1,0:T(8,128)S(1)}, f32[56,128]{1,0:T(8,128)S(1)}, u32[]{:S(2)}, u32[]{:S(2)}) collective-permute-start(f32[56,128]{1,0:T(8,128)S(1)} %pad_maximum_fusion), channel_id=1, source_target_pairs={{0,96},{16,112},{32,64},{48,80},{64,32},{80,48},{96,0},{112,16},{1... | collective-permute-start | bytes 86024 | tf_op jit(solution)/shard_map/ppermute | solution.py:426
  30.9 0.2 collective-permute-start.5
  31.1 0.0 collective-permute-done.6
  31.1 2.1 %collective-permute-done.7 = f32[56,128]{1,0:T(8,128)S(1)} collective-permute-done((f32[56,128]{1,0:T(8,128)S(1)}, f32[56,128]{1,0:T(8,128)S(1)}, u32[]{:S(2)}, u32[]{:S(2)}) %collective-permute-start.7) | collective-permute-done | bytes 28704 | tf_op jit(solution)/shard_map/ppermute | solution.py:426
  33.2 0.7 %collective-permute-done.5 = f32[56,128]{1,0:T(8,128)S(1)} collective-permute-done((f32[56,128]{1,0:T(8,128)S(1)}, f32[56,128]{1,0:T(8,128)S(1)}, u32[]{:S(2)}, u32[]{:S(2)}) %collective-permute-start.5) | collective-permute-done | bytes 28704 | tf_op jit(solution)/shard_map/ppermute | solution.py:426
  34.0 5.2 %collective-permute-start.8 = (f32[56,128]{1,0:T(8,128)S(1)}, f32[56,128]{1,0:T(8,128)S(1)}, u32[]{:S(2)}, u32[]{:S(2)}) collective-permute-start(f32[56,128]{1,0:T(8,128)S(1)} %pad_maximum_fusion.1), channel_id=1, source_target_pairs={{0,128},{16,144},{32,160},{48,176},{64,192},{80,208},{96,224},{112... | collective-permute-start | bytes 86024 | tf_op jit(solution)/shard_map/ppermute | solution.py:426
  39.2 1.5 %collective-permute-done.8 = f32[56,128]{1,0:T(8,128)S(1)} collective-permute-done((f32[56,128]{1,0:T(8,128)S(1)}, f32[56,128]{1,0:T(8,128)S(1)}, u32[]{:S(2)}, u32[]{:S(2)}) %collective-permute-start.8) | collective-permute-done | bytes 28704 | tf_op jit(solution)/shard_map/ppermute | solution.py:426
  40.8 17.8 %all_to_all.5 = f32[16,56,128]{2,1,0:T(8,128)S(1)} all-to-all(f32[16,56,128]{2,1,0:T(8,128)S(1)} %broadcast_in_dim.32), channel_id=1, replica_groups=mesh['gx'=16,'gy'=16] {'gy'}, dimensions={0} | all-to-all | bytes 917504 | tf_op jit(solution)/shard_map/all_to_all | solution.py:431
  58.7 4.2 %collective-permute-start.9 = (f32[56,128]{1,0:T(8,128)S(1)}, f32[56,128]{1,0:T(8,128)S(1)}, u32[]{:S(2)}, u32[]{:S(2)}) collective-permute-start(f32[56,128]{1,0:T(8,128)S(1)} %pad_maximum_fusion.3.mine_ref), channel_id=1, source_target_pairs={{0,16},{16,0},{32,48},{48,32},{64,80},{80,64},{96,112},{112,96},{1... | collective-permute-start | bytes 86024 | tf_op jit(solution)/shard_map/ppermute | solution.py:426
  62.9 0.9 %collective-permute-done.9.other_ref = f32[56,128]{1,0:T(8,128)S(1)} collective-permute-done((f32[56,128]{1,0:T(8,128)S(1)}, f32[56,128]{1,0:T(8,128)S(1)}, u32[]{:S(2)}, u32[]{:S(2)}) %collective-permute-start.9) | collective-permute-done | bytes 28704 | tf_op jit(solution)/shard_map/ppermute | solution.py:426
  63.7 9.2 %shard_map.51 = (f32[4,32,1024]{2,1,0:T(8,128)}, f32[4,32,1024]{2,1,0:T(8,128)}) custom-call(f32[56,128]{1,0:T(8,128)S(1)} %pad_maximum_fusion.3.mine_ref, f32[56,128]{1,0:T(8,128)S(1)} %collective-permute-done.9.other_ref, f32[8,128]{1,0:T(8,128)S(1)} %get-tuple-element.8.unit_ref, f32[256,2048]{1,0:T(8,128)S(1)} %get-tuple-element.9.fields_ref), custom_call_target="tpu_custom_call" | custom-call | tf_op jit(solution)/shard_map/pallas_call | solution.py:398
  (15 shorter events, 0.2 us)
Async XLA Ops:
  2.7 5.9 %collective-permute-start = (f32[2,4,64]{2,1,0:T(4,128)S(1)}, f32[2,4,64]{2,1,0:T(4,128)S(1)}, u32[]{:S(2)}, u32[]{:S(2)}) collective-permute-start(f32[2,4,64]{2,1,0:T(4,128)S(1)} %get-tuple-element.28), channel_id=1, source_target_pairs={{1,0},{2,1},{3,2},{4,3},{5,4},{6,5},{7,6},{8,7},{9,8},{10,9},{11,1... | collective-permute-start | bytes 6152 | tf_op jit(solution)/shard_map/ppermute | solution.py:439
  4.0 5.3 %collective-permute-start.1 = (f32[2,4,64]{2,1,0:T(4,128)S(1)}, f32[2,4,64]{2,1,0:T(4,128)S(1)}, u32[]{:S(2)}, u32[]{:S(2)}) collective-permute-start(f32[2,4,64]{2,1,0:T(4,128)S(1)} %get-tuple-element.29), channel_id=1, source_target_pairs={{0,1},{1,2},{2,3},{3,4},{4,5},{5,6},{6,7},{7,8},{8,9},{9,10},{10,1... | collective-permute-start | bytes 6152 | tf_op jit(solution)/shard_map/ppermute | solution.py:439
  9.4 7.6 %collective-permute-start.3 = (f32[2,4,640]{2,1,0:T(4,128)S(1)}, f32[2,4,640]{2,1,0:T(4,128)S(1)}, u32[]{:S(2)}, u32[]{:S(2)}) collective-permute-start(f32[2,4,640]{2,1,0:T(4,128)S(1)} %pad_maximum_fusion.4.here_ref), channel_id=1, source_target_pairs={{16,0},{32,16},{48,32},{64,48},{80,64},{96,80},{112,96},{128,112},... | collective-permute-start | bytes 61448 | tf_op jit(solution)/shard_map/ppermute | solution.py:439
  15.1 3.1 %collective-permute-start.2 = (f32[2,4,640]{2,1,0:T(4,128)S(1)}, f32[2,4,640]{2,1,0:T(4,128)S(1)}, u32[]{:S(2)}, u32[]{:S(2)}) collective-permute-start(f32[2,4,640]{2,1,0:T(4,128)S(1)} %pad_maximum_fusion.4.here_ref), channel_id=1, source_target_pairs={{0,16},{16,32},{32,48},{48,64},{64,80},{80,96},{96,112},{112,128},... | collective-permute-start | bytes 61448 | tf_op jit(solution)/shard_map/ppermute | solution.py:439
  24.3 1.3 %collective-permute-start.4 = (f32[56,128]{1,0:T(8,128)S(1)}, f32[56,128]{1,0:T(8,128)S(1)}, u32[]{:S(2)}, u32[]{:S(2)}) collective-permute-start(f32[56,128]{1,0:T(8,128)S(1)} %get-tuple-element.7), channel_id=1, source_target_pairs={{0,16},{16,0},{32,48},{48,32},{64,80},{80,64},{96,112},{112,96},{1... | collective-permute-start | bytes 86024 | tf_op jit(solution)/shard_map/ppermute | solution.py:426
  25.6 5.5 %collective-permute-start.6 = (f32[56,128]{1,0:T(8,128)S(1)}, f32[56,128]{1,0:T(8,128)S(1)}, u32[]{:S(2)}, u32[]{:S(2)}) collective-permute-start(f32[56,128]{1,0:T(8,128)S(1)} %pad_maximum_fusion), channel_id=1, source_target_pairs={{0,64},{16,80},{32,96},{48,112},{64,0},{80,16},{96,32},{112,48},{1... | collective-permute-start | bytes 86024 | tf_op jit(solution)/shard_map/ppermute | solution.py:426
  28.7 4.5 %collective-permute-start.7 = (f32[56,128]{1,0:T(8,128)S(1)}, f32[56,128]{1,0:T(8,128)S(1)}, u32[]{:S(2)}, u32[]{:S(2)}) collective-permute-start(f32[56,128]{1,0:T(8,128)S(1)} %pad_maximum_fusion), channel_id=1, source_target_pairs={{0,96},{16,112},{32,64},{48,80},{64,32},{80,48},{96,0},{112,16},{1... | collective-permute-start | bytes 86024 | tf_op jit(solution)/shard_map/ppermute | solution.py:426
  30.9 3.0 %collective-permute-start.5 = (f32[56,128]{1,0:T(8,128)S(1)}, f32[56,128]{1,0:T(8,128)S(1)}, u32[]{:S(2)}, u32[]{:S(2)}) collective-permute-start(f32[56,128]{1,0:T(8,128)S(1)} %pad_maximum_fusion), channel_id=1, source_target_pairs={{0,32},{16,48},{32,0},{48,16},{64,96},{80,112},{96,64},{112,80},{1... | collective-permute-start | bytes 86024 | tf_op jit(solution)/shard_map/ppermute | solution.py:426
  34.0 6.7 %collective-permute-start.8 = (f32[56,128]{1,0:T(8,128)S(1)}, f32[56,128]{1,0:T(8,128)S(1)}, u32[]{:S(2)}, u32[]{:S(2)}) collective-permute-start(f32[56,128]{1,0:T(8,128)S(1)} %pad_maximum_fusion.1), channel_id=1, source_target_pairs={{0,128},{16,144},{32,160},{48,176},{64,192},{80,208},{96,224},{112... | collective-permute-start | bytes 86024 | tf_op jit(solution)/shard_map/ppermute | solution.py:426
  58.7 5.1 %collective-permute-start.9 = (f32[56,128]{1,0:T(8,128)S(1)}, f32[56,128]{1,0:T(8,128)S(1)}, u32[]{:S(2)}, u32[]{:S(2)}) collective-permute-start(f32[56,128]{1,0:T(8,128)S(1)} %pad_maximum_fusion.3.mine_ref), channel_id=1, source_target_pairs={{0,16},{16,0},{32,48},{48,32},{64,80},{80,64},{96,112},{112,96},{1... | collective-permute-start | bytes 86024 | tf_op jit(solution)/shard_map/ppermute | solution.py:426

commit v4 on v3

--- a/solution.py
+++ b/solution.py
@@ -280,12 +280,14 @@
             below = [splat(strip, after - base + j) for j in range(PANEL)]
         tiles = [t for t in range(0, total, 128) if t + 128 > after]
         values = small + ahead + [work[at:after, t:t + 128] for t in tiles]
+        scale = jnp.ones((PANEL, 128), F32)
         for j in range(PANEL):
-            factor = values[j]
-            inverse = 1.0 / line(factor, j)
+            inverse = 1.0 / line(values[j], j)
+            scale = jnp.where(sub == j, inverse, scale)
+            factor = jnp.where(sub == j, 0.0, values[j]) * inverse
             for i in range(j + 1, len(values)):
-                scaled = line(values[i], j) * inverse
-                values[i] = jnp.where(sub == j, scaled, values[i] - factor * scaled)
+                values[i] = values[i] - factor * line(values[i], j)
+        values = [value * scale for value in values]
         ahead = values[PANEL:PANEL + len(ahead)]
         rows = values[PANEL + len(ahead):]
         if after < stop:
@@ -325,7 +327,8 @@
 
 
 def finish_kernel(
-    mine_ref, other_ref, unit_ref, fields_ref, solution_ref, residual_ref, work, coeff, mixed
+    mine_ref, other_ref, unit_ref, fields_ref, solution_out, residual_out,
+    work, coeff, mixed, solution_ref, residual_ref, sems,
 ):
     rows, cols = solution_ref.shape[:2]
     size = ITERS * K
@@ -381,6 +384,7 @@
     coeff[3 * K:4 * K, K:2 * K] = -unit * y2
     own = cols * NZ
     low = lax.broadcasted_iota(jnp.int32, (cols, 2 * K), 1) < K
+    copies = []
     for row in range(rows):
         mixed[...] = lax.dot_general(
             coeff[...], fields_ref[:, row * own:(row + 1) * own], (((0,), (0,)), ((), ())),
@@ -391,6 +395,14 @@
             odd = mixed[pl.ds(z + 1, cols, stride=NZ), :]
             solution_ref[row, :, z * K:(z + 2) * K] = jnp.where(low, even, pltpu.roll(odd, K, 1))
             residual_ref[row, :, z * K:(z + 2) * K] = jnp.where(low, pltpu.roll(even, K, 1), odd)
+        for side, (here, there) in enumerate(
+            ((solution_ref, solution_out), (residual_ref, residual_out))
+        ):
+            copy = pltpu.make_async_copy(here.at[row], there.at[row], sems.at[side, row])
+            copy.start()
+            copies.append(copy)
+    for copy in copies:
+        copy.wait()
 
 
 def finish(mine, other, unit, fields, rows, cols):
@@ -399,11 +411,14 @@
         finish_kernel,
         out_shape=(out, out),
         in_specs=[pl.BlockSpec(memory_space=pltpu.VMEM)] * 4,
-        out_specs=[pl.BlockSpec(memory_space=pltpu.VMEM)] * 2,
+        out_specs=[pl.BlockSpec(memory_space=pl.ANY)] * 2,
         scratch_shapes=[
             pltpu.VMEM((ITERS * K, (ITERS + 1) * K), F32),
             pltpu.VMEM(((ITERS + 1) * K, 2 * K), F32),
             pltpu.VMEM((cols * NZ, 2 * K), F32),
+            pltpu.VMEM((rows, cols, NZ * K), F32),
+            pltpu.VMEM((rows, cols, NZ * K), F32),
+            pltpu.SemaphoreType.DMA((2, rows)),
         ],
         compiler_params=pltpu.CompilerParams(vmem_limit_bytes=40 * 1024 * 1024),
     )(mine, other, unit, fields)
@@ -434,9 +449,12 @@
 
 def from_both(first, last, axis):
     count = lax.axis_size(axis)
-    forward = [(i, i + 1) for i in range(count - 1)]
-    backward = [(target, source) for source, target in forward]
-    return lax.ppermute(last, axis, forward), lax.ppermute(first, axis, backward)
+    even = lax.rem(lax.axis_index(axis), 2) == 0
+    outer = [(i, ((i + 1) ^ 1) - 1) for i in range(1, count - 1)]
+    inner = [(i, i ^ 1) for i in range(count)]
+    one = lax.ppermute(jnp.where(even, first, last), axis, outer)
+    two = lax.ppermute(jnp.where(even, last, first), axis, inner)
+    return jnp.where(even, one, two), jnp.where(even, two, one)
 
 
 def shards(diffusivity, labels, obstacles):
@@ -444,7 +462,7 @@
     conductive = diffusivity * (1 - obstacles).astype(F32)
     plane = lax.broadcasted_iota(jnp.int32, (2,) + conductive.shape, 0)
     cells = jnp.where(plane == 0, conductive[None], labels.astype(F32)[None])
-    cells = cells.reshape(2, rows, cols * NZ)
+    cells = lax.optimization_barrier(cells).reshape(2, rows, cols * NZ)
     edge = DEEP * NZ
     before, after = from_both(cells[:, :, :edge], cells[:, :, -edge:], "gy")
     here = jnp.concatenate([cells, after, before], axis=2)

time: 73.3 us -> 69.8 us (0.952)
  starting transfers between devices: 28.6 us -> 21.5 us
  waiting for transfers between devices: 8.1 us -> 10.5 us
  blocking collectives: 17.8 us -> 19.7 us
  Pallas kernels: 15.4 us -> 14.6 us
    ppermute x4, starting transfers between devices: 13.5 us -> 8.46 us  [the longest x2 5.9 us: from_both(): two = lax.ppermute(jnp.where(even, last, first), axis, inner)]
    ppermute x6, starting transfers between devices: 15.1 us -> 13 us  [flipped(): lax.ppermute(value, axis, [(i, i ^ mask) for i in range(count)])]
    all_to_all x1, blocking collectives: 17.8 us -> 19.7 us  [sum_of_all(): lax.all_to_all(jnp.broadcast_to(value[None], (count,) + value.shape), axi...]
    ppermute x4, waiting for transfers between devices: 1.88 us -> 3.5 us  [the longest x2 3.16 us: from_both(): one = lax.ppermute(jnp.where(even, first, last), axis, outer)]
    pallas_call x1, Pallas kernels: 9.24 us -> 8.43 us  [finish(): pl.pallas_call(finish_kernel, out_shape=(out, out), in_specs=[pl.BlockSpe...]
    ppermute x6, waiting for transfers between devices: 6.22 us -> 7.02 us  [flipped(): lax.ppermute(value, axis, [(i, i ^ mask) for i in range(count)])]
where the time goes in v4:
time: 69.8 us; the launch traced here: 69.5 us
  starting transfers between devices  21.5 us (31%)
  blocking collectives  19.7 us (28%)
  Pallas kernels  14.6 us (21%)
  waiting for transfers between devices  10.5 us (15%)
  other arithmetic  1.97 us (3%)
  between operations  0.92 us (1%)
    all_to_all x1, blocking collectives, sum_of_all(): lax.all_to_all(jnp.broadcast_to(value[None], (count,) + value.shape), axi...  19.7 us
    ppermute x6, starting transfers between devices, flipped(): lax.ppermute(value, axis, [(i, i ^ mask) for i in range(count)])  13 us
    pallas_call x1, Pallas kernels, finish(): pl.pallas_call(finish_kernel, out_shape=(out, out), in_specs=[pl.BlockSpe...  8.43 us
    ppermute x6, waiting for transfers between devices, flipped(): lax.ppermute(value, axis, [(i, i ^ mask) for i in range(count)])  7.02 us
    pallas_call x1, Pallas kernels, krylov(): pl.pallas_call(krylov_kernel, out_shape=(jax.ShapeDtypeStruct(((ITERS + 1...  6.15 us
    ppermute x2, starting transfers between devices, from_both(): two = lax.ppermute(jnp.where(even, last, first), axis, inner)  5.9 us
    ppermute x2, waiting for transfers between devices, from_both(): one = lax.ppermute(jnp.where(even, first, last), axis, outer)  3.16 us
    ppermute x2, starting transfers between devices, from_both(): one = lax.ppermute(jnp.where(even, first, last), axis, outer)  2.56 us
  transfers between devices with their start and end apart: 10, of which 7 were waited for; matrix products, arithmetic and copies ran while one was open for 0% of the time, Pallas kernels for 0%

profile of v4, /device:TPU:1, one launch (start us, length us, event | category | flops | bytes accessed | tf_op | source)
XLA Modules:
  0.0 69.5 jit_solution(12655648371409857246)
XLA Ops:
  0.7 0.8 %convert_multiply_fusion = f32[4,32,16]{1,2,0:T(8,128)S(1)} fusion(f32[4,32,16]{1,2,0:T(8,128)} %param.3, s32[4,32,16]{1,2,0:T(8,128)} %param.5), kind=kLoop, calls=%fused_computation.1 | loop fusion | flops 6144 | bytes 24576 | tf_op jit(solution)/shard_map/mul | solution.py:462
  1.4 0.1 copy.7
  1.5 0.8 %convert_element_type.7 = f32[4,32,16]{1,2,0:T(8,128)S(1)} convert(s32[4,32,16]{1,2,0:T(8,128)} %param.4) | non-fusion elementwise | flops 2048 | bytes 16384 | tf_op jit(solution)/shard_map/convert_element_type | solution.py:464
  2.3 0.1 copy.8
  2.4 0.1 broadcast_select_fusion
  2.5 0.1 reshape.34
  2.6 0.1 slice_select_fusion.1
  2.6 2.1 %collective-permute-start = (f32[2,4,64]{2,1,0:T(4,128)S(1)}, f32[2,4,64]{2,1,0:T(4,128)S(1)}, u32[]{:S(2)}, u32[]{:S(2)}) collective-permute-start(f32[2,4,64]{2,1,0:T(4,128)S(1)} %get-tuple-element.30), channel_id=1, source_target_pairs={{0,1},{1,0},{2,3},{3,2},{4,5},{5,4},{6,7},{7,6},{8,9},{9,8},{10,11... | collective-permute-start | bytes 6152 | tf_op jit(solution)/shard_map/ppermute | solution.py:456
  4.7 0.6 collective-permute-start.1
  5.4 0.3 collective-permute-done
  5.7 0.0 collective-permute-done.1
  5.7 0.1 pad_maximum_fusion.4.here_ref
  5.8 3.8 %collective-permute-start.3 = (f32[2,4,640]{2,1,0:T(4,128)S(1)}, f32[2,4,640]{2,1,0:T(4,128)S(1)}, u32[]{:S(2)}, u32[]{:S(2)}) collective-permute-start(f32[2,4,640]{2,1,0:T(4,128)S(1)} %pad_maximum_fusion.4.here_ref), channel_id=1, source_target_pairs={{0,16},{16,0},{32,48},{48,32},{64,80},{80,64},{96,112},{112,96},{1... | collective-permute-start | bytes 61448 | tf_op jit(solution)/shard_map/ppermute | solution.py:456
  9.6 1.9 %collective-permute-start.2 = (f32[2,4,640]{2,1,0:T(4,128)S(1)}, f32[2,4,640]{2,1,0:T(4,128)S(1)}, u32[]{:S(2)}, u32[]{:S(2)}) collective-permute-start(f32[2,4,640]{2,1,0:T(4,128)S(1)} %pad_maximum_fusion.4.here_ref), channel_id=1, source_target_pairs={{16,32},{32,16},{48,64},{64,48},{80,96},{96,80},{112,128},{128,112... | collective-permute-start | bytes 61448 | tf_op jit(solution)/shard_map/ppermute | solution.py:455
  11.6 0.0 collective-permute-done.3
  11.6 3.2 %collective-permute-done.2 = f32[2,4,640]{2,1,0:T(4,128)S(1)} collective-permute-done((f32[2,4,640]{2,1,0:T(4,128)S(1)}, f32[2,4,640]{2,1,0:T(4,128)S(1)}, u32[]{:S(2)}, u32[]{:S(2)}) %collective-permute-start.2) | collective-permute-done | bytes 20512 | tf_op jit(solution)/shard_map/ppermute | solution.py:455
  14.7 6.1 %shard_map.50 = (f32[256,2048]{1,0:T(8,128)S(1)}, f32[56,128]{1,0:T(8,128)S(1)}, f32[56,128]{1,0:T(8,128)S(1)}, f32[8,128]{1,0:T(8,128)S(1)}) custom-call(f32[2,4,640]{2,1,0:T(4,128)S(1)} %bitcast.232, f32[2,4,640]{2,1,0:T(4,128)S(1)} %pad_maximum_fusion.4.here_ref, f32[2,4,640]{2,1,0:T(4,128)S(1)} %bitcast.231), custom_call_target="tpu_custom_call" | custom-call | tf_op jit(solution)/shard_map/pallas_call | solution.py:228
  20.9 0.1 collective-permute-start.4
  21.0 1.2 %collective-permute-done.4 = f32[56,128]{1,0:T(8,128)S(1)} collective-permute-done((f32[56,128]{1,0:T(8,128)S(1)}, f32[56,128]{1,0:T(8,128)S(1)}, u32[]{:S(2)}, u32[]{:S(2)}) %collective-permute-start.4) | collective-permute-done | bytes 28704 | tf_op jit(solution)/shard_map/ppermute | solution.py:441
  22.2 1.3 %collective-permute-start.6 = (f32[56,128]{1,0:T(8,128)S(1)}, f32[56,128]{1,0:T(8,128)S(1)}, u32[]{:S(2)}, u32[]{:S(2)}) collective-permute-start(f32[56,128]{1,0:T(8,128)S(1)} %pad_maximum_fusion), channel_id=1, source_target_pairs={{0,64},{16,80},{32,96},{48,112},{64,0},{80,16},{96,32},{112,48},{1... | collective-permute-start | bytes 86024 | tf_op jit(solution)/shard_map/ppermute | solution.py:441
  23.6 2.7 %collective-permute-start.7 = (f32[56,128]{1,0:T(8,128)S(1)}, f32[56,128]{1,0:T(8,128)S(1)}, u32[]{:S(2)}, u32[]{:S(2)}) collective-permute-start(f32[56,128]{1,0:T(8,128)S(1)} %pad_maximum_fusion), channel_id=1, source_target_pairs={{0,96},{16,112},{32,64},{48,80},{64,32},{80,48},{96,0},{112,16},{1... | collective-permute-start | bytes 86024 | tf_op jit(solution)/shard_map/ppermute | solution.py:441
  26.2 0.2 collective-permute-start.5
  26.4 0.0 collective-permute-done.6
  26.4 1.7 %collective-permute-done.7 = f32[56,128]{1,0:T(8,128)S(1)} collective-permute-done((f32[56,128]{1,0:T(8,128)S(1)}, f32[56,128]{1,0:T(8,128)S(1)}, u32[]{:S(2)}, u32[]{:S(2)}) %collective-permute-start.7) | collective-permute-done | bytes 28704 | tf_op jit(solution)/shard_map/ppermute | solution.py:441
  28.1 1.2 %collective-permute-done.5 = f32[56,128]{1,0:T(8,128)S(1)} collective-permute-done((f32[56,128]{1,0:T(8,128)S(1)}, f32[56,128]{1,0:T(8,128)S(1)}, u32[]{:S(2)}, u32[]{:S(2)}) %collective-permute-start.5) | collective-permute-done | bytes 28704 | tf_op jit(solution)/shard_map/ppermute | solution.py:441
  29.3 4.6 %collective-permute-start.8 = (f32[56,128]{1,0:T(8,128)S(1)}, f32[56,128]{1,0:T(8,128)S(1)}, u32[]{:S(2)}, u32[]{:S(2)}) collective-permute-start(f32[56,128]{1,0:T(8,128)S(1)} %pad_maximum_fusion.1), channel_id=1, source_target_pairs={{0,128},{16,144},{32,160},{48,176},{64,192},{80,208},{96,224},{112... | collective-permute-start | bytes 86024 | tf_op jit(solution)/shard_map/ppermute | solution.py:441
  33.9 2.1 %collective-permute-done.8 = f32[56,128]{1,0:T(8,128)S(1)} collective-permute-done((f32[56,128]{1,0:T(8,128)S(1)}, f32[56,128]{1,0:T(8,128)S(1)}, u32[]{:S(2)}, u32[]{:S(2)}) %collective-permute-start.8) | collective-permute-done | bytes 28704 | tf_op jit(solution)/shard_map/ppermute | solution.py:441
  36.1 19.7 %all_to_all.5 = f32[16,56,128]{2,1,0:T(8,128)S(1)} all-to-all(f32[16,56,128]{2,1,0:T(8,128)S(1)} %broadcast_in_dim.26), channel_id=1, replica_groups=mesh['gx'=16,'gy'=16] {'gy'}, dimensions={0} | all-to-all | bytes 917504 | tf_op jit(solution)/shard_map/all_to_all | solution.py:446
  55.9 4.1 %collective-permute-start.9 = (f32[56,128]{1,0:T(8,128)S(1)}, f32[56,128]{1,0:T(8,128)S(1)}, u32[]{:S(2)}, u32[]{:S(2)}) collective-permute-start(f32[56,128]{1,0:T(8,128)S(1)} %pad_maximum_fusion.3.mine_ref), channel_id=1, source_target_pairs={{0,16},{16,0},{32,48},{48,32},{64,80},{80,64},{96,112},{112,96},{1... | collective-permute-start | bytes 86024 | tf_op jit(solution)/shard_map/ppermute | solution.py:441
  60.0 0.9 %collective-permute-done.9.other_ref = f32[56,128]{1,0:T(8,128)S(1)} collective-permute-done((f32[56,128]{1,0:T(8,128)S(1)}, f32[56,128]{1,0:T(8,128)S(1)}, u32[]{:S(2)}, u32[]{:S(2)}) %collective-permute-start.9) | collective-permute-done | bytes 28704 | tf_op jit(solution)/shard_map/ppermute | solution.py:441
  60.9 8.4 %shard_map.51 = (f32[4,32,1024]{2,1,0:T(8,128)}, f32[4,32,1024]{2,1,0:T(8,128)}) custom-call(f32[56,128]{1,0:T(8,128)S(1)} %pad_maximum_fusion.3.mine_ref, f32[56,128]{1,0:T(8,128)S(1)} %collective-permute-done.9.other_ref, f32[8,128]{1,0:T(8,128)S(1)} %get-tuple-element.8.unit_ref, f32[256,2048]{1,0:T(8,128)S(1)} %get-tuple-element.9.fields_ref), custom_call_target="tpu_custom_call" | custom-call | tf_op jit(solution)/shard_map/pallas_call | solution.py:410
  (17 shorter events, 0.2 us)
Async XLA Ops:
  2.6 3.1 %collective-permute-start = (f32[2,4,64]{2,1,0:T(4,128)S(1)}, f32[2,4,64]{2,1,0:T(4,128)S(1)}, u32[]{:S(2)}, u32[]{:S(2)}) collective-permute-start(f32[2,4,64]{2,1,0:T(4,128)S(1)} %get-tuple-element.30), channel_id=1, source_target_pairs={{0,1},{1,0},{2,3},{3,2},{4,5},{5,4},{6,7},{7,6},{8,9},{9,8},{10,11... | collective-permute-start | bytes 6152 | tf_op jit(solution)/shard_map/ppermute | solution.py:456
  4.7 1.0 %collective-permute-start.1 = (f32[2,4,64]{2,1,0:T(4,128)S(1)}, f32[2,4,64]{2,1,0:T(4,128)S(1)}, u32[]{:S(2)}, u32[]{:S(2)}) collective-permute-start(f32[2,4,64]{2,1,0:T(4,128)S(1)} %get-tuple-element.31), channel_id=1, source_target_pairs={{1,2},{2,1},{3,4},{4,3},{5,6},{6,5},{7,8},{8,7},{9,10},{10,9},{11,... | collective-permute-start | bytes 6152 | tf_op jit(solution)/shard_map/ppermute | solution.py:455
  5.8 5.8 %collective-permute-start.3 = (f32[2,4,640]{2,1,0:T(4,128)S(1)}, f32[2,4,640]{2,1,0:T(4,128)S(1)}, u32[]{:S(2)}, u32[]{:S(2)}) collective-permute-start(f32[2,4,640]{2,1,0:T(4,128)S(1)} %pad_maximum_fusion.4.here_ref), channel_id=1, source_target_pairs={{0,16},{16,0},{32,48},{48,32},{64,80},{80,64},{96,112},{112,96},{1... | collective-permute-start | bytes 61448 | tf_op jit(solution)/shard_map/ppermute | solution.py:456
  9.6 5.1 %collective-permute-start.2 = (f32[2,4,640]{2,1,0:T(4,128)S(1)}, f32[2,4,640]{2,1,0:T(4,128)S(1)}, u32[]{:S(2)}, u32[]{:S(2)}) collective-permute-start(f32[2,4,640]{2,1,0:T(4,128)S(1)} %pad_maximum_fusion.4.here_ref), channel_id=1, source_target_pairs={{16,32},{32,16},{48,64},{64,48},{80,96},{96,80},{112,128},{128,112... | collective-permute-start | bytes 61448 | tf_op jit(solution)/shard_map/ppermute | solution.py:455
  20.9 1.3 %collective-permute-start.4 = (f32[56,128]{1,0:T(8,128)S(1)}, f32[56,128]{1,0:T(8,128)S(1)}, u32[]{:S(2)}, u32[]{:S(2)}) collective-permute-start(f32[56,128]{1,0:T(8,128)S(1)} %get-tuple-element.7), channel_id=1, source_target_pairs={{0,16},{16,0},{32,48},{48,32},{64,80},{80,64},{96,112},{112,96},{1... | collective-permute-start | bytes 86024 | tf_op jit(solution)/shard_map/ppermute | solution.py:441
  22.2 4.2 %collective-permute-start.6 = (f32[56,128]{1,0:T(8,128)S(1)}, f32[56,128]{1,0:T(8,128)S(1)}, u32[]{:S(2)}, u32[]{:S(2)}) collective-permute-start(f32[56,128]{1,0:T(8,128)S(1)} %pad_maximum_fusion), channel_id=1, source_target_pairs={{0,64},{16,80},{32,96},{48,112},{64,0},{80,16},{96,32},{112,48},{1... | collective-permute-start | bytes 86024 | tf_op jit(solution)/shard_map/ppermute | solution.py:441
  23.6 4.5 %collective-permute-start.7 = (f32[56,128]{1,0:T(8,128)S(1)}, f32[56,128]{1,0:T(8,128)S(1)}, u32[]{:S(2)}, u32[]{:S(2)}) collective-permute-start(f32[56,128]{1,0:T(8,128)S(1)} %pad_maximum_fusion), channel_id=1, source_target_pairs={{0,96},{16,112},{32,64},{48,80},{64,32},{80,48},{96,0},{112,16},{1... | collective-permute-start | bytes 86024 | tf_op jit(solution)/shard_map/ppermute | solution.py:441
  26.2 3.1 %collective-permute-start.5 = (f32[56,128]{1,0:T(8,128)S(1)}, f32[56,128]{1,0:T(8,128)S(1)}, u32[]{:S(2)}, u32[]{:S(2)}) collective-permute-start(f32[56,128]{1,0:T(8,128)S(1)} %pad_maximum_fusion), channel_id=1, source_target_pairs={{0,32},{16,48},{32,0},{48,16},{64,96},{80,112},{96,64},{112,80},{1... | collective-permute-start | bytes 86024 | tf_op jit(solution)/shard_map/ppermute | solution.py:441
  29.3 6.7 %collective-permute-start.8 = (f32[56,128]{1,0:T(8,128)S(1)}, f32[56,128]{1,0:T(8,128)S(1)}, u32[]{:S(2)}, u32[]{:S(2)}) collective-permute-start(f32[56,128]{1,0:T(8,128)S(1)} %pad_maximum_fusion.1), channel_id=1, source_target_pairs={{0,128},{16,144},{32,160},{48,176},{64,192},{80,208},{96,224},{112... | collective-permute-start | bytes 86024 | tf_op jit(solution)/shard_map/ppermute | solution.py:441
  55.9 5.0 %collective-permute-start.9 = (f32[56,128]{1,0:T(8,128)S(1)}, f32[56,128]{1,0:T(8,128)S(1)}, u32[]{:S(2)}, u32[]{:S(2)}) collective-permute-start(f32[56,128]{1,0:T(8,128)S(1)} %pad_maximum_fusion.3.mine_ref), channel_id=1, source_target_pairs={{0,16},{16,0},{32,48},{48,32},{64,80},{80,64},{96,112},{112,96},{1... | collective-permute-start | bytes 86024 | tf_op jit(solution)/shard_map/ppermute | solution.py:441

commit v5 on v4

--- a/solution.py
+++ b/solution.py
@@ -27,7 +27,7 @@
 
 def krylov_kernel(
     up_ref, here_ref, down_ref, fields_ref, keep_ref, send_ref, unit_ref,
-    cond, label, couple, weight, nbr, diag, v0, v1, v2, v3, gram,
+    cond, label, couple, weight, nbr, diag, v0, v1, v2, gram,
 ):
     rows = here_ref.shape[1]
     lanes = here_ref.shape[2]
@@ -68,55 +68,56 @@
     for side in range(6):
         couple[side] = couple[side] * inverse
 
-    step = 16
+    step = 32
     cluster = lax.broadcasted_iota(jnp.int32, (step, lanes), 0)
-
-    def fill(row, carry):
+    powers = (v0, v1, v2)
+
+    def store(order, row, cut, value):
+        if order < ITERS:
+            powers[order][row, cut, :] = value
+        at = row - (ITERS - order)
+        if 0 <= at < rows:
+            fields_ref[order * K + cut.start:order * K + cut.stop, at * own:(at + 1) * own] = (
+                value[:, 0:own]
+            )
+
+    def fill(row):
         for part in range(0, K, step):
             ids = (cluster + (part + 1)).astype(F32)
             acc = jnp.zeros((step, lanes), F32)
             for side in range(6):
-                hit = nbr[side, pl.ds(row, 1), :] == ids
-                acc = acc + jnp.where(hit, weight[side, pl.ds(row, 1), :], 0.0)
-            v0[row, part:part + step, :] = acc
-        return carry
-
-    lax.fori_loop(0, inner, fill, 0, unroll=True)
-
-    def power(source, target, offset, count):
-        def body(row, carry):
-            at = row + offset + 1
-            for part in range(0, K, step):
-                cut = slice(part, part + step)
-                mid = source[row + 1, cut, :]
-                acc = diag[pl.ds(at, 1), :] * mid
-                acc = acc - couple[0, pl.ds(at, 1), :] * source[row + 2, cut, :]
-                acc = acc - couple[1, pl.ds(at, 1), :] * source[row, cut, :]
-                acc = acc - couple[2, pl.ds(at, 1), :] * pltpu.roll(mid, lanes - NZ, 1)
-                acc = acc - couple[3, pl.ds(at, 1), :] * pltpu.roll(mid, NZ, 1)
-                acc = acc - couple[4, pl.ds(at, 1), :] * pltpu.roll(mid, lanes - 1, 1)
-                acc = acc - couple[5, pl.ds(at, 1), :] * pltpu.roll(mid, 1, 1)
-                target[row, cut, :] = acc
-            return carry
-
-        lax.fori_loop(0, count, body, 0, unroll=True)
-
-    power(v0, v1, 0, inner - 2)
-    power(v1, v2, 1, inner - 4)
-    power(v2, v3, 2, inner - 6)
-    for order, ref in enumerate((v0, v1, v2, v3)):
-        for row in range(rows):
-            fields_ref[order * K:(order + 1) * K, row * own:(row + 1) * own] = ref[
-                row + ITERS - order, :, 0:own
-            ]
-    chunk = 256
-    wide = fields_ref.shape[1]
-    for at in range(0, wide, chunk):
-        part = lax.dot_general(
-            fields_ref[0:ITERS * K, at:at + chunk], fields_ref[:, at:at + chunk],
-            (((1,), (1,)), ((), ())), precision=HIGH, preferred_element_type=F32,
-        )
-        gram[...] = part if at == 0 else gram[...] + part
+                hit = nbr[side, row:row + 1, :] == ids
+                acc = acc + jnp.where(hit, weight[side, row:row + 1, :], 0.0)
+            store(0, row, slice(part, part + step), acc)
+
+    def power(order, row):
+        source = powers[order - 1]
+        at = row + order
+        for part in range(0, K, step):
+            cut = slice(part, part + step)
+            mid = source[row + 1, cut, :]
+            acc = diag[at:at + 1, :] * mid
+            acc = acc - couple[0, at:at + 1, :] * source[row + 2, cut, :]
+            acc = acc - couple[1, at:at + 1, :] * source[row, cut, :]
+            acc = acc - couple[2, at:at + 1, :] * pltpu.roll(mid, lanes - NZ, 1)
+            acc = acc - couple[3, at:at + 1, :] * pltpu.roll(mid, NZ, 1)
+            acc = acc - couple[4, at:at + 1, :] * pltpu.roll(mid, lanes - 1, 1)
+            acc = acc - couple[5, at:at + 1, :] * pltpu.roll(mid, 1, 1)
+            store(order, row, cut, acc)
+
+    for front in range(inner):
+        fill(front)
+        for order in range(1, ITERS + 1):
+            if front >= 2 * order:
+                power(order, front - 2 * order)
+        at = front - 2 * ITERS
+        if at >= 0:
+            part = lax.dot_general(
+                fields_ref[0:ITERS * K, at * own:(at + 1) * own],
+                fields_ref[:, at * own:(at + 1) * own],
+                (((1,), (1,)), ((), ())), precision=HIGH, preferred_element_type=F32,
+            )
+            gram[...] = part if at == 0 else gram[...] + part
     pack(gram, unit, keep_ref, send_ref)
 
 
@@ -245,7 +246,6 @@
             pltpu.VMEM((inner, K, lanes), F32),
             pltpu.VMEM((inner - 2, K, lanes), F32),
             pltpu.VMEM((inner - 4, K, lanes), F32),
-            pltpu.VMEM((inner - 6, K, lanes), F32),
             pltpu.VMEM((ITERS * K, (ITERS + 1) * K), F32),
         ],
         compiler_params=pltpu.CompilerParams(vmem_limit_bytes=40 * 1024 * 1024),
@@ -449,20 +449,27 @@
 
 def from_both(first, last, axis):
     count = lax.axis_size(axis)
-    even = lax.rem(lax.axis_index(axis), 2) == 0
-    outer = [(i, ((i + 1) ^ 1) - 1) for i in range(1, count - 1)]
+    here = lax.axis_index(axis)
+    even = lax.rem(here, 2) == 0
+    outer = [(i, (((i + 1) ^ 1) - 1) % count) for i in range(count)]
     inner = [(i, i ^ 1) for i in range(count)]
     one = lax.ppermute(jnp.where(even, first, last), axis, outer)
     two = lax.ppermute(jnp.where(even, last, first), axis, inner)
-    return jnp.where(even, one, two), jnp.where(even, two, one)
+    odd = ~even
+    before, after = jnp.where(odd, two, one), jnp.where(odd, one, two)
+    return jnp.where(here == 0, 0.0, before), jnp.where(here == count - 1, 0.0, after)
 
 
 def shards(diffusivity, labels, obstacles):
     rows, cols = diffusivity.shape[:2]
+    diffusivity, labels, obstacles = (
+        jnp.transpose(value, (0, 2, 1)) for value in (diffusivity, labels, obstacles)
+    )
     conductive = diffusivity * (1 - obstacles).astype(F32)
     plane = lax.broadcasted_iota(jnp.int32, (2,) + conductive.shape, 0)
     cells = jnp.where(plane == 0, conductive[None], labels.astype(F32)[None])
-    cells = lax.optimization_barrier(cells).reshape(2, rows, cols * NZ)
+    cells = jnp.transpose(lax.optimization_barrier(cells), (0, 1, 3, 2))
+    cells = cells.reshape(2, rows, cols * NZ)
     edge = DEEP * NZ
     before, after = from_both(cells[:, :, :edge], cells[:, :, -edge:], "gy")
     here = jnp.concatenate([cells, after, before], axis=2)

time: 69.8 us -> 65.6 us (0.940)
  blocking collectives: 19.7 us -> 12.8 us
  starting transfers between devices: 21.5 us -> 24.7 us
    all_to_all x1, blocking collectives: 19.7 us -> 12.8 us  [sum_of_all(): lax.all_to_all(jnp.broadcast_to(value[None], (count,) + value.shape), axi...]
    ppermute x2, starting transfers between devices: 2.56 us -> 9.14 us  [from_both(): one = lax.ppermute(jnp.where(even, first, last), axis, outer)]
    ppermute x2, starting transfers between devices: 5.9 us -> 2.35 us  [from_both(): two = lax.ppermute(jnp.where(even, last, first), axis, inner)]
    ppermute x2, waiting for transfers between devices: 0.34 us -> 2.6 us  [from_both(): two = lax.ppermute(jnp.where(even, last, first), axis, inner)]
    ppermute x2, waiting for transfers between devices: 3.16 us -> 1 us  [from_both(): one = lax.ppermute(jnp.where(even, first, last), axis, outer)]
  transfers between devices with their start and end apart: 10 -> 10, of which waited for: 7 -> 8; matrix products, arithmetic and copies ran while one was open for 0% -> 0% of each run, Pallas kernels for 0% -> 0%
where the time goes in v5:
time: 65.6 us; the launch traced here: 65.4 us
  starting transfers between devices  24.7 us (38%)
  Pallas kernels  14.2 us (22%)
  blocking collectives  12.8 us (20%)
  waiting for transfers between devices  10.4 us (16%)
  other arithmetic  1.98 us (3%)
  between operations  0.89 us (1%)
    ppermute x6, starting transfers between devices, flipped(): lax.ppermute(value, axis, [(i, i ^ mask) for i in range(count)])  13.3 us
    all_to_all x1, blocking collectives, sum_of_all(): lax.all_to_all(jnp.broadcast_to(value[None], (count,) + value.shape), axi...  12.8 us
    ppermute x2, starting transfers between devices, from_both(): one = lax.ppermute(jnp.where(even, first, last), axis, outer)  9.14 us
    pallas_call x1, Pallas kernels, finish(): pl.pallas_call(finish_kernel, out_shape=(out, out), in_specs=[pl.BlockSpe...  8.43 us
    ppermute x6, waiting for transfers between devices, flipped(): lax.ppermute(value, axis, [(i, i ^ mask) for i in range(count)])  6.77 us
    pallas_call x1, Pallas kernels, krylov(): pl.pallas_call(krylov_kernel, out_shape=(jax.ShapeDtypeStruct(((ITERS + 1...  5.81 us
    ppermute x2, waiting for transfers between devices, from_both(): two = lax.ppermute(jnp.where(even, last, first), axis, inner)  2.6 us
    ppermute x2, starting transfers between devices, from_both(): two = lax.ppermute(jnp.where(even, last, first), axis, inner)  2.35 us
  transfers between devices with their start and end apart: 10, of which 8 were waited for; matrix products, arithmetic and copies ran while one was open for 0% of the time, Pallas kernels for 0%

profile of v5, /device:TPU:1, one launch (start us, length us, event | category | flops | bytes accessed | tf_op | source)
XLA Modules:
  0.0 65.4 jit_solution(10329393530458770916)
XLA Ops:
  0.7 0.8 %multiply_bitcast_fusion = f32[4,16,32]{2,1,0:T(8,128)S(1)} fusion(f32[4,32,16]{1,2,0:T(8,128)} %param.3, s32[4,32,16]{1,2,0:T(8,128)} %param.5), kind=kLoop, calls=%fused_computation.2 | loop fusion | flops 6144 | bytes 24576 | tf_op jit(solution)/shard_map/mul | solution.py:468
  1.4 0.1 copy.7
  1.5 0.8 %convert_bitcast_fusion = f32[4,16,32]{2,1,0:T(8,128)S(1)} fusion(s32[4,32,16]{1,2,0:T(8,128)} %param.4), kind=kLoop, calls=%fused_computation.1 | loop fusion | flops 2048 | bytes 16384 | tf_op jit(solution)/shard_map/convert_element_type | solution.py:470
  2.3 0.1 copy.8
  2.4 0.1 broadcast_select_fusion
  2.5 0.1 reshape.34
  2.6 0.1 slice_select_fusion.1
  2.6 5.8 %collective-permute-start = (f32[2,4,64]{2,1,0:T(4,128)S(1)}, f32[2,4,64]{2,1,0:T(4,128)S(1)}, u32[]{:S(2)}, u32[]{:S(2)}) collective-permute-start(f32[2,4,64]{2,1,0:T(4,128)S(1)} %get-tuple-element.30), channel_id=1, source_target_pairs={{0,15},{1,2},{2,1},{3,4},{4,3},{5,6},{6,5},{7,8},{8,7},{9,10},{10,... | collective-permute-start | bytes 6152 | tf_op jit(solution)/shard_map/ppermute | solution.py:456
  8.4 0.0 collective-permute-start.1
  8.4 1.0 %collective-permute-done = f32[2,4,64]{2,1,0:T(4,128)S(1)} collective-permute-done((f32[2,4,64]{2,1,0:T(4,128)S(1)}, f32[2,4,64]{2,1,0:T(4,128)S(1)}, u32[]{:S(2)}, u32[]{:S(2)}) %collective-permute-start) | collective-permute-done | bytes 2080 | tf_op jit(solution)/shard_map/ppermute | solution.py:456
  9.4 1.8 %collective-permute-done.1 = f32[2,4,64]{2,1,0:T(4,128)S(1)} collective-permute-done((f32[2,4,64]{2,1,0:T(4,128)S(1)}, f32[2,4,64]{2,1,0:T(4,128)S(1)}, u32[]{:S(2)}, u32[]{:S(2)}) %collective-permute-start.1) | collective-permute-done | bytes 2080 | tf_op jit(solution)/shard_map/ppermute | solution.py:457
  11.2 0.1 pad_maximum_fusion.4.here_ref
  11.3 3.4 %collective-permute-start.3 = (f32[2,4,640]{2,1,0:T(4,128)S(1)}, f32[2,4,640]{2,1,0:T(4,128)S(1)}, u32[]{:S(2)}, u32[]{:S(2)}) collective-permute-start(f32[2,4,640]{2,1,0:T(4,128)S(1)} %pad_maximum_fusion.4.here_ref), channel_id=1, source_target_pairs={{0,240},{16,32},{32,16},{48,64},{64,48},{80,96},{96,80},{112,128},... | collective-permute-start | bytes 61448 | tf_op jit(solution)/shard_map/ppermute | solution.py:456
  14.6 2.3 %collective-permute-start.2 = (f32[2,4,640]{2,1,0:T(4,128)S(1)}, f32[2,4,640]{2,1,0:T(4,128)S(1)}, u32[]{:S(2)}, u32[]{:S(2)}) collective-permute-start(f32[2,4,640]{2,1,0:T(4,128)S(1)} %pad_maximum_fusion.4.here_ref), channel_id=1, source_target_pairs={{0,16},{16,0},{32,48},{48,32},{64,80},{80,64},{96,112},{112,96},{1... | collective-permute-start | bytes 61448 | tf_op jit(solution)/shard_map/ppermute | solution.py:457
  17.0 0.0 collective-permute-done.3
  17.0 0.8 %collective-permute-done.2 = f32[2,4,640]{2,1,0:T(4,128)S(1)} collective-permute-done((f32[2,4,640]{2,1,0:T(4,128)S(1)}, f32[2,4,640]{2,1,0:T(4,128)S(1)}, u32[]{:S(2)}, u32[]{:S(2)}) %collective-permute-start.2) | collective-permute-done | bytes 20512 | tf_op jit(solution)/shard_map/ppermute | solution.py:457
  17.8 5.8 %shard_map.50 = (f32[256,2048]{1,0:T(8,128)S(1)}, f32[56,128]{1,0:T(8,128)S(1)}, f32[56,128]{1,0:T(8,128)S(1)}, f32[8,128]{1,0:T(8,128)S(1)}) custom-call(f32[2,4,640]{2,1,0:T(4,128)S(1)} %get-tuple-element.29.up_ref, f32[2,4,640]{2,1,0:T(4,128)S(1)} %pad_maximum_fusion.4.here_ref, f32[2,4,640]{2,1,0:T(4,128)S(1)} %get-tuple-element.28.down_ref), custom_call_target="tpu_custom_call" | custom-call | tf_op jit(solution)/shard_map/pallas_call | solution.py:229
  23.6 0.7 %collective-permute-start.4 = (f32[56,128]{1,0:T(8,128)S(1)}, f32[56,128]{1,0:T(8,128)S(1)}, u32[]{:S(2)}, u32[]{:S(2)}) collective-permute-start(f32[56,128]{1,0:T(8,128)S(1)} %get-tuple-element.7), channel_id=1, source_target_pairs={{0,16},{16,0},{32,48},{48,32},{64,80},{80,64},{96,112},{112,96},{1... | collective-permute-start | bytes 86024 | tf_op jit(solution)/shard_map/ppermute | solution.py:441
  24.4 0.9 %collective-permute-done.4 = f32[56,128]{1,0:T(8,128)S(1)} collective-permute-done((f32[56,128]{1,0:T(8,128)S(1)}, f32[56,128]{1,0:T(8,128)S(1)}, u32[]{:S(2)}, u32[]{:S(2)}) %collective-permute-start.4) | collective-permute-done | bytes 28704 | tf_op jit(solution)/shard_map/ppermute | solution.py:441
  25.3 1.1 %collective-permute-start.6 = (f32[56,128]{1,0:T(8,128)S(1)}, f32[56,128]{1,0:T(8,128)S(1)}, u32[]{:S(2)}, u32[]{:S(2)}) collective-permute-start(f32[56,128]{1,0:T(8,128)S(1)} %pad_maximum_fusion), channel_id=1, source_target_pairs={{0,64},{16,80},{32,96},{48,112},{64,0},{80,16},{96,32},{112,48},{1... | collective-permute-start | bytes 86024 | tf_op jit(solution)/shard_map/ppermute | solution.py:441
  26.3 2.7 %collective-permute-start.7 = (f32[56,128]{1,0:T(8,128)S(1)}, f32[56,128]{1,0:T(8,128)S(1)}, u32[]{:S(2)}, u32[]{:S(2)}) collective-permute-start(f32[56,128]{1,0:T(8,128)S(1)} %pad_maximum_fusion), channel_id=1, source_target_pairs={{0,96},{16,112},{32,64},{48,80},{64,32},{80,48},{96,0},{112,16},{1... | collective-permute-start | bytes 86024 | tf_op jit(solution)/shard_map/ppermute | solution.py:441
  29.0 0.2 collective-permute-start.5
  29.2 0.0 collective-permute-done.6
  29.2 1.7 %collective-permute-done.7 = f32[56,128]{1,0:T(8,128)S(1)} collective-permute-done((f32[56,128]{1,0:T(8,128)S(1)}, f32[56,128]{1,0:T(8,128)S(1)}, u32[]{:S(2)}, u32[]{:S(2)}) %collective-permute-start.7) | collective-permute-done | bytes 28704 | tf_op jit(solution)/shard_map/ppermute | solution.py:441
  30.8 1.2 %collective-permute-done.5 = f32[56,128]{1,0:T(8,128)S(1)} collective-permute-done((f32[56,128]{1,0:T(8,128)S(1)}, f32[56,128]{1,0:T(8,128)S(1)}, u32[]{:S(2)}, u32[]{:S(2)}) %collective-permute-start.5) | collective-permute-done | bytes 28704 | tf_op jit(solution)/shard_map/ppermute | solution.py:441
  32.1 4.6 %collective-permute-start.8 = (f32[56,128]{1,0:T(8,128)S(1)}, f32[56,128]{1,0:T(8,128)S(1)}, u32[]{:S(2)}, u32[]{:S(2)}) collective-permute-start(f32[56,128]{1,0:T(8,128)S(1)} %pad_maximum_fusion.1), channel_id=1, source_target_pairs={{0,128},{16,144},{32,160},{48,176},{64,192},{80,208},{96,224},{112... | collective-permute-start | bytes 86024 | tf_op jit(solution)/shard_map/ppermute | solution.py:441
  36.7 2.1 %collective-permute-done.8 = f32[56,128]{1,0:T(8,128)S(1)} collective-permute-done((f32[56,128]{1,0:T(8,128)S(1)}, f32[56,128]{1,0:T(8,128)S(1)}, u32[]{:S(2)}, u32[]{:S(2)}) %collective-permute-start.8) | collective-permute-done | bytes 28704 | tf_op jit(solution)/shard_map/ppermute | solution.py:441
  38.9 12.8 %all_to_all.5 = f32[16,56,128]{2,1,0:T(8,128)S(1)} all-to-all(f32[16,56,128]{2,1,0:T(8,128)S(1)} %broadcast_in_dim.38), channel_id=1, replica_groups=mesh['gx'=16,'gy'=16] {'gy'}, dimensions={0} | all-to-all | bytes 917504 | tf_op jit(solution)/shard_map/all_to_all | solution.py:446
  51.9 4.1 %collective-permute-start.9 = (f32[56,128]{1,0:T(8,128)S(1)}, f32[56,128]{1,0:T(8,128)S(1)}, u32[]{:S(2)}, u32[]{:S(2)}) collective-permute-start(f32[56,128]{1,0:T(8,128)S(1)} %pad_maximum_fusion.3.mine_ref), channel_id=1, source_target_pairs={{0,16},{16,0},{32,48},{48,32},{64,80},{80,64},{96,112},{112,96},{1... | collective-permute-start | bytes 86024 | tf_op jit(solution)/shard_map/ppermute | solution.py:441
  55.9 0.9 %collective-permute-done.9.other_ref = f32[56,128]{1,0:T(8,128)S(1)} collective-permute-done((f32[56,128]{1,0:T(8,128)S(1)}, f32[56,128]{1,0:T(8,128)S(1)}, u32[]{:S(2)}, u32[]{:S(2)}) %collective-permute-start.9) | collective-permute-done | bytes 28704 | tf_op jit(solution)/shard_map/ppermute | solution.py:441
  56.8 8.4 %shard_map.51 = (f32[4,32,1024]{2,1,0:T(8,128)}, f32[4,32,1024]{2,1,0:T(8,128)}) custom-call(f32[56,128]{1,0:T(8,128)S(1)} %pad_maximum_fusion.3.mine_ref, f32[56,128]{1,0:T(8,128)S(1)} %collective-permute-done.9.other_ref, f32[8,128]{1,0:T(8,128)S(1)} %get-tuple-element.8.unit_ref, f32[256,2048]{1,0:T(8,128)S(1)} %get-tuple-element.9.fields_ref), custom_call_target="tpu_custom_call" | custom-call | tf_op jit(solution)/shard_map/pallas_call | solution.py:410
  (17 shorter events, 0.2 us)
Async XLA Ops:
  2.6 6.8 %collective-permute-start = (f32[2,4,64]{2,1,0:T(4,128)S(1)}, f32[2,4,64]{2,1,0:T(4,128)S(1)}, u32[]{:S(2)}, u32[]{:S(2)}) collective-permute-start(f32[2,4,64]{2,1,0:T(4,128)S(1)} %get-tuple-element.30), channel_id=1, source_target_pairs={{0,15},{1,2},{2,1},{3,4},{4,3},{5,6},{6,5},{7,8},{8,7},{9,10},{10,... | collective-permute-start | bytes 6152 | tf_op jit(solution)/shard_map/ppermute | solution.py:456
  8.4 2.8 %collective-permute-start.1 = (f32[2,4,64]{2,1,0:T(4,128)S(1)}, f32[2,4,64]{2,1,0:T(4,128)S(1)}, u32[]{:S(2)}, u32[]{:S(2)}) collective-permute-start(f32[2,4,64]{2,1,0:T(4,128)S(1)} %get-tuple-element.31), channel_id=1, source_target_pairs={{0,1},{1,0},{2,3},{3,2},{4,5},{5,4},{6,7},{7,6},{8,9},{9,8},{10,11... | collective-permute-start | bytes 6152 | tf_op jit(solution)/shard_map/ppermute | solution.py:457
  11.3 5.7 %collective-permute-start.3 = (f32[2,4,640]{2,1,0:T(4,128)S(1)}, f32[2,4,640]{2,1,0:T(4,128)S(1)}, u32[]{:S(2)}, u32[]{:S(2)}) collective-permute-start(f32[2,4,640]{2,1,0:T(4,128)S(1)} %pad_maximum_fusion.4.here_ref), channel_id=1, source_target_pairs={{0,240},{16,32},{32,16},{48,64},{64,48},{80,96},{96,80},{112,128},... | collective-permute-start | bytes 61448 | tf_op jit(solution)/shard_map/ppermute | solution.py:456
  14.6 3.2 %collective-permute-start.2 = (f32[2,4,640]{2,1,0:T(4,128)S(1)}, f32[2,4,640]{2,1,0:T(4,128)S(1)}, u32[]{:S(2)}, u32[]{:S(2)}) collective-permute-start(f32[2,4,640]{2,1,0:T(4,128)S(1)} %pad_maximum_fusion.4.here_ref), channel_id=1, source_target_pairs={{0,16},{16,0},{32,48},{48,32},{64,80},{80,64},{96,112},{112,96},{1... | collective-permute-start | bytes 61448 | tf_op jit(solution)/shard_map/ppermute | solution.py:457
  23.6 1.6 %collective-permute-start.4 = (f32[56,128]{1,0:T(8,128)S(1)}, f32[56,128]{1,0:T(8,128)S(1)}, u32[]{:S(2)}, u32[]{:S(2)}) collective-permute-start(f32[56,128]{1,0:T(8,128)S(1)} %get-tuple-element.7), channel_id=1, source_target_pairs={{0,16},{16,0},{32,48},{48,32},{64,80},{80,64},{96,112},{112,96},{1... | collective-permute-start | bytes 86024 | tf_op jit(solution)/shard_map/ppermute | solution.py:441
  25.3 3.9 %collective-permute-start.6 = (f32[56,128]{1,0:T(8,128)S(1)}, f32[56,128]{1,0:T(8,128)S(1)}, u32[]{:S(2)}, u32[]{:S(2)}) collective-permute-start(f32[56,128]{1,0:T(8,128)S(1)} %pad_maximum_fusion), channel_id=1, source_target_pairs={{0,64},{16,80},{32,96},{48,112},{64,0},{80,16},{96,32},{112,48},{1... | collective-permute-start | bytes 86024 | tf_op jit(solution)/shard_map/ppermute | solution.py:441
  26.3 4.5 %collective-permute-start.7 = (f32[56,128]{1,0:T(8,128)S(1)}, f32[56,128]{1,0:T(8,128)S(1)}, u32[]{:S(2)}, u32[]{:S(2)}) collective-permute-start(f32[56,128]{1,0:T(8,128)S(1)} %pad_maximum_fusion), channel_id=1, source_target_pairs={{0,96},{16,112},{32,64},{48,80},{64,32},{80,48},{96,0},{112,16},{1... | collective-permute-start | bytes 86024 | tf_op jit(solution)/shard_map/ppermute | solution.py:441
  29.0 3.1 %collective-permute-start.5 = (f32[56,128]{1,0:T(8,128)S(1)}, f32[56,128]{1,0:T(8,128)S(1)}, u32[]{:S(2)}, u32[]{:S(2)}) collective-permute-start(f32[56,128]{1,0:T(8,128)S(1)} %pad_maximum_fusion), channel_id=1, source_target_pairs={{0,32},{16,48},{32,0},{48,16},{64,96},{80,112},{96,64},{112,80},{1... | collective-permute-start | bytes 86024 | tf_op jit(solution)/shard_map/ppermute | solution.py:441
  32.1 6.7 %collective-permute-start.8 = (f32[56,128]{1,0:T(8,128)S(1)}, f32[56,128]{1,0:T(8,128)S(1)}, u32[]{:S(2)}, u32[]{:S(2)}) collective-permute-start(f32[56,128]{1,0:T(8,128)S(1)} %pad_maximum_fusion.1), channel_id=1, source_target_pairs={{0,128},{16,144},{32,160},{48,176},{64,192},{80,208},{96,224},{112... | collective-permute-start | bytes 86024 | tf_op jit(solution)/shard_map/ppermute | solution.py:441
  51.9 4.9 %collective-permute-start.9 = (f32[56,128]{1,0:T(8,128)S(1)}, f32[56,128]{1,0:T(8,128)S(1)}, u32[]{:S(2)}, u32[]{:S(2)}) collective-permute-start(f32[56,128]{1,0:T(8,128)S(1)} %pad_maximum_fusion.3.mine_ref), channel_id=1, source_target_pairs={{0,16},{16,0},{32,48},{48,32},{64,80},{80,64},{96,112},{112,96},{1... | collective-permute-start | bytes 86024 | tf_op jit(solution)/shard_map/ppermute | solution.py:441

commit v6 on v5

--- a/solution.py
+++ b/solution.py
@@ -23,6 +23,40 @@
 def face(here, there):
     product = here * there
     return 2.0 * product / jnp.where(product > 0, here + there, 1.0)
+
+
+def cells_kernel(
+    diffusivity_hbm, labels_hbm, obstacles_hbm, cells_ref,
+    diffusivity_ref, labels_ref, obstacles_ref, sems,
+):
+    copies = [
+        pltpu.make_async_copy(there, here, sems.at[i])
+        for i, (there, here) in enumerate((
+            (obstacles_hbm, obstacles_ref),
+            (diffusivity_hbm, diffusivity_ref),
+            (labels_hbm, labels_ref),
+        ))
+    ]
+    for copy in copies:
+        copy.start()
+    for copy in copies:
+        copy.wait()
+    for row in range(diffusivity_ref.shape[0]):
+        clear = obstacles_ref[row] == 0
+        cells_ref[0, row] = jnp.where(clear, diffusivity_ref[row], 0.0).T
+        cells_ref[1, row] = labels_ref[row].astype(F32).T
+
+
+def cells_of(diffusivity, labels, obstacles):
+    views = [jnp.transpose(value, (0, 2, 1)) for value in (diffusivity, labels, obstacles)]
+    return pl.pallas_call(
+        cells_kernel,
+        out_shape=jax.ShapeDtypeStruct((2,) + diffusivity.shape, F32),
+        in_specs=[pl.BlockSpec(memory_space=pltpu.HBM)] * 3,
+        out_specs=pl.BlockSpec(memory_space=pltpu.VMEM),
+        scratch_shapes=[pltpu.VMEM(view.shape, view.dtype) for view in views]
+        + [pltpu.SemaphoreType.DMA((3,))],
+    )(*views)
 
 
 def krylov_kernel(
@@ -462,14 +496,7 @@
 
 def shards(diffusivity, labels, obstacles):
     rows, cols = diffusivity.shape[:2]
-    diffusivity, labels, obstacles = (
-        jnp.transpose(value, (0, 2, 1)) for value in (diffusivity, labels, obstacles)
-    )
-    conductive = diffusivity * (1 - obstacles).astype(F32)
-    plane = lax.broadcasted_iota(jnp.int32, (2,) + conductive.shape, 0)
-    cells = jnp.where(plane == 0, conductive[None], labels.astype(F32)[None])
-    cells = jnp.transpose(lax.optimization_barrier(cells), (0, 1, 3, 2))
-    cells = cells.reshape(2, rows, cols * NZ)
+    cells = cells_of(diffusivity, labels, obstacles).reshape(2, rows, cols * NZ)
     edge = DEEP * NZ
     before, after = from_both(cells[:, :, :edge], cells[:, :, -edge:], "gy")
     here = jnp.concatenate([cells, after, before], axis=2)
@@ -477,7 +504,7 @@
     fields, keep, send, unit = krylov(up, here, down)
     mine = add_parts(keep, *flipped(send, "gx", 1))
     mine = add_parts(mine, *flipped(mine, "gx", 2, 4, 6))
-    mine = add_parts(mine, *flipped(mine, "gx", 8))
+    mine = add_parts(mine, *flipped(mine, "gx", 12))
     mine = sum_of_all(mine, "gy")
     return finish(mine, *flipped(mine, "gx", 1), unit, fields, rows, cols)
 

time: 65.6 us -> 64.1 us (0.977)
  starting transfers between devices: 24.7 us -> 22.8 us
  other arithmetic: 1.98 us -> 0.33 us
  Pallas kernels: 14.2 us -> 15.5 us
  local copies, waits for them, and re-layouts: 0.31 us -> 1.06 us
    ppermute x6, starting transfers between devices: 13.3 us -> 11.3 us  [flipped(): lax.ppermute(value, axis, [(i, i ^ mask) for i in range(count)])]
    pallas_call x0 -> x1, Pallas kernels: none -> 1.57 us  [cells_of(): pl.pallas_call(cells_kernel, out_shape=jax.ShapeDtypeStruct((2,) + diffus...]
    reshape x1, local copies, waits for them, and re-layouts: 0.12 us -> 1.02 us  [shards(): cells = cells_of(diffusivity, labels, obstacles).reshape(2, rows, cols * NZ)]
    mul x1 -> x0, other arithmetic: 0.78 us -> none  [shards(): conductive = diffusivity * (1 - obstacles).astype(F32)]
    convert_element_type x1 -> x0, other arithmetic: 0.77 us -> none  [shards(): cells = jnp.where(plane == 0, conductive[None], labels.astype(F32)[None])]
where the time goes in v6:
time: 64.1 us; the launch traced here: 63.9 us
  starting transfers between devices  22.8 us (36%)
  Pallas kernels  15.5 us (24%)
  blocking collectives  12.8 us (20%)
  waiting for transfers between devices  10.5 us (16%)
  local copies, waits for them, and re-layouts  1.06 us (2%)
  between operations  0.88 us (1%)
    all_to_all x1, blocking collectives, sum_of_all(): lax.all_to_all(jnp.broadcast_to(value[None], (count,) + value.shape), axi...  12.8 us
    ppermute x6, starting transfers between devices, flipped(): lax.ppermute(value, axis, [(i, i ^ mask) for i in range(count)])  11.3 us
    ppermute x2, starting transfers between devices, from_both(): one = lax.ppermute(jnp.where(even, first, last), axis, outer)  9.14 us
    pallas_call x1, Pallas kernels, finish(): pl.pallas_call(finish_kernel, out_shape=(out, out), in_specs=[pl.BlockSpe...  8.39 us
    ppermute x6, waiting for transfers between devices, flipped(): lax.ppermute(value, axis, [(i, i ^ mask) for i in range(count)])  6.91 us
    pallas_call x1, Pallas kernels, krylov(): pl.pallas_call(krylov_kernel, out_shape=(jax.ShapeDtypeStruct(((ITERS + 1...  5.55 us
    ppermute x2, waiting for transfers between devices, from_both(): two = lax.ppermute(jnp.where(even, last, first), axis, inner)  2.6 us
    ppermute x2, starting transfers between devices, from_both(): two = lax.ppermute(jnp.where(even, last, first), axis, inner)  2.35 us
  transfers between devices with their start and end apart: 10, of which 8 were waited for; matrix products, arithmetic and copies ran while one was open for 0% of the time, Pallas kernels for 0%

profile of v6, /device:TPU:1, one launch (start us, length us, event | category | flops | bytes accessed | tf_op | source)
XLA Modules:
  0.0 63.9 jit_solution(15562473181005642199)
XLA Ops:
  0.6 1.6 %shard_map.50 = f32[2,4,32,16]{3,2,1,0:T(8,128)} custom-call(f32[4,16,32]{2,1,0:T(8,128)} %bitcast.231, s32[4,16,32]{2,1,0:T(8,128)} %bitcast.232, s32[4,16,32]{2,1,0:T(8,128)} %bitcast.233), custom_call_target="tpu_custom_call" | custom-call | tf_op jit(solution)/shard_map/pallas_call | solution.py:52
  2.2 1.0 %reshape.32 = f32[2,4,512]{2,1,0:T(4,128)S(1)} reshape(f32[2,4,32,16]{3,2,1,0:T(8,128)} %shard_map.50) | data formatting | bytes 32768 | tf_op jit(solution)/shard_map/reshape | solution.py:499
  3.2 0.1 slice_select_fusion.1
  3.3 5.8 %collective-permute-start = (f32[2,4,64]{2,1,0:T(4,128)S(1)}, f32[2,4,64]{2,1,0:T(4,128)S(1)}, u32[]{:S(2)}, u32[]{:S(2)}) collective-permute-start(f32[2,4,64]{2,1,0:T(4,128)S(1)} %get-tuple-element.30), channel_id=1, source_target_pairs={{0,15},{1,2},{2,1},{3,4},{4,3},{5,6},{6,5},{7,8},{8,7},{9,10},{10,... | collective-permute-start | bytes 6152 | tf_op jit(solution)/shard_map/ppermute | solution.py:490
  9.1 0.0 collective-permute-start.1
  9.1 1.0 %collective-permute-done = f32[2,4,64]{2,1,0:T(4,128)S(1)} collective-permute-done((f32[2,4,64]{2,1,0:T(4,128)S(1)}, f32[2,4,64]{2,1,0:T(4,128)S(1)}, u32[]{:S(2)}, u32[]{:S(2)}) %collective-permute-start) | collective-permute-done | bytes 2080 | tf_op jit(solution)/shard_map/ppermute | solution.py:490
  10.1 1.8 %collective-permute-done.1 = f32[2,4,64]{2,1,0:T(4,128)S(1)} collective-permute-done((f32[2,4,64]{2,1,0:T(4,128)S(1)}, f32[2,4,64]{2,1,0:T(4,128)S(1)}, u32[]{:S(2)}, u32[]{:S(2)}) %collective-permute-start.1) | collective-permute-done | bytes 2080 | tf_op jit(solution)/shard_map/ppermute | solution.py:491
  11.9 0.1 pad_maximum_fusion.4.here_ref
  11.9 3.4 %collective-permute-start.3 = (f32[2,4,640]{2,1,0:T(4,128)S(1)}, f32[2,4,640]{2,1,0:T(4,128)S(1)}, u32[]{:S(2)}, u32[]{:S(2)}) collective-permute-start(f32[2,4,640]{2,1,0:T(4,128)S(1)} %pad_maximum_fusion.4.here_ref), channel_id=1, source_target_pairs={{0,240},{16,32},{32,16},{48,64},{64,48},{80,96},{96,80},{112,128},... | collective-permute-start | bytes 61448 | tf_op jit(solution)/shard_map/ppermute | solution.py:490
  15.3 2.3 %collective-permute-start.2 = (f32[2,4,640]{2,1,0:T(4,128)S(1)}, f32[2,4,640]{2,1,0:T(4,128)S(1)}, u32[]{:S(2)}, u32[]{:S(2)}) collective-permute-start(f32[2,4,640]{2,1,0:T(4,128)S(1)} %pad_maximum_fusion.4.here_ref), channel_id=1, source_target_pairs={{0,16},{16,0},{32,48},{48,32},{64,80},{80,64},{96,112},{112,96},{1... | collective-permute-start | bytes 61448 | tf_op jit(solution)/shard_map/ppermute | solution.py:491
  17.6 0.0 collective-permute-done.3
  17.6 0.8 %collective-permute-done.2 = f32[2,4,640]{2,1,0:T(4,128)S(1)} collective-permute-done((f32[2,4,640]{2,1,0:T(4,128)S(1)}, f32[2,4,640]{2,1,0:T(4,128)S(1)}, u32[]{:S(2)}, u32[]{:S(2)}) %collective-permute-start.2) | collective-permute-done | bytes 20512 | tf_op jit(solution)/shard_map/ppermute | solution.py:491
  18.5 5.6 %shard_map.51 = (f32[256,2048]{1,0:T(8,128)S(1)}, f32[56,128]{1,0:T(8,128)S(1)}, f32[56,128]{1,0:T(8,128)S(1)}, f32[8,128]{1,0:T(8,128)S(1)}) custom-call(f32[2,4,640]{2,1,0:T(4,128)S(1)} %get-tuple-element.29.up_ref, f32[2,4,640]{2,1,0:T(4,128)S(1)} %pad_maximum_fusion.4.here_ref, f32[2,4,640]{2,1,0:T(4,128)S(1)} %get-tuple-element.28.down_ref), custom_call_target="tpu_custom_call" | custom-call | tf_op jit(solution)/shard_map/pallas_call | solution.py:263
  24.1 0.7 %collective-permute-start.4 = (f32[56,128]{1,0:T(8,128)S(1)}, f32[56,128]{1,0:T(8,128)S(1)}, u32[]{:S(2)}, u32[]{:S(2)}) collective-permute-start(f32[56,128]{1,0:T(8,128)S(1)} %get-tuple-element.7), channel_id=1, source_target_pairs={{0,16},{16,0},{32,48},{48,32},{64,80},{80,64},{96,112},{112,96},{1... | collective-permute-start | bytes 86024 | tf_op jit(solution)/shard_map/ppermute | solution.py:475
  24.8 0.9 %collective-permute-done.4 = f32[56,128]{1,0:T(8,128)S(1)} collective-permute-done((f32[56,128]{1,0:T(8,128)S(1)}, f32[56,128]{1,0:T(8,128)S(1)}, u32[]{:S(2)}, u32[]{:S(2)}) %collective-permute-start.4) | collective-permute-done | bytes 28704 | tf_op jit(solution)/shard_map/ppermute | solution.py:475
  25.7 1.1 %collective-permute-start.6 = (f32[56,128]{1,0:T(8,128)S(1)}, f32[56,128]{1,0:T(8,128)S(1)}, u32[]{:S(2)}, u32[]{:S(2)}) collective-permute-start(f32[56,128]{1,0:T(8,128)S(1)} %pad_maximum_fusion), channel_id=1, source_target_pairs={{0,64},{16,80},{32,96},{48,112},{64,0},{80,16},{96,32},{112,48},{1... | collective-permute-start | bytes 86024 | tf_op jit(solution)/shard_map/ppermute | solution.py:475
  26.7 2.7 %collective-permute-start.7 = (f32[56,128]{1,0:T(8,128)S(1)}, f32[56,128]{1,0:T(8,128)S(1)}, u32[]{:S(2)}, u32[]{:S(2)}) collective-permute-start(f32[56,128]{1,0:T(8,128)S(1)} %pad_maximum_fusion), channel_id=1, source_target_pairs={{0,96},{16,112},{32,64},{48,80},{64,32},{80,48},{96,0},{112,16},{1... | collective-permute-start | bytes 86024 | tf_op jit(solution)/shard_map/ppermute | solution.py:475
  29.4 0.2 collective-permute-start.5
  29.6 0.0 collective-permute-done.6
  29.6 1.7 %collective-permute-done.7 = f32[56,128]{1,0:T(8,128)S(1)} collective-permute-done((f32[56,128]{1,0:T(8,128)S(1)}, f32[56,128]{1,0:T(8,128)S(1)}, u32[]{:S(2)}, u32[]{:S(2)}) %collective-permute-start.7) | collective-permute-done | bytes 28704 | tf_op jit(solution)/shard_map/ppermute | solution.py:475
  31.3 1.3 %collective-permute-done.5 = f32[56,128]{1,0:T(8,128)S(1)} collective-permute-done((f32[56,128]{1,0:T(8,128)S(1)}, f32[56,128]{1,0:T(8,128)S(1)}, u32[]{:S(2)}, u32[]{:S(2)}) %collective-permute-start.5) | collective-permute-done | bytes 28704 | tf_op jit(solution)/shard_map/ppermute | solution.py:475
  32.6 2.6 %collective-permute-start.8 = (f32[56,128]{1,0:T(8,128)S(1)}, f32[56,128]{1,0:T(8,128)S(1)}, u32[]{:S(2)}, u32[]{:S(2)}) collective-permute-start(f32[56,128]{1,0:T(8,128)S(1)} %pad_maximum_fusion.1), channel_id=1, source_target_pairs={{0,192},{16,208},{32,224},{48,240},{64,128},{80,144},{96,160},{112... | collective-permute-start | bytes 86024 | tf_op jit(solution)/shard_map/ppermute | solution.py:475
  35.2 2.3 %collective-permute-done.8 = f32[56,128]{1,0:T(8,128)S(1)} collective-permute-done((f32[56,128]{1,0:T(8,128)S(1)}, f32[56,128]{1,0:T(8,128)S(1)}, u32[]{:S(2)}, u32[]{:S(2)}) %collective-permute-start.8) | collective-permute-done | bytes 28704 | tf_op jit(solution)/shard_map/ppermute | solution.py:475
  37.6 12.8 %all_to_all.5 = f32[16,56,128]{2,1,0:T(8,128)S(1)} all-to-all(f32[16,56,128]{2,1,0:T(8,128)S(1)} %broadcast_in_dim.18), channel_id=1, replica_groups=mesh['gx'=16,'gy'=16] {'gy'}, dimensions={0} | all-to-all | bytes 917504 | tf_op jit(solution)/shard_map/all_to_all | solution.py:480
  50.5 4.0 %collective-permute-start.9 = (f32[56,128]{1,0:T(8,128)S(1)}, f32[56,128]{1,0:T(8,128)S(1)}, u32[]{:S(2)}, u32[]{:S(2)}) collective-permute-start(f32[56,128]{1,0:T(8,128)S(1)} %pad_maximum_fusion.3.mine_ref), channel_id=1, source_target_pairs={{0,16},{16,0},{32,48},{48,32},{64,80},{80,64},{96,112},{112,96},{1... | collective-permute-start | bytes 86024 | tf_op jit(solution)/shard_map/ppermute | solution.py:475
  54.5 0.9 %collective-permute-done.9.other_ref = f32[56,128]{1,0:T(8,128)S(1)} collective-permute-done((f32[56,128]{1,0:T(8,128)S(1)}, f32[56,128]{1,0:T(8,128)S(1)}, u32[]{:S(2)}, u32[]{:S(2)}) %collective-permute-start.9) | collective-permute-done | bytes 28704 | tf_op jit(solution)/shard_map/ppermute | solution.py:475
  55.4 8.4 %shard_map.52 = (f32[4,32,1024]{2,1,0:T(8,128)}, f32[4,32,1024]{2,1,0:T(8,128)}) custom-call(f32[56,128]{1,0:T(8,128)S(1)} %pad_maximum_fusion.3.mine_ref, f32[56,128]{1,0:T(8,128)S(1)} %collective-permute-done.9.other_ref, f32[8,128]{1,0:T(8,128)S(1)} %get-tuple-element.8.unit_ref, f32[256,2048]{1,0:T(8,128)S(1)} %get-tuple-element.9.fields_ref), custom_call_target="tpu_custom_call" | custom-call | tf_op jit(solution)/shard_map/pallas_call | solution.py:444
  (16 shorter events, 0.2 us)
Async XLA Ops:
  3.3 6.8 %collective-permute-start = (f32[2,4,64]{2,1,0:T(4,128)S(1)}, f32[2,4,64]{2,1,0:T(4,128)S(1)}, u32[]{:S(2)}, u32[]{:S(2)}) collective-permute-start(f32[2,4,64]{2,1,0:T(4,128)S(1)} %get-tuple-element.30), channel_id=1, source_target_pairs={{0,15},{1,2},{2,1},{3,4},{4,3},{5,6},{6,5},{7,8},{8,7},{9,10},{10,... | collective-permute-start | bytes 6152 | tf_op jit(solution)/shard_map/ppermute | solution.py:490
  9.1 2.8 %collective-permute-start.1 = (f32[2,4,64]{2,1,0:T(4,128)S(1)}, f32[2,4,64]{2,1,0:T(4,128)S(1)}, u32[]{:S(2)}, u32[]{:S(2)}) collective-permute-start(f32[2,4,64]{2,1,0:T(4,128)S(1)} %get-tuple-element.31), channel_id=1, source_target_pairs={{0,1},{1,0},{2,3},{3,2},{4,5},{5,4},{6,7},{7,6},{8,9},{9,8},{10,11... | collective-permute-start | bytes 6152 | tf_op jit(solution)/shard_map/ppermute | solution.py:491
  11.9 5.7 %collective-permute-start.3 = (f32[2,4,640]{2,1,0:T(4,128)S(1)}, f32[2,4,640]{2,1,0:T(4,128)S(1)}, u32[]{:S(2)}, u32[]{:S(2)}) collective-permute-start(f32[2,4,640]{2,1,0:T(4,128)S(1)} %pad_maximum_fusion.4.here_ref), channel_id=1, source_target_pairs={{0,240},{16,32},{32,16},{48,64},{64,48},{80,96},{96,80},{112,128},... | collective-permute-start | bytes 61448 | tf_op jit(solution)/shard_map/ppermute | solution.py:490
  15.3 3.2 %collective-permute-start.2 = (f32[2,4,640]{2,1,0:T(4,128)S(1)}, f32[2,4,640]{2,1,0:T(4,128)S(1)}, u32[]{:S(2)}, u32[]{:S(2)}) collective-permute-start(f32[2,4,640]{2,1,0:T(4,128)S(1)} %pad_maximum_fusion.4.here_ref), channel_id=1, source_target_pairs={{0,16},{16,0},{32,48},{48,32},{64,80},{80,64},{96,112},{112,96},{1... | collective-permute-start | bytes 61448 | tf_op jit(solution)/shard_map/ppermute | solution.py:491
  24.1 1.6 %collective-permute-start.4 = (f32[56,128]{1,0:T(8,128)S(1)}, f32[56,128]{1,0:T(8,128)S(1)}, u32[]{:S(2)}, u32[]{:S(2)}) collective-permute-start(f32[56,128]{1,0:T(8,128)S(1)} %get-tuple-element.7), channel_id=1, source_target_pairs={{0,16},{16,0},{32,48},{48,32},{64,80},{80,64},{96,112},{112,96},{1... | collective-permute-start | bytes 86024 | tf_op jit(solution)/shard_map/ppermute | solution.py:475
  25.7 3.9 %collective-permute-start.6 = (f32[56,128]{1,0:T(8,128)S(1)}, f32[56,128]{1,0:T(8,128)S(1)}, u32[]{:S(2)}, u32[]{:S(2)}) collective-permute-start(f32[56,128]{1,0:T(8,128)S(1)} %pad_maximum_fusion), channel_id=1, source_target_pairs={{0,64},{16,80},{32,96},{48,112},{64,0},{80,16},{96,32},{112,48},{1... | collective-permute-start | bytes 86024 | tf_op jit(solution)/shard_map/ppermute | solution.py:475
  26.7 4.5 %collective-permute-start.7 = (f32[56,128]{1,0:T(8,128)S(1)}, f32[56,128]{1,0:T(8,128)S(1)}, u32[]{:S(2)}, u32[]{:S(2)}) collective-permute-start(f32[56,128]{1,0:T(8,128)S(1)} %pad_maximum_fusion), channel_id=1, source_target_pairs={{0,96},{16,112},{32,64},{48,80},{64,32},{80,48},{96,0},{112,16},{1... | collective-permute-start | bytes 86024 | tf_op jit(solution)/shard_map/ppermute | solution.py:475
  29.4 3.1 %collective-permute-start.5 = (f32[56,128]{1,0:T(8,128)S(1)}, f32[56,128]{1,0:T(8,128)S(1)}, u32[]{:S(2)}, u32[]{:S(2)}) collective-permute-start(f32[56,128]{1,0:T(8,128)S(1)} %pad_maximum_fusion), channel_id=1, source_target_pairs={{0,32},{16,48},{32,0},{48,16},{64,96},{80,112},{96,64},{112,80},{1... | collective-permute-start | bytes 86024 | tf_op jit(solution)/shard_map/ppermute | solution.py:475
  32.6 4.9 %collective-permute-start.8 = (f32[56,128]{1,0:T(8,128)S(1)}, f32[56,128]{1,0:T(8,128)S(1)}, u32[]{:S(2)}, u32[]{:S(2)}) collective-permute-start(f32[56,128]{1,0:T(8,128)S(1)} %pad_maximum_fusion.1), channel_id=1, source_target_pairs={{0,192},{16,208},{32,224},{48,240},{64,128},{80,144},{96,160},{112... | collective-permute-start | bytes 86024 | tf_op jit(solution)/shard_map/ppermute | solution.py:475
  50.5 4.9 %collective-permute-start.9 = (f32[56,128]{1,0:T(8,128)S(1)}, f32[56,128]{1,0:T(8,128)S(1)}, u32[]{:S(2)}, u32[]{:S(2)}) collective-permute-start(f32[56,128]{1,0:T(8,128)S(1)} %pad_maximum_fusion.3.mine_ref), channel_id=1, source_target_pairs={{0,16},{16,0},{32,48},{48,32},{64,80},{80,64},{96,112},{112,96},{1... | collective-permute-start | bytes 86024 | tf_op jit(solution)/shard_map/ppermute | solution.py:475

commit v7 on v6

--- a/solution.py
+++ b/solution.py
@@ -56,6 +56,7 @@
         out_specs=pl.BlockSpec(memory_space=pltpu.VMEM),
         scratch_shapes=[pltpu.VMEM(view.shape, view.dtype) for view in views]
         + [pltpu.SemaphoreType.DMA((3,))],
+        compiler_params=pltpu.CompilerParams(vmem_limit_bytes=2 * 1024 * 1024),
     )(*views)
 
 
@@ -485,7 +486,7 @@
     count = lax.axis_size(axis)
     here = lax.axis_index(axis)
     even = lax.rem(here, 2) == 0
-    outer = [(i, (((i + 1) ^ 1) - 1) % count) for i in range(count)]
+    outer = [(i, i if i in (0, count - 1) else ((i + 1) ^ 1) - 1) for i in range(count)]
     inner = [(i, i ^ 1) for i in range(count)]
     one = lax.ppermute(jnp.where(even, first, last), axis, outer)
     two = lax.ppermute(jnp.where(even, last, first), axis, inner)

time: 64.1 us -> 67.3 us (1.050)
  blocking collectives: 12.8 us -> 15.9 us
  local copies, waits for them, and re-layouts: 1.06 us -> 2.42 us
  Pallas kernels: 15.5 us -> 14.5 us
  waiting for transfers between devices: 10.5 us -> 9.59 us
    ppermute x2, starting transfers between devices: 9.14 us -> 5.9 us  [from_both(): one = lax.ppermute(jnp.where(even, first, last), axis, outer)]
    all_to_all x1, blocking collectives: 12.8 us -> 15.9 us  [sum_of_all(): lax.all_to_all(jnp.broadcast_to(value[None], (count,) + value.shape), axi...]
    ppermute x2, starting transfers between devices: 2.35 us -> 4.68 us  [from_both(): two = lax.ppermute(jnp.where(even, last, first), axis, inner)]
    unnamed x0 -> x6, local copies, waits for them, and re-layouts: none -> 2.27 us
    ppermute x2, waiting for transfers between devices: 2.6 us -> 1 us  [from_both(): two = lax.ppermute(jnp.where(even, last, first), axis, inner)]
    ppermute x6, starting transfers between devices: 11.3 us -> 12.7 us  [flipped(): lax.ppermute(value, axis, [(i, i ^ mask) for i in range(count)])]
    pallas_call x1, Pallas kernels: 1.57 us -> 0.22 us  [cells_of(): pl.pallas_call(cells_kernel, out_shape=jax.ShapeDtypeStruct((2,) + diffus...]
    reshape x1, local copies, waits for them, and re-layouts: 1.02 us -> 0.12 us  [shards(): cells = cells_of(diffusivity, labels, obstacles).reshape(2, rows, cols * NZ)]
  transfers between devices with their start and end apart: 10 -> 10, of which waited for: 8 -> 7; matrix products, arithmetic and copies ran while one was open for 0% -> 0% of each run, Pallas kernels for 0% -> 0%
where the time goes in v7:
time: 67.3 us; the launch traced here: 66.9 us
  starting transfers between devices  23.3 us (35%)
  blocking collectives  15.9 us (24%)
  Pallas kernels  14.5 us (22%)
  waiting for transfers between devices  9.59 us (14%)
  local copies, waits for them, and re-layouts  2.42 us (4%)
  between operations  0.94 us (1%)
    all_to_all x1, blocking collectives, sum_of_all(): lax.all_to_all(jnp.broadcast_to(value[None], (count,) + value.shape), axi...  15.9 us
    ppermute x6, starting transfers between devices, flipped(): lax.ppermute(value, axis, [(i, i ^ mask) for i in range(count)])  12.7 us
    pallas_call x1, Pallas kernels, finish(): pl.pallas_call(finish_kernel, out_shape=(out, out), in_specs=[pl.BlockSpe...  8.43 us
    ppermute x6, waiting for transfers between devices, flipped(): lax.ppermute(value, axis, [(i, i ^ mask) for i in range(count)])  7.25 us
    ppermute x2, starting transfers between devices, from_both(): one = lax.ppermute(jnp.where(even, first, last), axis, outer)  5.9 us
    pallas_call x1, Pallas kernels, krylov(): pl.pallas_call(krylov_kernel, out_shape=(jax.ShapeDtypeStruct(((ITERS + 1...  5.81 us
    ppermute x2, starting transfers between devices, from_both(): two = lax.ppermute(jnp.where(even, last, first), axis, inner)  4.68 us
    unnamed x6, local copies, waits for them, and re-layouts  2.27 us
  transfers between devices with their start and end apart: 10, of which 7 were waited for; matrix products, arithmetic and copies ran while one was open for 0% of the time, Pallas kernels for 0%

profile of v7, /device:TPU:1, one launch (start us, length us, event | category | flops | bytes accessed | tf_op | source)
XLA Modules:
  0.0 66.9 jit_solution(7561224494311728370)
XLA Ops:
  0.6 0.0 copy-start
  0.6 0.7 %copy-done = f32[4,32,16]{1,2,0:T(8,128)S(1)} copy-done((f32[4,32,16]{1,2,0:T(8,128)S(1)}, f32[4,32,16]{1,2,0:T(8,128)}, u32[]{:S(2)}) %copy-start) | copy-done | bytes 8216
  1.4 0.0 copy-start.1
  1.4 0.8 %copy-done.1 = s32[4,32,16]{1,2,0:T(8,128)S(1)} copy-done((s32[4,32,16]{1,2,0:T(8,128)S(1)}, s32[4,32,16]{1,2,0:T(8,128)}, u32[]{:S(2)}) %copy-start.1) | copy-done | bytes 8216
  2.2 0.0 copy-start.2
  2.2 0.8 %copy-done.2 = s32[4,32,16]{1,2,0:T(8,128)S(1)} copy-done((s32[4,32,16]{1,2,0:T(8,128)S(1)}, s32[4,32,16]{1,2,0:T(8,128)}, u32[]{:S(2)}) %copy-start.2) | copy-done | bytes 8216
  2.9 0.2 shard_map.50
  3.1 0.1 reshape.32
  3.3 0.1 slice_select_fusion.1
  3.3 0.7 collective-permute-start
  4.0 4.6 %collective-permute-start.1 = (f32[2,4,64]{2,1,0:T(4,128)S(1)}, f32[2,4,64]{2,1,0:T(4,128)S(1)}, u32[]{:S(2)}, u32[]{:S(2)}) collective-permute-start(f32[2,4,64]{2,1,0:T(4,128)S(1)} %get-tuple-element.31), channel_id=1, source_target_pairs={{0,1},{1,0},{2,3},{3,2},{4,5},{5,4},{6,7},{7,6},{8,9},{9,8},{10,11... | collective-permute-start | bytes 6152 | tf_op jit(solution)/shard_map/ppermute | solution.py:492
  8.6 0.0 collective-permute-done
  8.6 1.0 %collective-permute-done.1 = f32[2,4,64]{2,1,0:T(4,128)S(1)} collective-permute-done((f32[2,4,64]{2,1,0:T(4,128)S(1)}, f32[2,4,64]{2,1,0:T(4,128)S(1)}, u32[]{:S(2)}, u32[]{:S(2)}) %collective-permute-start.1) | collective-permute-done | bytes 2080 | tf_op jit(solution)/shard_map/ppermute | solution.py:492
  9.6 0.1 pad_maximum_fusion.4.here_ref
  9.7 5.2 %collective-permute-start.3 = (f32[2,4,640]{2,1,0:T(4,128)S(1)}, f32[2,4,640]{2,1,0:T(4,128)S(1)}, u32[]{:S(2)}, u32[]{:S(2)}) collective-permute-start(f32[2,4,640]{2,1,0:T(4,128)S(1)} %pad_maximum_fusion.4.here_ref), channel_id=1, source_target_pairs={{0,0},{16,32},{32,16},{48,64},{64,48},{80,96},{96,80},{112,128},{1... | collective-permute-start | bytes 61448 | tf_op jit(solution)/shard_map/ppermute | solution.py:491
  14.9 0.1 collective-permute-start.2
  15.0 1.3 %collective-permute-done.3 = f32[2,4,640]{2,1,0:T(4,128)S(1)} collective-permute-done((f32[2,4,640]{2,1,0:T(4,128)S(1)}, f32[2,4,640]{2,1,0:T(4,128)S(1)}, u32[]{:S(2)}, u32[]{:S(2)}) %collective-permute-start.3) | collective-permute-done | bytes 20512 | tf_op jit(solution)/shard_map/ppermute | solution.py:491
  16.4 0.0 collective-permute-done.2
  16.4 5.8 %shard_map.51 = (f32[256,2048]{1,0:T(8,128)S(1)}, f32[56,128]{1,0:T(8,128)S(1)}, f32[56,128]{1,0:T(8,128)S(1)}, f32[8,128]{1,0:T(8,128)S(1)}) custom-call(f32[2,4,640]{2,1,0:T(4,128)S(1)} %get-tuple-element.29.up_ref, f32[2,4,640]{2,1,0:T(4,128)S(1)} %pad_maximum_fusion.4.here_ref, f32[2,4,640]{2,1,0:T(4,128)S(1)} %get-tuple-element.28.down_ref), custom_call_target="tpu_custom_call" | custom-call | tf_op jit(solution)/shard_map/pallas_call | solution.py:264
  22.2 0.1 collective-permute-start.4
  22.3 1.2 %collective-permute-done.4 = f32[56,128]{1,0:T(8,128)S(1)} collective-permute-done((f32[56,128]{1,0:T(8,128)S(1)}, f32[56,128]{1,0:T(8,128)S(1)}, u32[]{:S(2)}, u32[]{:S(2)}) %collective-permute-start.4) | collective-permute-done | bytes 28704 | tf_op jit(solution)/shard_map/ppermute | solution.py:476
  23.5 3.1 %collective-permute-start.6 = (f32[56,128]{1,0:T(8,128)S(1)}, f32[56,128]{1,0:T(8,128)S(1)}, u32[]{:S(2)}, u32[]{:S(2)}) collective-permute-start(f32[56,128]{1,0:T(8,128)S(1)} %pad_maximum_fusion), channel_id=1, source_target_pairs={{0,64},{16,80},{32,96},{48,112},{64,0},{80,16},{96,32},{112,48},{1... | collective-permute-start | bytes 86024 | tf_op jit(solution)/shard_map/ppermute | solution.py:476
  26.6 2.7 %collective-permute-start.7 = (f32[56,128]{1,0:T(8,128)S(1)}, f32[56,128]{1,0:T(8,128)S(1)}, u32[]{:S(2)}, u32[]{:S(2)}) collective-permute-start(f32[56,128]{1,0:T(8,128)S(1)} %pad_maximum_fusion), channel_id=1, source_target_pairs={{0,96},{16,112},{32,64},{48,80},{64,32},{80,48},{96,0},{112,16},{1... | collective-permute-start | bytes 86024 | tf_op jit(solution)/shard_map/ppermute | solution.py:476
  29.3 0.2 collective-permute-start.5
  29.5 0.0 collective-permute-done.6
  29.5 1.7 %collective-permute-done.7 = f32[56,128]{1,0:T(8,128)S(1)} collective-permute-done((f32[56,128]{1,0:T(8,128)S(1)}, f32[56,128]{1,0:T(8,128)S(1)}, u32[]{:S(2)}, u32[]{:S(2)}) %collective-permute-start.7) | collective-permute-done | bytes 28704 | tf_op jit(solution)/shard_map/ppermute | solution.py:476
  31.1 1.2 %collective-permute-done.5 = f32[56,128]{1,0:T(8,128)S(1)} collective-permute-done((f32[56,128]{1,0:T(8,128)S(1)}, f32[56,128]{1,0:T(8,128)S(1)}, u32[]{:S(2)}, u32[]{:S(2)}) %collective-permute-start.5) | collective-permute-done | bytes 28704 | tf_op jit(solution)/shard_map/ppermute | solution.py:476
  32.4 2.6 %collective-permute-start.8 = (f32[56,128]{1,0:T(8,128)S(1)}, f32[56,128]{1,0:T(8,128)S(1)}, u32[]{:S(2)}, u32[]{:S(2)}) collective-permute-start(f32[56,128]{1,0:T(8,128)S(1)} %pad_maximum_fusion.1), channel_id=1, source_target_pairs={{0,192},{16,208},{32,224},{48,240},{64,128},{80,144},{96,160},{112... | collective-permute-start | bytes 86024 | tf_op jit(solution)/shard_map/ppermute | solution.py:476
  35.0 2.3 %collective-permute-done.8 = f32[56,128]{1,0:T(8,128)S(1)} collective-permute-done((f32[56,128]{1,0:T(8,128)S(1)}, f32[56,128]{1,0:T(8,128)S(1)}, u32[]{:S(2)}, u32[]{:S(2)}) %collective-permute-start.8) | collective-permute-done | bytes 28704 | tf_op jit(solution)/shard_map/ppermute | solution.py:476
  37.4 15.9 %all_to_all.5 = f32[16,56,128]{2,1,0:T(8,128)S(1)} all-to-all(f32[16,56,128]{2,1,0:T(8,128)S(1)} %broadcast_in_dim.18), channel_id=1, replica_groups=mesh['gx'=16,'gy'=16] {'gy'}, dimensions={0} | all-to-all | bytes 917504 | tf_op jit(solution)/shard_map/all_to_all | solution.py:481
  53.4 4.1 %collective-permute-start.9 = (f32[56,128]{1,0:T(8,128)S(1)}, f32[56,128]{1,0:T(8,128)S(1)}, u32[]{:S(2)}, u32[]{:S(2)}) collective-permute-start(f32[56,128]{1,0:T(8,128)S(1)} %pad_maximum_fusion.3.mine_ref), channel_id=1, source_target_pairs={{0,16},{16,0},{32,48},{48,32},{64,80},{80,64},{96,112},{112,96},{1... | collective-permute-start | bytes 86024 | tf_op jit(solution)/shard_map/ppermute | solution.py:476
  57.5 0.9 %collective-permute-done.9.other_ref = f32[56,128]{1,0:T(8,128)S(1)} collective-permute-done((f32[56,128]{1,0:T(8,128)S(1)}, f32[56,128]{1,0:T(8,128)S(1)}, u32[]{:S(2)}, u32[]{:S(2)}) %collective-permute-start.9) | collective-permute-done | bytes 28704 | tf_op jit(solution)/shard_map/ppermute | solution.py:476
  58.3 8.4 %shard_map.52 = (f32[4,32,1024]{2,1,0:T(8,128)}, f32[4,32,1024]{2,1,0:T(8,128)}) custom-call(f32[56,128]{1,0:T(8,128)S(1)} %pad_maximum_fusion.3.mine_ref, f32[56,128]{1,0:T(8,128)S(1)} %collective-permute-done.9.other_ref, f32[8,128]{1,0:T(8,128)S(1)} %get-tuple-element.8.unit_ref, f32[256,2048]{1,0:T(8,128)S(1)} %get-tuple-element.9.fields_ref), custom_call_target="tpu_custom_call" | custom-call | tf_op jit(solution)/shard_map/pallas_call | solution.py:445
  (16 shorter events, 0.2 us)
Async XLA Ops:
  0.6 0.8 %copy-start = (f32[4,32,16]{1,2,0:T(8,128)S(1)}, f32[4,32,16]{1,2,0:T(8,128)}, u32[]{:S(2)}) copy-start(f32[4,32,16]{1,2,0:T(8,128)} %param.3) | copy-start | bytes 24580
  1.4 0.8 %copy-start.1 = (s32[4,32,16]{1,2,0:T(8,128)S(1)}, s32[4,32,16]{1,2,0:T(8,128)}, u32[]{:S(2)}) copy-start(s32[4,32,16]{1,2,0:T(8,128)} %param.4) | copy-start | bytes 24580
  2.2 0.8 %copy-start.2 = (s32[4,32,16]{1,2,0:T(8,128)S(1)}, s32[4,32,16]{1,2,0:T(8,128)}, u32[]{:S(2)}) copy-start(s32[4,32,16]{1,2,0:T(8,128)} %param.5) | copy-start | bytes 24580
  3.3 5.2 %collective-permute-start = (f32[2,4,64]{2,1,0:T(4,128)S(1)}, f32[2,4,64]{2,1,0:T(4,128)S(1)}, u32[]{:S(2)}, u32[]{:S(2)}) collective-permute-start(f32[2,4,64]{2,1,0:T(4,128)S(1)} %get-tuple-element.30), channel_id=1, source_target_pairs={{0,0},{1,2},{2,1},{3,4},{4,3},{5,6},{6,5},{7,8},{8,7},{9,10},{10,9... | collective-permute-start | bytes 6152 | tf_op jit(solution)/shard_map/ppermute | solution.py:491
  4.0 5.6 %collective-permute-start.1 = (f32[2,4,64]{2,1,0:T(4,128)S(1)}, f32[2,4,64]{2,1,0:T(4,128)S(1)}, u32[]{:S(2)}, u32[]{:S(2)}) collective-permute-start(f32[2,4,64]{2,1,0:T(4,128)S(1)} %get-tuple-element.31), channel_id=1, source_target_pairs={{0,1},{1,0},{2,3},{3,2},{4,5},{5,4},{6,7},{7,6},{8,9},{9,8},{10,11... | collective-permute-start | bytes 6152 | tf_op jit(solution)/shard_map/ppermute | solution.py:492
  9.7 6.7 %collective-permute-start.3 = (f32[2,4,640]{2,1,0:T(4,128)S(1)}, f32[2,4,640]{2,1,0:T(4,128)S(1)}, u32[]{:S(2)}, u32[]{:S(2)}) collective-permute-start(f32[2,4,640]{2,1,0:T(4,128)S(1)} %pad_maximum_fusion.4.here_ref), channel_id=1, source_target_pairs={{0,0},{16,32},{32,16},{48,64},{64,48},{80,96},{96,80},{112,128},{1... | collective-permute-start | bytes 61448 | tf_op jit(solution)/shard_map/ppermute | solution.py:491
  14.9 1.5 %collective-permute-start.2 = (f32[2,4,640]{2,1,0:T(4,128)S(1)}, f32[2,4,640]{2,1,0:T(4,128)S(1)}, u32[]{:S(2)}, u32[]{:S(2)}) collective-permute-start(f32[2,4,640]{2,1,0:T(4,128)S(1)} %pad_maximum_fusion.4.here_ref), channel_id=1, source_target_pairs={{0,16},{16,0},{32,48},{48,32},{64,80},{80,64},{96,112},{112,96},{1... | collective-permute-start | bytes 61448 | tf_op jit(solution)/shard_map/ppermute | solution.py:492
  22.2 1.3 %collective-permute-start.4 = (f32[56,128]{1,0:T(8,128)S(1)}, f32[56,128]{1,0:T(8,128)S(1)}, u32[]{:S(2)}, u32[]{:S(2)}) collective-permute-start(f32[56,128]{1,0:T(8,128)S(1)} %get-tuple-element.7), channel_id=1, source_target_pairs={{0,16},{16,0},{32,48},{48,32},{64,80},{80,64},{96,112},{112,96},{1... | collective-permute-start | bytes 86024 | tf_op jit(solution)/shard_map/ppermute | solution.py:476
  23.5 5.9 %collective-permute-start.6 = (f32[56,128]{1,0:T(8,128)S(1)}, f32[56,128]{1,0:T(8,128)S(1)}, u32[]{:S(2)}, u32[]{:S(2)}) collective-permute-start(f32[56,128]{1,0:T(8,128)S(1)} %pad_maximum_fusion), channel_id=1, source_target_pairs={{0,64},{16,80},{32,96},{48,112},{64,0},{80,16},{96,32},{112,48},{1... | collective-permute-start | bytes 86024 | tf_op jit(solution)/shard_map/ppermute | solution.py:476
  26.6 4.5 %collective-permute-start.7 = (f32[56,128]{1,0:T(8,128)S(1)}, f32[56,128]{1,0:T(8,128)S(1)}, u32[]{:S(2)}, u32[]{:S(2)}) collective-permute-start(f32[56,128]{1,0:T(8,128)S(1)} %pad_maximum_fusion), channel_id=1, source_target_pairs={{0,96},{16,112},{32,64},{48,80},{64,32},{80,48},{96,0},{112,16},{1... | collective-permute-start | bytes 86024 | tf_op jit(solution)/shard_map/ppermute | solution.py:476
  29.3 3.1 %collective-permute-start.5 = (f32[56,128]{1,0:T(8,128)S(1)}, f32[56,128]{1,0:T(8,128)S(1)}, u32[]{:S(2)}, u32[]{:S(2)}) collective-permute-start(f32[56,128]{1,0:T(8,128)S(1)} %pad_maximum_fusion), channel_id=1, source_target_pairs={{0,32},{16,48},{32,0},{48,16},{64,96},{80,112},{96,64},{112,80},{1... | collective-permute-start | bytes 86024 | tf_op jit(solution)/shard_map/ppermute | solution.py:476
  32.4 4.9 %collective-permute-start.8 = (f32[56,128]{1,0:T(8,128)S(1)}, f32[56,128]{1,0:T(8,128)S(1)}, u32[]{:S(2)}, u32[]{:S(2)}) collective-permute-start(f32[56,128]{1,0:T(8,128)S(1)} %pad_maximum_fusion.1), channel_id=1, source_target_pairs={{0,192},{16,208},{32,224},{48,240},{64,128},{80,144},{96,160},{112... | collective-permute-start | bytes 86024 | tf_op jit(solution)/shard_map/ppermute | solution.py:476
  53.4 4.9 %collective-permute-start.9 = (f32[56,128]{1,0:T(8,128)S(1)}, f32[56,128]{1,0:T(8,128)S(1)}, u32[]{:S(2)}, u32[]{:S(2)}) collective-permute-start(f32[56,128]{1,0:T(8,128)S(1)} %pad_maximum_fusion.3.mine_ref), channel_id=1, source_target_pairs={{0,16},{16,0},{32,48},{48,32},{64,80},{80,64},{96,112},{112,96},{1... | collective-permute-start | bytes 86024 | tf_op jit(solution)/shard_map/ppermute | solution.py:476

commit v8 on v5

--- a/solution.py
+++ b/solution.py
@@ -447,17 +447,29 @@
     return add_parts(*(parts[i] for i in range(count)))
 
 
-def from_both(first, last, axis):
+def from_both(first, last, axis, outer):
     count = lax.axis_size(axis)
     here = lax.axis_index(axis)
     even = lax.rem(here, 2) == 0
-    outer = [(i, (((i + 1) ^ 1) - 1) % count) for i in range(count)]
-    inner = [(i, i ^ 1) for i in range(count)]
-    one = lax.ppermute(jnp.where(even, first, last), axis, outer)
-    two = lax.ppermute(jnp.where(even, last, first), axis, inner)
     odd = ~even
+    one = lax.ppermute(jnp.where(even, first, last), ("gx", "gy"), outer)
+    two = lax.ppermute(jnp.where(even, last, first), axis, [(i, i ^ 1) for i in range(count)])
     before, after = jnp.where(odd, two, one), jnp.where(odd, one, two)
     return jnp.where(here == 0, 0.0, before), jnp.where(here == count - 1, 0.0, after)
+
+
+def outer_pairs():
+    wide, high = lax.axis_size("gx"), lax.axis_size("gy")
+    along_x, along_y = [], []
+    for i in range(wide):
+        for j in range(high):
+            here = i * high + j
+            along_x.append((here, (((i + 1) ^ 1) - 1) % wide * high + j))
+            if j in (0, high - 1):
+                along_y.append((here, (i ^ 1) * high + j))
+            else:
+                along_y.append((here, i * high + ((j + 1) ^ 1) - 1))
+    return along_x, along_y
 
 
 def shards(diffusivity, labels, obstacles):
@@ -466,18 +478,19 @@
         jnp.transpose(value, (0, 2, 1)) for value in (diffusivity, labels, obstacles)
     )
     conductive = diffusivity * (1 - obstacles).astype(F32)
-    plane = lax.broadcasted_iota(jnp.int32, (2,) + conductive.shape, 0)
-    cells = jnp.where(plane == 0, conductive[None], labels.astype(F32)[None])
-    cells = jnp.transpose(lax.optimization_barrier(cells), (0, 1, 3, 2))
+    cells = jnp.concatenate([conductive, labels.astype(F32)], axis=0)
+    cells = lax.optimization_barrier(cells).reshape(2, rows, NZ, cols)
+    cells = jnp.transpose(cells, (0, 1, 3, 2))
     cells = cells.reshape(2, rows, cols * NZ)
     edge = DEEP * NZ
-    before, after = from_both(cells[:, :, :edge], cells[:, :, -edge:], "gy")
+    along_x, along_y = outer_pairs()
+    before, after = from_both(cells[:, :, :edge], cells[:, :, -edge:], "gy", along_y)
     here = jnp.concatenate([cells, after, before], axis=2)
-    up, down = from_both(here[:, :DEEP], here[:, rows - DEEP:], "gx")
+    up, down = from_both(here[:, :DEEP], here[:, rows - DEEP:], "gx", along_x)
     fields, keep, send, unit = krylov(up, here, down)
     mine = add_parts(keep, *flipped(send, "gx", 1))
     mine = add_parts(mine, *flipped(mine, "gx", 2, 4, 6))
-    mine = add_parts(mine, *flipped(mine, "gx", 8))
+    mine = add_parts(mine, *flipped(mine, "gx", 12))
     mine = sum_of_all(mine, "gy")
     return finish(mine, *flipped(mine, "gx", 1), unit, fields, rows, cols)
 

time: 65.6 us -> 62.6 us (0.954)
  starting transfers between devices: 24.7 us -> 18.9 us
  blocking collectives: 12.8 us -> 16 us
    ppermute x4, starting transfers between devices: 11.5 us -> 7.8 us  [the longest x2 5.17 us: from_both(): one = lax.ppermute(jnp.where(even, first, last), ('gx', 'gy'), outer)]
    all_to_all x1, blocking collectives: 12.8 us -> 16 us  [sum_of_all(): lax.all_to_all(jnp.broadcast_to(value[None], (count,) + value.shape), axi...]
    ppermute x6, starting transfers between devices: 13.3 us -> 11.1 us  [flipped(): lax.ppermute(value, axis, [(i, i ^ mask) for i in range(count)])]
  transfers between devices with their start and end apart: 10 -> 10, of which waited for: 8 -> 9; matrix products, arithmetic and copies ran while one was open for 0% -> 0% of each run, Pallas kernels for 0% -> 0%
where the time goes in v8:
time: 62.6 us; the launch traced here: 62.4 us
  starting transfers between devices  18.9 us (30%)
  blocking collectives  16 us (26%)
  Pallas kernels  14.2 us (23%)
  waiting for transfers between devices  10.2 us (16%)
  other arithmetic  1.88 us (3%)
  between operations  0.89 us (1%)
    all_to_all x1, blocking collectives, sum_of_all(): lax.all_to_all(jnp.broadcast_to(value[None], (count,) + value.shape), axi...  16 us
    ppermute x6, starting transfers between devices, flipped(): lax.ppermute(value, axis, [(i, i ^ mask) for i in range(count)])  11.1 us
    pallas_call x1, Pallas kernels, finish(): pl.pallas_call(finish_kernel, out_shape=(out, out), in_specs=[pl.BlockSpe...  8.43 us
    ppermute x6, waiting for transfers between devices, flipped(): lax.ppermute(value, axis, [(i, i ^ mask) for i in range(count)])  6.92 us
    pallas_call x1, Pallas kernels, krylov(): pl.pallas_call(krylov_kernel, out_shape=(jax.ShapeDtypeStruct(((ITERS + 1...  5.8 us
    ppermute x2, starting transfers between devices, from_both(): one = lax.ppermute(jnp.where(even, first, last), ('gx', 'gy'), outer)  5.17 us
    ppermute x2, starting transfers between devices, from_both(): lax.ppermute(jnp.where(even, last, first), axis, [(i, i ^ 1) for i in ran...  2.63 us
    ppermute x2, waiting for transfers between devices, from_both(): lax.ppermute(jnp.where(even, last, first), axis, [(i, i ^ 1) for i in ran...  2.49 us
  transfers between devices with their start and end apart: 10, of which 9 were waited for; matrix products, arithmetic and copies ran while one was open for 0% of the time, Pallas kernels for 0%

profile of v8, /device:TPU:1, one launch (start us, length us, event | category | flops | bytes accessed | tf_op | source)
XLA Modules:
  0.0 62.4 jit_solution(16143073214266718186)
XLA Ops:
  0.6 0.8 %convert_bitcast_fusion = f32[4,16,32]{2,1,0:T(8,128)S(1)} fusion(s32[4,32,16]{1,2,0:T(8,128)} %param.4), kind=kLoop, calls=%fused_computation.1 | loop fusion | flops 2048 | bytes 16384 | tf_op jit(solution)/shard_map/convert_element_type | solution.py:481
  1.4 0.8 %multiply_bitcast_fusion = f32[4,16,32]{2,1,0:T(8,128)S(1)} fusion(f32[4,32,16]{1,2,0:T(8,128)} %param.3, s32[4,32,16]{1,2,0:T(8,128)} %param.5), kind=kLoop, calls=%fused_computation.2 | loop fusion | flops 6144 | bytes 24576 | tf_op jit(solution)/shard_map/mul | solution.py:480
  2.2 0.1 copy.6
  2.3 0.1 reshape.36
  2.4 0.1 slice_select_fusion.1
  2.5 3.3 %collective-permute-start = (f32[2,4,64]{2,1,0:T(4,128)S(1)}, f32[2,4,64]{2,1,0:T(4,128)S(1)}, u32[]{:S(2)}, u32[]{:S(2)}) collective-permute-start(f32[2,4,64]{2,1,0:T(4,128)S(1)} %get-tuple-element.30), channel_id=1, source_target_pairs={{0,16},{1,2},{2,1},{3,4},{4,3},{5,6},{6,5},{7,8},{8,7},{9,10},{10,... | collective-permute-start | bytes 6152 | tf_op jit(solution)/shard_map/ppermute | solution.py:455
  5.8 0.0 collective-permute-start.1
  5.8 0.8 %collective-permute-done = f32[2,4,64]{2,1,0:T(4,128)S(1)} collective-permute-done((f32[2,4,64]{2,1,0:T(4,128)S(1)}, f32[2,4,64]{2,1,0:T(4,128)S(1)}, u32[]{:S(2)}, u32[]{:S(2)}) %collective-permute-start) | collective-permute-done | bytes 2080 | tf_op jit(solution)/shard_map/ppermute | solution.py:455
  6.6 1.7 %collective-permute-done.1 = f32[2,4,64]{2,1,0:T(4,128)S(1)} collective-permute-done((f32[2,4,64]{2,1,0:T(4,128)S(1)}, f32[2,4,64]{2,1,0:T(4,128)S(1)}, u32[]{:S(2)}, u32[]{:S(2)}) %collective-permute-start.1) | collective-permute-done | bytes 2080 | tf_op jit(solution)/shard_map/ppermute | solution.py:456
  8.2 0.1 pad_maximum_fusion.5.here_ref
  8.3 1.9 %collective-permute-start.3 = (f32[2,4,640]{2,1,0:T(4,128)S(1)}, f32[2,4,640]{2,1,0:T(4,128)S(1)}, u32[]{:S(2)}, u32[]{:S(2)}) collective-permute-start(f32[2,4,640]{2,1,0:T(4,128)S(1)} %pad_maximum_fusion.5.here_ref), channel_id=1, source_target_pairs={{0,240},{1,241},{2,242},{3,243},{4,244},{5,245},{6,246},{7,247},{8... | collective-permute-start | bytes 61448 | tf_op jit(solution)/shard_map/ppermute | solution.py:455
  10.2 2.6 %collective-permute-start.2 = (f32[2,4,640]{2,1,0:T(4,128)S(1)}, f32[2,4,640]{2,1,0:T(4,128)S(1)}, u32[]{:S(2)}, u32[]{:S(2)}) collective-permute-start(f32[2,4,640]{2,1,0:T(4,128)S(1)} %pad_maximum_fusion.5.here_ref), channel_id=1, source_target_pairs={{0,16},{16,0},{32,48},{48,32},{64,80},{80,64},{96,112},{112,96},{1... | collective-permute-start | bytes 61448 | tf_op jit(solution)/shard_map/ppermute | solution.py:456
  12.8 0.0 collective-permute-done.3
  12.8 0.8 %collective-permute-done.2 = f32[2,4,640]{2,1,0:T(4,128)S(1)} collective-permute-done((f32[2,4,640]{2,1,0:T(4,128)S(1)}, f32[2,4,640]{2,1,0:T(4,128)S(1)}, u32[]{:S(2)}, u32[]{:S(2)}) %collective-permute-start.2) | collective-permute-done | bytes 20512 | tf_op jit(solution)/shard_map/ppermute | solution.py:456
  13.7 5.8 %shard_map.50 = (f32[256,2048]{1,0:T(8,128)S(1)}, f32[56,128]{1,0:T(8,128)S(1)}, f32[56,128]{1,0:T(8,128)S(1)}, f32[8,128]{1,0:T(8,128)S(1)}) custom-call(f32[2,4,640]{2,1,0:T(4,128)S(1)} %get-tuple-element.29.up_ref, f32[2,4,640]{2,1,0:T(4,128)S(1)} %pad_maximum_fusion.5.here_ref, f32[2,4,640]{2,1,0:T(4,128)S(1)} %get-tuple-element.28.down_ref), custom_call_target="tpu_custom_call" | custom-call | tf_op jit(solution)/shard_map/pallas_call | solution.py:229
  19.5 0.7 %collective-permute-start.4 = (f32[56,128]{1,0:T(8,128)S(1)}, f32[56,128]{1,0:T(8,128)S(1)}, u32[]{:S(2)}, u32[]{:S(2)}) collective-permute-start(f32[56,128]{1,0:T(8,128)S(1)} %get-tuple-element.7), channel_id=1, source_target_pairs={{0,16},{16,0},{32,48},{48,32},{64,80},{80,64},{96,112},{112,96},{1... | collective-permute-start | bytes 86024 | tf_op jit(solution)/shard_map/ppermute | solution.py:441
  20.2 0.9 %collective-permute-done.4 = f32[56,128]{1,0:T(8,128)S(1)} collective-permute-done((f32[56,128]{1,0:T(8,128)S(1)}, f32[56,128]{1,0:T(8,128)S(1)}, u32[]{:S(2)}, u32[]{:S(2)}) %collective-permute-start.4) | collective-permute-done | bytes 28704 | tf_op jit(solution)/shard_map/ppermute | solution.py:441
  21.1 0.8 %collective-permute-start.6 = (f32[56,128]{1,0:T(8,128)S(1)}, f32[56,128]{1,0:T(8,128)S(1)}, u32[]{:S(2)}, u32[]{:S(2)}) collective-permute-start(f32[56,128]{1,0:T(8,128)S(1)} %pad_maximum_fusion.1), channel_id=1, source_target_pairs={{0,64},{16,80},{32,96},{48,112},{64,0},{80,16},{96,32},{112,48},{1... | collective-permute-start | bytes 86024 | tf_op jit(solution)/shard_map/ppermute | solution.py:441
  21.9 2.7 %collective-permute-start.7 = (f32[56,128]{1,0:T(8,128)S(1)}, f32[56,128]{1,0:T(8,128)S(1)}, u32[]{:S(2)}, u32[]{:S(2)}) collective-permute-start(f32[56,128]{1,0:T(8,128)S(1)} %pad_maximum_fusion.1), channel_id=1, source_target_pairs={{0,96},{16,112},{32,64},{48,80},{64,32},{80,48},{96,0},{112,16},{1... | collective-permute-start | bytes 86024 | tf_op jit(solution)/shard_map/ppermute | solution.py:441
  24.6 0.2 collective-permute-start.5
  24.8 0.1 collective-permute-done.6
  24.8 1.6 %collective-permute-done.7 = f32[56,128]{1,0:T(8,128)S(1)} collective-permute-done((f32[56,128]{1,0:T(8,128)S(1)}, f32[56,128]{1,0:T(8,128)S(1)}, u32[]{:S(2)}, u32[]{:S(2)}) %collective-permute-start.7) | collective-permute-done | bytes 28704 | tf_op jit(solution)/shard_map/ppermute | solution.py:441
  26.4 1.2 %collective-permute-done.5 = f32[56,128]{1,0:T(8,128)S(1)} collective-permute-done((f32[56,128]{1,0:T(8,128)S(1)}, f32[56,128]{1,0:T(8,128)S(1)}, u32[]{:S(2)}, u32[]{:S(2)}) %collective-permute-start.5) | collective-permute-done | bytes 28704 | tf_op jit(solution)/shard_map/ppermute | solution.py:441
  27.7 2.6 %collective-permute-start.8 = (f32[56,128]{1,0:T(8,128)S(1)}, f32[56,128]{1,0:T(8,128)S(1)}, u32[]{:S(2)}, u32[]{:S(2)}) collective-permute-start(f32[56,128]{1,0:T(8,128)S(1)} %pad_maximum_fusion.2), channel_id=1, source_target_pairs={{0,192},{16,208},{32,224},{48,240},{64,128},{80,144},{96,160},{112... | collective-permute-start | bytes 86024 | tf_op jit(solution)/shard_map/ppermute | solution.py:441
  30.4 2.3 %collective-permute-done.8 = f32[56,128]{1,0:T(8,128)S(1)} collective-permute-done((f32[56,128]{1,0:T(8,128)S(1)}, f32[56,128]{1,0:T(8,128)S(1)}, u32[]{:S(2)}, u32[]{:S(2)}) %collective-permute-start.8) | collective-permute-done | bytes 28704 | tf_op jit(solution)/shard_map/ppermute | solution.py:441
  32.7 16.0 %all_to_all.5 = f32[16,56,128]{2,1,0:T(8,128)S(1)} all-to-all(f32[16,56,128]{2,1,0:T(8,128)S(1)} %broadcast_in_dim.18), channel_id=1, replica_groups=mesh['gx'=16,'gy'=16] {'gy'}, dimensions={0} | all-to-all | bytes 917504 | tf_op jit(solution)/shard_map/all_to_all | solution.py:446
  48.9 4.1 %collective-permute-start.9 = (f32[56,128]{1,0:T(8,128)S(1)}, f32[56,128]{1,0:T(8,128)S(1)}, u32[]{:S(2)}, u32[]{:S(2)}) collective-permute-start(f32[56,128]{1,0:T(8,128)S(1)} %pad_maximum_fusion.4.mine_ref), channel_id=1, source_target_pairs={{0,16},{16,0},{32,48},{48,32},{64,80},{80,64},{96,112},{112,96},{1... | collective-permute-start | bytes 86024 | tf_op jit(solution)/shard_map/ppermute | solution.py:441
  52.9 0.9 %collective-permute-done.9.other_ref = f32[56,128]{1,0:T(8,128)S(1)} collective-permute-done((f32[56,128]{1,0:T(8,128)S(1)}, f32[56,128]{1,0:T(8,128)S(1)}, u32[]{:S(2)}, u32[]{:S(2)}) %collective-permute-start.9) | collective-permute-done | bytes 28704 | tf_op jit(solution)/shard_map/ppermute | solution.py:441
  53.8 8.4 %shard_map.51 = (f32[4,32,1024]{2,1,0:T(8,128)}, f32[4,32,1024]{2,1,0:T(8,128)}) custom-call(f32[56,128]{1,0:T(8,128)S(1)} %pad_maximum_fusion.4.mine_ref, f32[56,128]{1,0:T(8,128)S(1)} %collective-permute-done.9.other_ref, f32[8,128]{1,0:T(8,128)S(1)} %get-tuple-element.8.unit_ref, f32[256,2048]{1,0:T(8,128)S(1)} %get-tuple-element.9.fields_ref), custom_call_target="tpu_custom_call" | custom-call | tf_op jit(solution)/shard_map/pallas_call | solution.py:410
  (17 shorter events, 0.2 us)
Async XLA Ops:
  2.5 4.1 %collective-permute-start = (f32[2,4,64]{2,1,0:T(4,128)S(1)}, f32[2,4,64]{2,1,0:T(4,128)S(1)}, u32[]{:S(2)}, u32[]{:S(2)}) collective-permute-start(f32[2,4,64]{2,1,0:T(4,128)S(1)} %get-tuple-element.30), channel_id=1, source_target_pairs={{0,16},{1,2},{2,1},{3,4},{4,3},{5,6},{6,5},{7,8},{8,7},{9,10},{10,... | collective-permute-start | bytes 6152 | tf_op jit(solution)/shard_map/ppermute | solution.py:455
  5.8 2.5 %collective-permute-start.1 = (f32[2,4,64]{2,1,0:T(4,128)S(1)}, f32[2,4,64]{2,1,0:T(4,128)S(1)}, u32[]{:S(2)}, u32[]{:S(2)}) collective-permute-start(f32[2,4,64]{2,1,0:T(4,128)S(1)} %get-tuple-element.31), channel_id=1, source_target_pairs={{0,1},{1,0},{2,3},{3,2},{4,5},{5,4},{6,7},{7,6},{8,9},{9,8},{10,11... | collective-permute-start | bytes 6152 | tf_op jit(solution)/shard_map/ppermute | solution.py:456
  8.3 4.5 %collective-permute-start.3 = (f32[2,4,640]{2,1,0:T(4,128)S(1)}, f32[2,4,640]{2,1,0:T(4,128)S(1)}, u32[]{:S(2)}, u32[]{:S(2)}) collective-permute-start(f32[2,4,640]{2,1,0:T(4,128)S(1)} %pad_maximum_fusion.5.here_ref), channel_id=1, source_target_pairs={{0,240},{1,241},{2,242},{3,243},{4,244},{5,245},{6,246},{7,247},{8... | collective-permute-start | bytes 61448 | tf_op jit(solution)/shard_map/ppermute | solution.py:455
  10.2 3.5 %collective-permute-start.2 = (f32[2,4,640]{2,1,0:T(4,128)S(1)}, f32[2,4,640]{2,1,0:T(4,128)S(1)}, u32[]{:S(2)}, u32[]{:S(2)}) collective-permute-start(f32[2,4,640]{2,1,0:T(4,128)S(1)} %pad_maximum_fusion.5.here_ref), channel_id=1, source_target_pairs={{0,16},{16,0},{32,48},{48,32},{64,80},{80,64},{96,112},{112,96},{1... | collective-permute-start | bytes 61448 | tf_op jit(solution)/shard_map/ppermute | solution.py:456
  19.5 1.6 %collective-permute-start.4 = (f32[56,128]{1,0:T(8,128)S(1)}, f32[56,128]{1,0:T(8,128)S(1)}, u32[]{:S(2)}, u32[]{:S(2)}) collective-permute-start(f32[56,128]{1,0:T(8,128)S(1)} %get-tuple-element.7), channel_id=1, source_target_pairs={{0,16},{16,0},{32,48},{48,32},{64,80},{80,64},{96,112},{112,96},{1... | collective-permute-start | bytes 86024 | tf_op jit(solution)/shard_map/ppermute | solution.py:441
  21.1 3.7 %collective-permute-start.6 = (f32[56,128]{1,0:T(8,128)S(1)}, f32[56,128]{1,0:T(8,128)S(1)}, u32[]{:S(2)}, u32[]{:S(2)}) collective-permute-start(f32[56,128]{1,0:T(8,128)S(1)} %pad_maximum_fusion.1), channel_id=1, source_target_pairs={{0,64},{16,80},{32,96},{48,112},{64,0},{80,16},{96,32},{112,48},{1... | collective-permute-start | bytes 86024 | tf_op jit(solution)/shard_map/ppermute | solution.py:441
  21.9 4.5 %collective-permute-start.7 = (f32[56,128]{1,0:T(8,128)S(1)}, f32[56,128]{1,0:T(8,128)S(1)}, u32[]{:S(2)}, u32[]{:S(2)}) collective-permute-start(f32[56,128]{1,0:T(8,128)S(1)} %pad_maximum_fusion.1), channel_id=1, source_target_pairs={{0,96},{16,112},{32,64},{48,80},{64,32},{80,48},{96,0},{112,16},{1... | collective-permute-start | bytes 86024 | tf_op jit(solution)/shard_map/ppermute | solution.py:441
  24.6 3.1 %collective-permute-start.5 = (f32[56,128]{1,0:T(8,128)S(1)}, f32[56,128]{1,0:T(8,128)S(1)}, u32[]{:S(2)}, u32[]{:S(2)}) collective-permute-start(f32[56,128]{1,0:T(8,128)S(1)} %pad_maximum_fusion.1), channel_id=1, source_target_pairs={{0,32},{16,48},{32,0},{48,16},{64,96},{80,112},{96,64},{112,80},{1... | collective-permute-start | bytes 86024 | tf_op jit(solution)/shard_map/ppermute | solution.py:441
  27.7 4.9 %collective-permute-start.8 = (f32[56,128]{1,0:T(8,128)S(1)}, f32[56,128]{1,0:T(8,128)S(1)}, u32[]{:S(2)}, u32[]{:S(2)}) collective-permute-start(f32[56,128]{1,0:T(8,128)S(1)} %pad_maximum_fusion.2), channel_id=1, source_target_pairs={{0,192},{16,208},{32,224},{48,240},{64,128},{80,144},{96,160},{112... | collective-permute-start | bytes 86024 | tf_op jit(solution)/shard_map/ppermute | solution.py:441
  48.9 4.9 %collective-permute-start.9 = (f32[56,128]{1,0:T(8,128)S(1)}, f32[56,128]{1,0:T(8,128)S(1)}, u32[]{:S(2)}, u32[]{:S(2)}) collective-permute-start(f32[56,128]{1,0:T(8,128)S(1)} %pad_maximum_fusion.4.mine_ref), channel_id=1, source_target_pairs={{0,16},{16,0},{32,48},{48,32},{64,80},{80,64},{96,112},{112,96},{1... | collective-permute-start | bytes 86024 | tf_op jit(solution)/shard_map/ppermute | solution.py:441

commit v9 on v8

--- a/solution.py
+++ b/solution.py
@@ -489,7 +489,7 @@
     up, down = from_both(here[:, :DEEP], here[:, rows - DEEP:], "gx", along_x)
     fields, keep, send, unit = krylov(up, here, down)
     mine = add_parts(keep, *flipped(send, "gx", 1))
-    mine = add_parts(mine, *flipped(mine, "gx", 2, 4, 6))
+    mine = add_parts(mine, *flipped(mine, "gx", 2, 6, 4))
     mine = add_parts(mine, *flipped(mine, "gx", 12))
     mine = sum_of_all(mine, "gy")
     return finish(mine, *flipped(mine, "gx", 1), unit, fields, rows, cols)

time: 62.6 us -> 63.4 us (1.013)
  transfers between devices with their start and end apart: 10 -> 10, of which waited for: 9 -> 8; matrix products, arithmetic and copies ran while one was open for 0% -> 0% of each run, Pallas kernels for 0% -> 0%
where the time goes in v9:
time: 63.4 us; the launch traced here: 63.2 us
  starting transfers between devices  19.2 us (30%)
  blocking collectives  16.1 us (25%)
  Pallas kernels  14.2 us (22%)
  waiting for transfers between devices  10.7 us (17%)
  other arithmetic  1.88 us (3%)
  between operations  0.89 us (1%)
    all_to_all x1, blocking collectives, sum_of_all(): lax.all_to_all(jnp.broadcast_to(value[None], (count,) + value.shape), axi...  16.1 us
    ppermute x6, starting transfers between devices, flipped(): lax.ppermute(value, axis, [(i, i ^ mask) for i in range(count)])  11.4 us
    pallas_call x1, Pallas kernels, finish(): pl.pallas_call(finish_kernel, out_shape=(out, out), in_specs=[pl.BlockSpe...  8.43 us
    ppermute x6, waiting for transfers between devices, flipped(): lax.ppermute(value, axis, [(i, i ^ mask) for i in range(count)])  7.38 us
    pallas_call x1, Pallas kernels, krylov(): pl.pallas_call(krylov_kernel, out_shape=(jax.ShapeDtypeStruct(((ITERS + 1...  5.8 us
    ppermute x2, starting transfers between devices, from_both(): one = lax.ppermute(jnp.where(even, first, last), ('gx', 'gy'), outer)  5.17 us
    ppermute x2, starting transfers between devices, from_both(): lax.ppermute(jnp.where(even, last, first), axis, [(i, i ^ 1) for i in ran...  2.63 us
    ppermute x2, waiting for transfers between devices, from_both(): lax.ppermute(jnp.where(even, last, first), axis, [(i, i ^ 1) for i in ran...  2.49 us
  transfers between devices with their start and end apart: 10, of which 8 were waited for; matrix products, arithmetic and copies ran while one was open for 0% of the time, Pallas kernels for 0%

profile of v9, /device:TPU:1, one launch (start us, length us, event | category | flops | bytes accessed | tf_op | source)
XLA Modules:
  0.0 63.2 jit_solution(12717868601685178079)
XLA Ops:
  0.6 0.8 %convert_bitcast_fusion = f32[4,16,32]{2,1,0:T(8,128)S(1)} fusion(s32[4,32,16]{1,2,0:T(8,128)} %param.4), kind=kLoop, calls=%fused_computation.1 | loop fusion | flops 2048 | bytes 16384 | tf_op jit(solution)/shard_map/convert_element_type | solution.py:481
  1.4 0.8 %multiply_bitcast_fusion = f32[4,16,32]{2,1,0:T(8,128)S(1)} fusion(f32[4,32,16]{1,2,0:T(8,128)} %param.3, s32[4,32,16]{1,2,0:T(8,128)} %param.5), kind=kLoop, calls=%fused_computation.2 | loop fusion | flops 6144 | bytes 24576 | tf_op jit(solution)/shard_map/mul | solution.py:480
  2.2 0.1 copy.6
  2.3 0.1 reshape.36
  2.4 0.1 slice_select_fusion.1
  2.5 3.3 %collective-permute-start = (f32[2,4,64]{2,1,0:T(4,128)S(1)}, f32[2,4,64]{2,1,0:T(4,128)S(1)}, u32[]{:S(2)}, u32[]{:S(2)}) collective-permute-start(f32[2,4,64]{2,1,0:T(4,128)S(1)} %get-tuple-element.30), channel_id=1, source_target_pairs={{0,16},{1,2},{2,1},{3,4},{4,3},{5,6},{6,5},{7,8},{8,7},{9,10},{10,... | collective-permute-start | bytes 6152 | tf_op jit(solution)/shard_map/ppermute | solution.py:455
  5.8 0.0 collective-permute-start.1
  5.8 0.8 %collective-permute-done = f32[2,4,64]{2,1,0:T(4,128)S(1)} collective-permute-done((f32[2,4,64]{2,1,0:T(4,128)S(1)}, f32[2,4,64]{2,1,0:T(4,128)S(1)}, u32[]{:S(2)}, u32[]{:S(2)}) %collective-permute-start) | collective-permute-done | bytes 2080 | tf_op jit(solution)/shard_map/ppermute | solution.py:455
  6.6 1.7 %collective-permute-done.1 = f32[2,4,64]{2,1,0:T(4,128)S(1)} collective-permute-done((f32[2,4,64]{2,1,0:T(4,128)S(1)}, f32[2,4,64]{2,1,0:T(4,128)S(1)}, u32[]{:S(2)}, u32[]{:S(2)}) %collective-permute-start.1) | collective-permute-done | bytes 2080 | tf_op jit(solution)/shard_map/ppermute | solution.py:456
  8.2 0.1 pad_maximum_fusion.5.here_ref
  8.3 1.9 %collective-permute-start.3 = (f32[2,4,640]{2,1,0:T(4,128)S(1)}, f32[2,4,640]{2,1,0:T(4,128)S(1)}, u32[]{:S(2)}, u32[]{:S(2)}) collective-permute-start(f32[2,4,640]{2,1,0:T(4,128)S(1)} %pad_maximum_fusion.5.here_ref), channel_id=1, source_target_pairs={{0,240},{1,241},{2,242},{3,243},{4,244},{5,245},{6,246},{7,247},{8... | collective-permute-start | bytes 61448 | tf_op jit(solution)/shard_map/ppermute | solution.py:455
  10.2 2.6 %collective-permute-start.2 = (f32[2,4,640]{2,1,0:T(4,128)S(1)}, f32[2,4,640]{2,1,0:T(4,128)S(1)}, u32[]{:S(2)}, u32[]{:S(2)}) collective-permute-start(f32[2,4,640]{2,1,0:T(4,128)S(1)} %pad_maximum_fusion.5.here_ref), channel_id=1, source_target_pairs={{0,16},{16,0},{32,48},{48,32},{64,80},{80,64},{96,112},{112,96},{1... | collective-permute-start | bytes 61448 | tf_op jit(solution)/shard_map/ppermute | solution.py:456
  12.8 0.0 collective-permute-done.3
  12.8 0.8 %collective-permute-done.2 = f32[2,4,640]{2,1,0:T(4,128)S(1)} collective-permute-done((f32[2,4,640]{2,1,0:T(4,128)S(1)}, f32[2,4,640]{2,1,0:T(4,128)S(1)}, u32[]{:S(2)}, u32[]{:S(2)}) %collective-permute-start.2) | collective-permute-done | bytes 20512 | tf_op jit(solution)/shard_map/ppermute | solution.py:456
  13.7 5.8 %shard_map.50 = (f32[256,2048]{1,0:T(8,128)S(1)}, f32[56,128]{1,0:T(8,128)S(1)}, f32[56,128]{1,0:T(8,128)S(1)}, f32[8,128]{1,0:T(8,128)S(1)}) custom-call(f32[2,4,640]{2,1,0:T(4,128)S(1)} %get-tuple-element.29.up_ref, f32[2,4,640]{2,1,0:T(4,128)S(1)} %pad_maximum_fusion.5.here_ref, f32[2,4,640]{2,1,0:T(4,128)S(1)} %get-tuple-element.28.down_ref), custom_call_target="tpu_custom_call" | custom-call | tf_op jit(solution)/shard_map/pallas_call | solution.py:229
  19.5 0.7 %collective-permute-start.4 = (f32[56,128]{1,0:T(8,128)S(1)}, f32[56,128]{1,0:T(8,128)S(1)}, u32[]{:S(2)}, u32[]{:S(2)}) collective-permute-start(f32[56,128]{1,0:T(8,128)S(1)} %get-tuple-element.7), channel_id=1, source_target_pairs={{0,16},{16,0},{32,48},{48,32},{64,80},{80,64},{96,112},{112,96},{1... | collective-permute-start | bytes 86024 | tf_op jit(solution)/shard_map/ppermute | solution.py:441
  20.2 0.9 %collective-permute-done.4 = f32[56,128]{1,0:T(8,128)S(1)} collective-permute-done((f32[56,128]{1,0:T(8,128)S(1)}, f32[56,128]{1,0:T(8,128)S(1)}, u32[]{:S(2)}, u32[]{:S(2)}) %collective-permute-start.4) | collective-permute-done | bytes 28704 | tf_op jit(solution)/shard_map/ppermute | solution.py:441
  21.1 3.3 %collective-permute-start.6 = (f32[56,128]{1,0:T(8,128)S(1)}, f32[56,128]{1,0:T(8,128)S(1)}, u32[]{:S(2)}, u32[]{:S(2)}) collective-permute-start(f32[56,128]{1,0:T(8,128)S(1)} %pad_maximum_fusion.1), channel_id=1, source_target_pairs={{0,96},{16,112},{32,64},{48,80},{64,32},{80,48},{96,0},{112,16},{1... | collective-permute-start | bytes 86024 | tf_op jit(solution)/shard_map/ppermute | solution.py:441
  24.5 0.0 collective-permute-start.7
  24.5 0.4 collective-permute-start.5
  24.9 0.9 %collective-permute-done.6 = f32[56,128]{1,0:T(8,128)S(1)} collective-permute-done((f32[56,128]{1,0:T(8,128)S(1)}, f32[56,128]{1,0:T(8,128)S(1)}, u32[]{:S(2)}, u32[]{:S(2)}) %collective-permute-start.6) | collective-permute-done | bytes 28704 | tf_op jit(solution)/shard_map/ppermute | solution.py:441
  25.7 2.4 %collective-permute-done.7 = f32[56,128]{1,0:T(8,128)S(1)} collective-permute-done((f32[56,128]{1,0:T(8,128)S(1)}, f32[56,128]{1,0:T(8,128)S(1)}, u32[]{:S(2)}, u32[]{:S(2)}) %collective-permute-start.7) | collective-permute-done | bytes 28704 | tf_op jit(solution)/shard_map/ppermute | solution.py:441
  28.1 0.0 collective-permute-done.5
  28.2 2.5 %collective-permute-start.8 = (f32[56,128]{1,0:T(8,128)S(1)}, f32[56,128]{1,0:T(8,128)S(1)}, u32[]{:S(2)}, u32[]{:S(2)}) collective-permute-start(f32[56,128]{1,0:T(8,128)S(1)} %pad_maximum_fusion.2), channel_id=1, source_target_pairs={{0,192},{16,208},{32,224},{48,240},{64,128},{80,144},{96,160},{112... | collective-permute-start | bytes 86024 | tf_op jit(solution)/shard_map/ppermute | solution.py:441
  30.7 2.4 %collective-permute-done.8 = f32[56,128]{1,0:T(8,128)S(1)} collective-permute-done((f32[56,128]{1,0:T(8,128)S(1)}, f32[56,128]{1,0:T(8,128)S(1)}, u32[]{:S(2)}, u32[]{:S(2)}) %collective-permute-start.8) | collective-permute-done | bytes 28704 | tf_op jit(solution)/shard_map/ppermute | solution.py:441
  33.2 16.1 %all_to_all.5 = f32[16,56,128]{2,1,0:T(8,128)S(1)} all-to-all(f32[16,56,128]{2,1,0:T(8,128)S(1)} %broadcast_in_dim.18), channel_id=1, replica_groups=mesh['gx'=16,'gy'=16] {'gy'}, dimensions={0} | all-to-all | bytes 917504 | tf_op jit(solution)/shard_map/all_to_all | solution.py:446
  49.3 4.4 %collective-permute-start.9 = (f32[56,128]{1,0:T(8,128)S(1)}, f32[56,128]{1,0:T(8,128)S(1)}, u32[]{:S(2)}, u32[]{:S(2)}) collective-permute-start(f32[56,128]{1,0:T(8,128)S(1)} %pad_maximum_fusion.4.mine_ref), channel_id=1, source_target_pairs={{0,16},{16,0},{32,48},{48,32},{64,80},{80,64},{96,112},{112,96},{1... | collective-permute-start | bytes 86024 | tf_op jit(solution)/shard_map/ppermute | solution.py:441
  53.7 0.9 %collective-permute-done.9.other_ref = f32[56,128]{1,0:T(8,128)S(1)} collective-permute-done((f32[56,128]{1,0:T(8,128)S(1)}, f32[56,128]{1,0:T(8,128)S(1)}, u32[]{:S(2)}, u32[]{:S(2)}) %collective-permute-start.9) | collective-permute-done | bytes 28704 | tf_op jit(solution)/shard_map/ppermute | solution.py:441
  54.6 8.4 %shard_map.51 = (f32[4,32,1024]{2,1,0:T(8,128)}, f32[4,32,1024]{2,1,0:T(8,128)}) custom-call(f32[56,128]{1,0:T(8,128)S(1)} %pad_maximum_fusion.4.mine_ref, f32[56,128]{1,0:T(8,128)S(1)} %collective-permute-done.9.other_ref, f32[8,128]{1,0:T(8,128)S(1)} %get-tuple-element.8.unit_ref, f32[256,2048]{1,0:T(8,128)S(1)} %get-tuple-element.9.fields_ref), custom_call_target="tpu_custom_call" | custom-call | tf_op jit(solution)/shard_map/pallas_call | solution.py:410
  (17 shorter events, 0.2 us)
Async XLA Ops:
  2.5 4.1 %collective-permute-start = (f32[2,4,64]{2,1,0:T(4,128)S(1)}, f32[2,4,64]{2,1,0:T(4,128)S(1)}, u32[]{:S(2)}, u32[]{:S(2)}) collective-permute-start(f32[2,4,64]{2,1,0:T(4,128)S(1)} %get-tuple-element.30), channel_id=1, source_target_pairs={{0,16},{1,2},{2,1},{3,4},{4,3},{5,6},{6,5},{7,8},{8,7},{9,10},{10,... | collective-permute-start | bytes 6152 | tf_op jit(solution)/shard_map/ppermute | solution.py:455
  5.8 2.5 %collective-permute-start.1 = (f32[2,4,64]{2,1,0:T(4,128)S(1)}, f32[2,4,64]{2,1,0:T(4,128)S(1)}, u32[]{:S(2)}, u32[]{:S(2)}) collective-permute-start(f32[2,4,64]{2,1,0:T(4,128)S(1)} %get-tuple-element.31), channel_id=1, source_target_pairs={{0,1},{1,0},{2,3},{3,2},{4,5},{5,4},{6,7},{7,6},{8,9},{9,8},{10,11... | collective-permute-start | bytes 6152 | tf_op jit(solution)/shard_map/ppermute | solution.py:456
  8.3 4.5 %collective-permute-start.3 = (f32[2,4,640]{2,1,0:T(4,128)S(1)}, f32[2,4,640]{2,1,0:T(4,128)S(1)}, u32[]{:S(2)}, u32[]{:S(2)}) collective-permute-start(f32[2,4,640]{2,1,0:T(4,128)S(1)} %pad_maximum_fusion.5.here_ref), channel_id=1, source_target_pairs={{0,240},{1,241},{2,242},{3,243},{4,244},{5,245},{6,246},{7,247},{8... | collective-permute-start | bytes 61448 | tf_op jit(solution)/shard_map/ppermute | solution.py:455
  10.2 3.5 %collective-permute-start.2 = (f32[2,4,640]{2,1,0:T(4,128)S(1)}, f32[2,4,640]{2,1,0:T(4,128)S(1)}, u32[]{:S(2)}, u32[]{:S(2)}) collective-permute-start(f32[2,4,640]{2,1,0:T(4,128)S(1)} %pad_maximum_fusion.5.here_ref), channel_id=1, source_target_pairs={{0,16},{16,0},{32,48},{48,32},{64,80},{80,64},{96,112},{112,96},{1... | collective-permute-start | bytes 61448 | tf_op jit(solution)/shard_map/ppermute | solution.py:456
  19.5 1.6 %collective-permute-start.4 = (f32[56,128]{1,0:T(8,128)S(1)}, f32[56,128]{1,0:T(8,128)S(1)}, u32[]{:S(2)}, u32[]{:S(2)}) collective-permute-start(f32[56,128]{1,0:T(8,128)S(1)} %get-tuple-element.7), channel_id=1, source_target_pairs={{0,16},{16,0},{32,48},{48,32},{64,80},{80,64},{96,112},{112,96},{1... | collective-permute-start | bytes 86024 | tf_op jit(solution)/shard_map/ppermute | solution.py:441
  21.1 4.6 %collective-permute-start.6 = (f32[56,128]{1,0:T(8,128)S(1)}, f32[56,128]{1,0:T(8,128)S(1)}, u32[]{:S(2)}, u32[]{:S(2)}) collective-permute-start(f32[56,128]{1,0:T(8,128)S(1)} %pad_maximum_fusion.1), channel_id=1, source_target_pairs={{0,96},{16,112},{32,64},{48,80},{64,32},{80,48},{96,0},{112,16},{1... | collective-permute-start | bytes 86024 | tf_op jit(solution)/shard_map/ppermute | solution.py:441
  24.5 3.6 %collective-permute-start.7 = (f32[56,128]{1,0:T(8,128)S(1)}, f32[56,128]{1,0:T(8,128)S(1)}, u32[]{:S(2)}, u32[]{:S(2)}) collective-permute-start(f32[56,128]{1,0:T(8,128)S(1)} %pad_maximum_fusion.1), channel_id=1, source_target_pairs={{0,64},{16,80},{32,96},{48,112},{64,0},{80,16},{96,32},{112,48},{1... | collective-permute-start | bytes 86024 | tf_op jit(solution)/shard_map/ppermute | solution.py:441
  24.5 3.6 %collective-permute-start.5 = (f32[56,128]{1,0:T(8,128)S(1)}, f32[56,128]{1,0:T(8,128)S(1)}, u32[]{:S(2)}, u32[]{:S(2)}) collective-permute-start(f32[56,128]{1,0:T(8,128)S(1)} %pad_maximum_fusion.1), channel_id=1, source_target_pairs={{0,32},{16,48},{32,0},{48,16},{64,96},{80,112},{96,64},{112,80},{1... | collective-permute-start | bytes 86024 | tf_op jit(solution)/shard_map/ppermute | solution.py:441
  28.2 4.9 %collective-permute-start.8 = (f32[56,128]{1,0:T(8,128)S(1)}, f32[56,128]{1,0:T(8,128)S(1)}, u32[]{:S(2)}, u32[]{:S(2)}) collective-permute-start(f32[56,128]{1,0:T(8,128)S(1)} %pad_maximum_fusion.2), channel_id=1, source_target_pairs={{0,192},{16,208},{32,224},{48,240},{64,128},{80,144},{96,160},{112... | collective-permute-start | bytes 86024 | tf_op jit(solution)/shard_map/ppermute | solution.py:441
  49.3 5.3 %collective-permute-start.9 = (f32[56,128]{1,0:T(8,128)S(1)}, f32[56,128]{1,0:T(8,128)S(1)}, u32[]{:S(2)}, u32[]{:S(2)}) collective-permute-start(f32[56,128]{1,0:T(8,128)S(1)} %pad_maximum_fusion.4.mine_ref), channel_id=1, source_target_pairs={{0,16},{16,0},{32,48},{48,32},{64,80},{80,64},{96,112},{112,96},{1... | collective-permute-start | bytes 86024 | tf_op jit(solution)/shard_map/ppermute | solution.py:441

commit v10 on v9

--- a/solution.py
+++ b/solution.py
@@ -441,6 +441,19 @@
     return [lax.ppermute(value, axis, [(i, i ^ mask) for i in range(count)]) for mask in masks]
 
 
+def across(value, *steps):
+    chips = lax.axis_size("gx") // 2
+
+    def partner(i, step):
+        chip, core = i // 2, i % 2
+        return (chip + (step if chip % 2 == 0 else -step)) % chips * 2 + core
+
+    return [
+        lax.ppermute(value, "gx", [(i, partner(i, step)) for i in range(2 * chips)])
+        for step in steps
+    ]
+
+
 def sum_of_all(value, axis):
     count = lax.axis_size(axis)
     parts = lax.all_to_all(jnp.broadcast_to(value[None], (count,) + value.shape), axis, 0, 0)
@@ -489,8 +502,8 @@
     up, down = from_both(here[:, :DEEP], here[:, rows - DEEP:], "gx", along_x)
     fields, keep, send, unit = krylov(up, here, down)
     mine = add_parts(keep, *flipped(send, "gx", 1))
-    mine = add_parts(mine, *flipped(mine, "gx", 2, 6, 4))
-    mine = add_parts(mine, *flipped(mine, "gx", 12))
+    mine = add_parts(mine, *across(mine, 1))
+    mine = add_parts(mine, *across(mine, 3, -1, -3))
     mine = sum_of_all(mine, "gy")
     return finish(mine, *flipped(mine, "gx", 1), unit, fields, rows, cols)
 

time: 63.4 us -> 64.2 us (1.013)
  starting transfers between devices: 19.2 us -> 20.2 us
    ppermute x0 -> x4, starting transfers between devices: none -> 7.07 us  [across(): lax.ppermute(value, 'gx', [(i, partner(i, step)) for i in range(2 * chips)])]
    ppermute x6 -> x2, starting transfers between devices: 11.4 us -> 5.35 us  [flipped(): lax.ppermute(value, axis, [(i, i ^ mask) for i in range(count)])]
    ppermute x6 -> x2, waiting for transfers between devices: 7.38 us -> 1.71 us  [flipped(): lax.ppermute(value, axis, [(i, i ^ mask) for i in range(count)])]
    ppermute x0 -> x4, waiting for transfers between devices: none -> 5.13 us  [across(): lax.ppermute(value, 'gx', [(i, partner(i, step)) for i in range(2 * chips)])]
where the time goes in v10:
time: 64.2 us; the launch traced here: 63.9 us
  starting transfers between devices  20.2 us (31%)
  blocking collectives  16.3 us (25%)
  Pallas kernels  14.2 us (22%)
  waiting for transfers between devices  10.1 us (16%)
  other arithmetic  1.88 us (3%)
  between operations  0.89 us (1%)
    all_to_all x1, blocking collectives, sum_of_all(): lax.all_to_all(jnp.broadcast_to(value[None], (count,) + value.shape), axi...  16.3 us
    pallas_call x1, Pallas kernels, finish(): pl.pallas_call(finish_kernel, out_shape=(out, out), in_specs=[pl.BlockSpe...  8.43 us
    ppermute x4, starting transfers between devices, across(): lax.ppermute(value, 'gx', [(i, partner(i, step)) for i in range(2 * chips)])  7.07 us
    pallas_call x1, Pallas kernels, krylov(): pl.pallas_call(krylov_kernel, out_shape=(jax.ShapeDtypeStruct(((ITERS + 1...  5.8 us
    ppermute x2, starting transfers between devices, flipped(): lax.ppermute(value, axis, [(i, i ^ mask) for i in range(count)])  5.35 us
    ppermute x2, starting transfers between devices, from_both(): one = lax.ppermute(jnp.where(even, first, last), ('gx', 'gy'), outer)  5.17 us
    ppermute x4, waiting for transfers between devices, across(): lax.ppermute(value, 'gx', [(i, partner(i, step)) for i in range(2 * chips)])  5.13 us
    ppermute x2, starting transfers between devices, from_both(): lax.ppermute(jnp.where(even, last, first), axis, [(i, i ^ 1) for i in ran...  2.63 us
  transfers between devices with their start and end apart: 10, of which 8 were waited for; matrix products, arithmetic and copies ran while one was open for 0% of the time, Pallas kernels for 0%

profile of v10, /device:TPU:1, one launch (start us, length us, event | category | flops | bytes accessed | tf_op | source)
XLA Modules:
  0.0 63.9 jit_solution(12329240393822593955)
XLA Ops:
  0.6 0.8 %convert_bitcast_fusion = f32[4,16,32]{2,1,0:T(8,128)S(1)} fusion(s32[4,32,16]{1,2,0:T(8,128)} %param.4), kind=kLoop, calls=%fused_computation.1 | loop fusion | flops 2048 | bytes 16384 | tf_op jit(solution)/shard_map/convert_element_type | solution.py:494
  1.4 0.8 %multiply_bitcast_fusion = f32[4,16,32]{2,1,0:T(8,128)S(1)} fusion(f32[4,32,16]{1,2,0:T(8,128)} %param.3, s32[4,32,16]{1,2,0:T(8,128)} %param.5), kind=kLoop, calls=%fused_computation.2 | loop fusion | flops 6144 | bytes 24576 | tf_op jit(solution)/shard_map/mul | solution.py:493
  2.2 0.1 copy.6
  2.3 0.1 reshape.36
  2.4 0.1 slice_select_fusion.1
  2.5 3.3 %collective-permute-start = (f32[2,4,64]{2,1,0:T(4,128)S(1)}, f32[2,4,64]{2,1,0:T(4,128)S(1)}, u32[]{:S(2)}, u32[]{:S(2)}) collective-permute-start(f32[2,4,64]{2,1,0:T(4,128)S(1)} %get-tuple-element.30), channel_id=1, source_target_pairs={{0,16},{1,2},{2,1},{3,4},{4,3},{5,6},{6,5},{7,8},{8,7},{9,10},{10,... | collective-permute-start | bytes 6152 | tf_op jit(solution)/shard_map/ppermute | solution.py:468
  5.8 0.0 collective-permute-start.1
  5.8 0.8 %collective-permute-done = f32[2,4,64]{2,1,0:T(4,128)S(1)} collective-permute-done((f32[2,4,64]{2,1,0:T(4,128)S(1)}, f32[2,4,64]{2,1,0:T(4,128)S(1)}, u32[]{:S(2)}, u32[]{:S(2)}) %collective-permute-start) | collective-permute-done | bytes 2080 | tf_op jit(solution)/shard_map/ppermute | solution.py:468
  6.6 1.7 %collective-permute-done.1 = f32[2,4,64]{2,1,0:T(4,128)S(1)} collective-permute-done((f32[2,4,64]{2,1,0:T(4,128)S(1)}, f32[2,4,64]{2,1,0:T(4,128)S(1)}, u32[]{:S(2)}, u32[]{:S(2)}) %collective-permute-start.1) | collective-permute-done | bytes 2080 | tf_op jit(solution)/shard_map/ppermute | solution.py:469
  8.2 0.1 pad_maximum_fusion.5.here_ref
  8.3 1.9 %collective-permute-start.3 = (f32[2,4,640]{2,1,0:T(4,128)S(1)}, f32[2,4,640]{2,1,0:T(4,128)S(1)}, u32[]{:S(2)}, u32[]{:S(2)}) collective-permute-start(f32[2,4,640]{2,1,0:T(4,128)S(1)} %pad_maximum_fusion.5.here_ref), channel_id=1, source_target_pairs={{0,240},{1,241},{2,242},{3,243},{4,244},{5,245},{6,246},{7,247},{8... | collective-permute-start | bytes 61448 | tf_op jit(solution)/shard_map/ppermute | solution.py:468
  10.2 2.6 %collective-permute-start.2 = (f32[2,4,640]{2,1,0:T(4,128)S(1)}, f32[2,4,640]{2,1,0:T(4,128)S(1)}, u32[]{:S(2)}, u32[]{:S(2)}) collective-permute-start(f32[2,4,640]{2,1,0:T(4,128)S(1)} %pad_maximum_fusion.5.here_ref), channel_id=1, source_target_pairs={{0,16},{16,0},{32,48},{48,32},{64,80},{80,64},{96,112},{112,96},{1... | collective-permute-start | bytes 61448 | tf_op jit(solution)/shard_map/ppermute | solution.py:469
  12.8 0.0 collective-permute-done.3
  12.8 0.8 %collective-permute-done.2 = f32[2,4,640]{2,1,0:T(4,128)S(1)} collective-permute-done((f32[2,4,640]{2,1,0:T(4,128)S(1)}, f32[2,4,640]{2,1,0:T(4,128)S(1)}, u32[]{:S(2)}, u32[]{:S(2)}) %collective-permute-start.2) | collective-permute-done | bytes 20512 | tf_op jit(solution)/shard_map/ppermute | solution.py:469
  13.7 5.8 %shard_map.50 = (f32[256,2048]{1,0:T(8,128)S(1)}, f32[56,128]{1,0:T(8,128)S(1)}, f32[56,128]{1,0:T(8,128)S(1)}, f32[8,128]{1,0:T(8,128)S(1)}) custom-call(f32[2,4,640]{2,1,0:T(4,128)S(1)} %get-tuple-element.29.up_ref, f32[2,4,640]{2,1,0:T(4,128)S(1)} %pad_maximum_fusion.5.here_ref, f32[2,4,640]{2,1,0:T(4,128)S(1)} %get-tuple-element.28.down_ref), custom_call_target="tpu_custom_call" | custom-call | tf_op jit(solution)/shard_map/pallas_call | solution.py:229
  19.5 0.7 %collective-permute-start.4 = (f32[56,128]{1,0:T(8,128)S(1)}, f32[56,128]{1,0:T(8,128)S(1)}, u32[]{:S(2)}, u32[]{:S(2)}) collective-permute-start(f32[56,128]{1,0:T(8,128)S(1)} %get-tuple-element.7), channel_id=1, source_target_pairs={{0,16},{16,0},{32,48},{48,32},{64,80},{80,64},{96,112},{112,96},{1... | collective-permute-start | bytes 86024 | tf_op jit(solution)/shard_map/ppermute | solution.py:441
  20.2 0.9 %collective-permute-done.4 = f32[56,128]{1,0:T(8,128)S(1)} collective-permute-done((f32[56,128]{1,0:T(8,128)S(1)}, f32[56,128]{1,0:T(8,128)S(1)}, u32[]{:S(2)}, u32[]{:S(2)}) %collective-permute-start.4) | collective-permute-done | bytes 28704 | tf_op jit(solution)/shard_map/ppermute | solution.py:441
  21.1 0.1 collective-permute-start.5
  21.2 2.7 %collective-permute-done.5 = f32[56,128]{1,0:T(8,128)S(1)} collective-permute-done((f32[56,128]{1,0:T(8,128)S(1)}, f32[56,128]{1,0:T(8,128)S(1)}, u32[]{:S(2)}, u32[]{:S(2)}) %collective-permute-start.5) | collective-permute-done | bytes 28704 | tf_op jit(solution)/shard_map/ppermute | solution.py:452
  24.0 3.2 %collective-permute-start.7 = (f32[56,128]{1,0:T(8,128)S(1)}, f32[56,128]{1,0:T(8,128)S(1)}, u32[]{:S(2)}, u32[]{:S(2)}) collective-permute-start(f32[56,128]{1,0:T(8,128)S(1)} %pad_maximum_fusion.2), channel_id=1, source_target_pairs={{0,224},{16,240},{32,64},{48,80},{64,32},{80,48},{96,128},{112,144... | collective-permute-start | bytes 86024 | tf_op jit(solution)/shard_map/ppermute | solution.py:452
  27.2 1.6 %collective-permute-start.8 = (f32[56,128]{1,0:T(8,128)S(1)}, f32[56,128]{1,0:T(8,128)S(1)}, u32[]{:S(2)}, u32[]{:S(2)}) collective-permute-start(f32[56,128]{1,0:T(8,128)S(1)} %pad_maximum_fusion.2), channel_id=1, source_target_pairs={{0,160},{16,176},{32,128},{48,144},{64,224},{80,240},{96,192},{112... | collective-permute-start | bytes 86024 | tf_op jit(solution)/shard_map/ppermute | solution.py:452
  28.9 2.1 %collective-permute-start.6 = (f32[56,128]{1,0:T(8,128)S(1)}, f32[56,128]{1,0:T(8,128)S(1)}, u32[]{:S(2)}, u32[]{:S(2)}) collective-permute-start(f32[56,128]{1,0:T(8,128)S(1)} %pad_maximum_fusion.2), channel_id=1, source_target_pairs={{0,96},{16,112},{32,192},{48,208},{64,160},{80,176},{96,0},{112,16... | collective-permute-start | bytes 86024 | tf_op jit(solution)/shard_map/ppermute | solution.py:452
  31.0 0.0 collective-permute-done.7
  31.0 2.2 %collective-permute-done.8 = f32[56,128]{1,0:T(8,128)S(1)} collective-permute-done((f32[56,128]{1,0:T(8,128)S(1)}, f32[56,128]{1,0:T(8,128)S(1)}, u32[]{:S(2)}, u32[]{:S(2)}) %collective-permute-start.8) | collective-permute-done | bytes 28704 | tf_op jit(solution)/shard_map/ppermute | solution.py:452
  33.2 0.2 collective-permute-done.6
  33.5 16.3 %all_to_all.5 = f32[16,56,128]{2,1,0:T(8,128)S(1)} all-to-all(f32[16,56,128]{2,1,0:T(8,128)S(1)} %broadcast_in_dim.18), channel_id=1, replica_groups=mesh['gx'=16,'gy'=16] {'gy'}, dimensions={0} | all-to-all | bytes 917504 | tf_op jit(solution)/shard_map/all_to_all | solution.py:459
  49.9 4.6 %collective-permute-start.9 = (f32[56,128]{1,0:T(8,128)S(1)}, f32[56,128]{1,0:T(8,128)S(1)}, u32[]{:S(2)}, u32[]{:S(2)}) collective-permute-start(f32[56,128]{1,0:T(8,128)S(1)} %pad_maximum_fusion.4.mine_ref), channel_id=1, source_target_pairs={{0,16},{16,0},{32,48},{48,32},{64,80},{80,64},{96,112},{112,96},{1... | collective-permute-start | bytes 86024 | tf_op jit(solution)/shard_map/ppermute | solution.py:441
  54.5 0.9 %collective-permute-done.9.other_ref = f32[56,128]{1,0:T(8,128)S(1)} collective-permute-done((f32[56,128]{1,0:T(8,128)S(1)}, f32[56,128]{1,0:T(8,128)S(1)}, u32[]{:S(2)}, u32[]{:S(2)}) %collective-permute-start.9) | collective-permute-done | bytes 28704 | tf_op jit(solution)/shard_map/ppermute | solution.py:441
  55.4 8.4 %shard_map.51 = (f32[4,32,1024]{2,1,0:T(8,128)}, f32[4,32,1024]{2,1,0:T(8,128)}) custom-call(f32[56,128]{1,0:T(8,128)S(1)} %pad_maximum_fusion.4.mine_ref, f32[56,128]{1,0:T(8,128)S(1)} %collective-permute-done.9.other_ref, f32[8,128]{1,0:T(8,128)S(1)} %get-tuple-element.8.unit_ref, f32[256,2048]{1,0:T(8,128)S(1)} %get-tuple-element.9.fields_ref), custom_call_target="tpu_custom_call" | custom-call | tf_op jit(solution)/shard_map/pallas_call | solution.py:410
  (17 shorter events, 0.2 us)
Async XLA Ops:
  2.5 4.1 %collective-permute-start = (f32[2,4,64]{2,1,0:T(4,128)S(1)}, f32[2,4,64]{2,1,0:T(4,128)S(1)}, u32[]{:S(2)}, u32[]{:S(2)}) collective-permute-start(f32[2,4,64]{2,1,0:T(4,128)S(1)} %get-tuple-element.30), channel_id=1, source_target_pairs={{0,16},{1,2},{2,1},{3,4},{4,3},{5,6},{6,5},{7,8},{8,7},{9,10},{10,... | collective-permute-start | bytes 6152 | tf_op jit(solution)/shard_map/ppermute | solution.py:468
  5.8 2.5 %collective-permute-start.1 = (f32[2,4,64]{2,1,0:T(4,128)S(1)}, f32[2,4,64]{2,1,0:T(4,128)S(1)}, u32[]{:S(2)}, u32[]{:S(2)}) collective-permute-start(f32[2,4,64]{2,1,0:T(4,128)S(1)} %get-tuple-element.31), channel_id=1, source_target_pairs={{0,1},{1,0},{2,3},{3,2},{4,5},{5,4},{6,7},{7,6},{8,9},{9,8},{10,11... | collective-permute-start | bytes 6152 | tf_op jit(solution)/shard_map/ppermute | solution.py:469
  8.3 4.5 %collective-permute-start.3 = (f32[2,4,640]{2,1,0:T(4,128)S(1)}, f32[2,4,640]{2,1,0:T(4,128)S(1)}, u32[]{:S(2)}, u32[]{:S(2)}) collective-permute-start(f32[2,4,640]{2,1,0:T(4,128)S(1)} %pad_maximum_fusion.5.here_ref), channel_id=1, source_target_pairs={{0,240},{1,241},{2,242},{3,243},{4,244},{5,245},{6,246},{7,247},{8... | collective-permute-start | bytes 61448 | tf_op jit(solution)/shard_map/ppermute | solution.py:468
  10.2 3.5 %collective-permute-start.2 = (f32[2,4,640]{2,1,0:T(4,128)S(1)}, f32[2,4,640]{2,1,0:T(4,128)S(1)}, u32[]{:S(2)}, u32[]{:S(2)}) collective-permute-start(f32[2,4,640]{2,1,0:T(4,128)S(1)} %pad_maximum_fusion.5.here_ref), channel_id=1, source_target_pairs={{0,16},{16,0},{32,48},{48,32},{64,80},{80,64},{96,112},{112,96},{1... | collective-permute-start | bytes 61448 | tf_op jit(solution)/shard_map/ppermute | solution.py:469
  19.5 1.6 %collective-permute-start.4 = (f32[56,128]{1,0:T(8,128)S(1)}, f32[56,128]{1,0:T(8,128)S(1)}, u32[]{:S(2)}, u32[]{:S(2)}) collective-permute-start(f32[56,128]{1,0:T(8,128)S(1)} %get-tuple-element.7), channel_id=1, source_target_pairs={{0,16},{16,0},{32,48},{48,32},{64,80},{80,64},{96,112},{112,96},{1... | collective-permute-start | bytes 86024 | tf_op jit(solution)/shard_map/ppermute | solution.py:441
  21.1 2.8 %collective-permute-start.5 = (f32[56,128]{1,0:T(8,128)S(1)}, f32[56,128]{1,0:T(8,128)S(1)}, u32[]{:S(2)}, u32[]{:S(2)}) collective-permute-start(f32[56,128]{1,0:T(8,128)S(1)} %pad_maximum_fusion.1), channel_id=1, source_target_pairs={{0,32},{16,48},{32,0},{48,16},{64,96},{80,112},{96,64},{112,80},{1... | collective-permute-start | bytes 86024 | tf_op jit(solution)/shard_map/ppermute | solution.py:452
  24.0 7.0 %collective-permute-start.7 = (f32[56,128]{1,0:T(8,128)S(1)}, f32[56,128]{1,0:T(8,128)S(1)}, u32[]{:S(2)}, u32[]{:S(2)}) collective-permute-start(f32[56,128]{1,0:T(8,128)S(1)} %pad_maximum_fusion.2), channel_id=1, source_target_pairs={{0,224},{16,240},{32,64},{48,80},{64,32},{80,48},{96,128},{112,144... | collective-permute-start | bytes 86024 | tf_op jit(solution)/shard_map/ppermute | solution.py:452
  27.2 6.0 %collective-permute-start.8 = (f32[56,128]{1,0:T(8,128)S(1)}, f32[56,128]{1,0:T(8,128)S(1)}, u32[]{:S(2)}, u32[]{:S(2)}) collective-permute-start(f32[56,128]{1,0:T(8,128)S(1)} %pad_maximum_fusion.2), channel_id=1, source_target_pairs={{0,160},{16,176},{32,128},{48,144},{64,224},{80,240},{96,192},{112... | collective-permute-start | bytes 86024 | tf_op jit(solution)/shard_map/ppermute | solution.py:452
  28.9 4.5 %collective-permute-start.6 = (f32[56,128]{1,0:T(8,128)S(1)}, f32[56,128]{1,0:T(8,128)S(1)}, u32[]{:S(2)}, u32[]{:S(2)}) collective-permute-start(f32[56,128]{1,0:T(8,128)S(1)} %pad_maximum_fusion.2), channel_id=1, source_target_pairs={{0,96},{16,112},{32,192},{48,208},{64,160},{80,176},{96,0},{112,16... | collective-permute-start | bytes 86024 | tf_op jit(solution)/shard_map/ppermute | solution.py:452
  49.9 5.5 %collective-permute-start.9 = (f32[56,128]{1,0:T(8,128)S(1)}, f32[56,128]{1,0:T(8,128)S(1)}, u32[]{:S(2)}, u32[]{:S(2)}) collective-permute-start(f32[56,128]{1,0:T(8,128)S(1)} %pad_maximum_fusion.4.mine_ref), channel_id=1, source_target_pairs={{0,16},{16,0},{32,48},{48,32},{64,80},{80,64},{96,112},{112,96},{1... | collective-permute-start | bytes 86024 | tf_op jit(solution)/shard_map/ppermute | solution.py:441
